TPU v7x, 256 devices: a whole 4x4x8 slice. The times are simulated.
256 devices in a mesh: row: 16 (over x, z_lo), col: 16 (over z_hi, y, core).
Axes of the slice: x: 4, y: 4, z: 8 (z_hi: 2, z_lo: 4; z = z_hi * 4 + z_lo), core: 2. Of those that a mesh axis runs over, the one named last changes fastest.
Arguments:
- features_in: bfloat16 [256, 2048, 256], P('row', 'col'), may hold values from -6 to 6
- stencil: bfloat16 [3, 7, 256, 2048], P(None, None, 'row', 'col'), may hold values from -2.5 to 2.5
- weights_first: bfloat16 [4, 256, 256], replicated, may hold values from -0.1875 to 0.1875
- weights_second: bfloat16 [4, 256, 256], replicated, may hold values from -0.1875 to 0.1875
- cotangent: bfloat16 [256, 2048, 256], P('row', 'col'), may hold values from -6 to 6
Outputs:
- input_grad: bfloat16 [256, 2048, 256], P('row', 'col')
- grad_first: float32 [4, 256, 256], replicated
- grad_second: float32 [4, 256, 256], replicated
All inputs are finite; a program needn't handle non-finite values.
Results may differ from a plain program's by a relative error of at most 0.0068.
Values may be sent and summed in bfloat16 or wider, within the bound.
No kernel may reach another device: no remote copies, remote signals or barrier semaphores. Data moves between devices by JAX's collectives and lax.ppermute only.
A program may use at most 128 MiB of HBM per device.

v0:
```python
import math

import jax
import jax.numpy as jnp
from jax import lax
from jax.sharding import PartitionSpec as P

OFFSETS = ((0, 0), (0, 1), (0, -1), (1, 0), (-1, 0), (1, 1), (-1, -1))


def extended_2(cells, sides, width, closed):
    for axis, dim in sides:
        count = lax.axis_size(axis)
        ends = count if closed else count - 1
        head = lax.slice_in_dim(cells, 0, width, axis=dim)
        tail = lax.slice_in_dim(cells, cells.shape[dim] - width, cells.shape[dim], axis=dim)
        cells = jnp.concatenate(
            [
                lax.ppermute(tail, axis, [(i, (i + 1) % count) for i in range(ends)]),
                cells,
                lax.ppermute(head, axis, [((i + 1) % count, i) for i in range(ends)]),
            ],
            axis=dim,
        )
    return cells


def stencil_apply(extended, coefficient, height, breadth):
    accumulated = None
    for position, (row_step, col_step) in enumerate(OFFSETS):
        portion = extended[
            1 + row_step : 1 + row_step + height, 1 + col_step : 1 + col_step + breadth
        ]
        addend = coefficient[position][:, :, None] * portion.astype(jnp.float32)
        accumulated = addend if position == 0 else accumulated + addend
    return accumulated


def extend_features(field):
    taller = extended_2(field, (("row", 0),), 1, False)
    return extended_2(taller, (("col", 1),), 1, True)


def feature_stack(field, coefficients):
    height, breadth = (field.shape[0], field.shape[1])
    extended = extend_features(field)
    stacked = [field]
    for operator in range(3):
        stacked.append(
            stencil_apply(extended, coefficients[operator], height, breadth).astype(jnp.bfloat16)
        )
    return jnp.concatenate(stacked, axis=2)


def weight_grad(flattened, grad_flat):
    return lax.dot_general(
        flattened, grad_flat, (((0,), (0,)), ((), ())), preferred_element_type=jnp.float32
    )


def apply_transposed(extended, extended_weights, height, breadth, channels):
    accumulated = None
    for operator in range(3):
        for position, (row_step, col_step) in enumerate(OFFSETS):
            row_start = 1 - row_step
            col_start = 1 - col_step
            weight_part = extended_weights[
                operator, position, row_start : row_start + height, col_start : col_start + breadth
            ]
            field_part = extended[
                row_start : row_start + height,
                col_start : col_start + breadth,
                operator * channels : (operator + 1) * channels,
            ]
            addend = weight_part[:, :, None] * field_part.astype(jnp.float32)
            accumulated = addend if accumulated is None else accumulated + addend
    return accumulated


def body(features_in, stencil, weights_first, weights_second, cotangent):
    height, breadth, channels = features_in.shape
    coefficients = stencil.astype(jnp.float32)
    scale_factor = 1.0 / math.sqrt(height * breadth * lax.axis_size("row") * lax.axis_size("col"))
    flat_weights = stencil.reshape(21, height, breadth)
    taller_weights = extended_2(flat_weights, (("row", 1),), 1, False)
    extended_weights = extended_2(taller_weights, (("col", 2),), 1, True)
    extended_weights = extended_weights.astype(jnp.float32).reshape(3, 7, height + 2, breadth + 2)

    def backward_input(grad_flat, weights):
        projected = lax.dot_general(
            grad_flat,
            weights.reshape(-1, channels),
            (((1,), (1,)), ((), ())),
            preferred_element_type=jnp.float32,
        ).astype(jnp.bfloat16)
        centre = projected[:, :channels].astype(jnp.float32)
        directional = projected[:, channels:].reshape(height, breadth, 3 * channels)
        taller = extended_2(directional, (("row", 0),), 1, False)
        extended = extended_2(taller, (("col", 1),), 1, True)
        return centre + apply_transposed(
            extended, extended_weights, height, breadth, channels
        ).reshape(-1, channels)

    first_flat = feature_stack(features_in, coefficients).reshape(-1, 4 * channels)
    first_pre = jnp.dot(
        first_flat, weights_first.reshape(-1, channels), preferred_element_type=jnp.float32
    )
    hidden = jax.nn.silu(first_pre).astype(jnp.bfloat16).reshape(height, breadth, channels)
    second_flat = feature_stack(hidden, coefficients).reshape(-1, 4 * channels)
    cot_flat = cotangent.reshape(-1, channels)
    second_total = lax.psum(weight_grad(second_flat, cot_flat), ("row", "col"))
    grad_second = (second_total * scale_factor).reshape(4, channels, channels)
    hidden_grad = backward_input(cot_flat, weights_second)
    sigmoid_value = jax.nn.sigmoid(first_pre)
    pre_grad = (hidden_grad * sigmoid_value * (1.0 + first_pre * (1.0 - sigmoid_value))).astype(
        jnp.bfloat16
    )
    first_total = lax.psum(weight_grad(first_flat, pre_grad), ("row", "col"))
    grad_first = (first_total * scale_factor).reshape(4, channels, channels)
    input_grad = (
        backward_input(pre_grad, weights_first)
        .astype(jnp.bfloat16)
        .reshape(height, breadth, channels)
    )
    return (input_grad, grad_first, grad_second)


def solution(mesh):
    return jax.shard_map(
        body,
        mesh=mesh,
        in_specs=(
            P("row", "col", None),
            P(None, None, "row", "col"),
            P(),
            P(),
            P("row", "col", None),
        ),
        out_specs=(P("row", "col", None), P(), P()),
        check_vma=False,
    )
```

profile of v0, /device:TPU:1, one launch (start us, length us, event | category | flops | bytes accessed | tf_op | source)
XLA Modules:
  0.0 460.0 jit_solution(13267026391594525501)
XLA Ops:
  7.2 0.9 fusion.62
  8.2 4.4 collective-permute-start
  12.6 1.3 collective-permute-start.1
  13.9 1.6 copy.51
  15.5 1.3 collective-permute-start.9
  16.8 4.8 %collective-permute-start.8 = (bf16[1,128,256]{1,2,0:T(8,128)(2,1)S(1)}, bf16[1,128,256]{1,2,0:T(8,128)(2,1)S(1)}, u32[]{:S(2)}, u32[]{:S(2)}) collective-permute-start(bf16[1,128,256]{1,2,0:T(8,128)(2,1)S(1)} %get-tuple-element.26), channel_id=1, source_target_pairs={{0,16},{16,32},{32,48},{48,64},{64,80},{80,96},{96,112},{112,128},... | collective-permute-start | bytes 196616 | tf_op jit(solution)/shard_map/ppermute | solution.py:19
  21.6 1.3 convolution_convert_fusion.1
  22.9 0.9 slice_bitcast_fusion.3
  23.8 3.5 collective-permute-start.4
  27.4 0.7 slice_bitcast_fusion.26
  28.3 3.0 collective-permute-start.2
  31.8 2.0 slice.675
  33.8 1.3 collective-permute-start.5
  35.6 0.7 convert_bitcast_fusion.14
  36.3 0.7 convert_bitcast_fusion.15
  37.0 0.7 convert_bitcast_fusion.16
  37.7 0.7 convert_bitcast_fusion.17
  38.3 0.7 convert_bitcast_fusion.18
  39.0 0.7 convert_bitcast_fusion.19
  39.9 1.9 fusion.59
  41.8 1.8 copy.47
  43.6 2.4 copy.45
  46.0 7.6 %collective-permute-start.10 = (bf16[18,1,256]{2,0,1:T(8,128)(2,1)}, bf16[18,1,256]{2,0,1:T(8,128)(2,1)}, u32[]{:S(2)}, u32[]{:S(2)}) collective-permute-start(bf16[18,1,256]{2,0,1:T(8,128)(2,1)} %copy.45), channel_id=1, source_target_pairs={{1,0},{2,1},{3,2},{4,3},{5,4},{6,5},{7,6},{8,7},{9,8},{10,9},{11,1... | collective-permute-start | bytes 27656 | tf_op jit(solution)/shard_map/ppermute | solution.py:21
  53.6 0.7 convert_bitcast_fusion.13
  54.3 5.1 %collective-permute-done.11 = bf16[18,1,256]{2,0,1:T(8,128)(2,1)} collective-permute-done((bf16[18,1,256]{2,0,1:T(8,128)(2,1)S(1)}, bf16[18,1,256]{2,0,1:T(8,128)(2,1)}, u32[]{:S(2)}, u32[]{:S(2)}) %collective-permute-start.11) | collective-permute-done | bytes 9248 | tf_op jit(solution)/shard_map/ppermute | solution.py:19
  59.4 1.3 copy.48
  60.8 2.2 copy.46
  63.0 5.8 %fusion.21 = bf16[16,128,256]{1,2,0:T(8,128)(2,1)S(1)} fusion(bf16[16,128,256]{1,2,0:T(8,128)(2,1)S(1)} %copy.51, bf16[1,128,256]{1,2,0:T(8,128)(2,1)} %copy-done.12, bf16[1,128,256]{1,2,0:T(8,128)(2,1)S(1)} %collective-permute-done.9, f32[16,128]{1,0:T(8,128)} %get-tuple-element.56, f32[16,128]{1,0:T(8,128)} %get-tuple-element.57, ...), kind=kLoop, calls=%fused_computation.70 | loop fusion | flops 28835840 | bytes 2304000 | tf_op jit(solution)/shard_map/convert_element_type | solution.py:50
  69.0 4.2 fusion.14
  73.2 4.2 fusion.28
  77.4 0.8 pad_maximum_fusion.35
  78.3 8.5 %collective-permute-start.7 = (bf16[18,1,768]{2,1,0:T(2,128)(2,1)S(1)}, bf16[18,1,768]{2,1,0:T(2,128)(2,1)S(1)}, u32[]{:S(2)}, u32[]{:S(2)}) collective-permute-start(bf16[18,1,768]{2,1,0:T(2,128)(2,1)S(1)} %get-tuple-element.16), channel_id=1, source_target_pairs={{1,0},{2,1},{3,2},{4,3},{5,4},{6,5},{7,6},{8,7},{9,8},{10,9},{11,1... | collective-permute-start | bytes 82952 | tf_op jit(solution)/shard_map/ppermute | solution.py:21
  86.8 2.2 pad_maximum_fusion
  89.1 6.4 %copy.52 = bf16[16,128,1024]{2,1,0:T(8,128)(2,1)} copy(bf16[16,128,1024]{1,2,0:T(8,128)(2,1)} %pad_maximum_fusion) | data formatting | bytes 8388608 | tf_op jit(solution)/shard_map/concatenate | solution.py:52
  95.7 4.9 %maximum_maximum_fusion = (bf16[18,129,768]{2,1,0:T(8,128)(2,1)S(1)}, bf16[18,129,768]{2,1,0:T(8,128)(2,1)S(1)}) fusion(bf16[1,128,768]{2,1,0:T(8,128)(2,1)} %collective-permute-done.5, bf16[16,128,768]{2,1,0:T(8,128)(2,1)} %bitcast.135, bf16[1,128,768]{2,1,0:T(8,128)(2,1)S(1)} %collective-permute-done.4, bf16[18,1,768]{2,1,0:T(2,128)(2,1)S(1)} %collective-permute-done.6, ...), kind=kLoop, calls=%fused_computation.11 | loop fusion | flops 28532736 | bytes 10727424 | tf_op jit(solution)/shard_map/concatenate | solution.py:17
  100.8 10.0 %multiply_add_fusion.1 = f32[16,128,256]{2,1,0:T(8,128)S(1)} fusion(bf16[18,129,768]{2,1,0:T(8,128)(2,1)S(1)} %get-tuple-element.14, bf16[18,129,768]{2,1,0:T(8,128)(2,1)S(1)} %get-tuple-element.13, bf16[1,128,768]{2,1,0:T(8,128)(2,1)} %collective-permute-done.5, bf16[16,128,768]{2,1,0:T(8,128)(2,1)S(1)} %bitcast.137, ...), kind=kLoop, calls=%fused_computation.108 | loop fusion | flops 41943040 | bytes 21536768 | tf_op jit(solution)/shard_map/add | solution.py:76
  110.8 3.2 multiply_convert_fusion
  114.1 2.3 fusion.63
  116.4 1.3 collective-permute-start.17
  117.7 4.4 collective-permute-start.16
  122.1 3.3 convolution_convert_fusion
  125.4 0.7 copy.65
  126.3 0.6 copy-done.10
  127.1 1.6 fusion.58
  128.7 2.4 copy.59
  131.1 1.1 copy.57
  132.2 8.0 %collective-permute-start.18 = (bf16[18,1,256]{2,0,1:T(8,128)(2,1)}, bf16[18,1,256]{2,0,1:T(8,128)(2,1)}, u32[]{:S(2)}, u32[]{:S(2)}) collective-permute-start(bf16[18,1,256]{2,0,1:T(8,128)(2,1)} %copy.57), channel_id=1, source_target_pairs={{1,0},{2,1},{3,2},{4,3},{5,4},{6,5},{7,6},{8,7},{9,8},{10,9},{11,1... | collective-permute-start | bytes 27656 | tf_op jit(solution)/shard_map/ppermute | solution.py:21
  140.2 1.8 slice_bitcast_fusion.1
  142.0 3.8 slice.719
  145.8 6.1 %collective-permute-start.12 = (bf16[1,128,768]{2,1,0:T(8,128)(2,1)}, bf16[1,128,768]{2,1,0:T(8,128)(2,1)S(1)}, u32[]{:S(2)}, u32[]{:S(2)}) collective-permute-start(bf16[1,128,768]{2,1,0:T(8,128)(2,1)} %get-tuple-element.5), channel_id=1, source_target_pairs={{0,16},{16,32},{32,48},{48,64},{64,80},{80,96},{96,112},{112,128},... | collective-permute-start | bytes 589832 | tf_op jit(solution)/shard_map/ppermute | solution.py:19
  152.0 1.3 collective-permute-start.13
  153.3 1.3 copy.60
  154.6 2.2 copy.58
  156.8 5.8 %fusion.42 = bf16[16,128,256]{1,2,0:T(8,128)(2,1)S(1)} fusion(bf16[16,128,256]{1,2,0:T(8,128)(2,1)S(1)} %copy.65, bf16[1,128,256]{1,2,0:T(8,128)(2,1)} %copy-done.10, bf16[1,128,256]{1,2,0:T(8,128)(2,1)S(1)} %copy.56, f32[16,128]{1,0:T(8,128)} %get-tuple-element.56, f32[16,128]{1,0:T(8,128)} %get-tuple-element.57, f32[16,128]{1,0:T(8,128)} %get-tuple-element.58, ...), kind=kLoop, calls=%fused_computation.91 | loop fusion | flops 28835840 | bytes 2304000 | tf_op jit(solution)/shard_map/convert_element_type | solution.py:50
  162.8 4.2 fusion.35
  167.0 4.2 fusion.49
  171.2 0.8 pad_maximum_fusion.32
  172.2 1.1 collective-permute-start.15
  173.3 2.2 fusion.54
  176.1 4.9 %maximum_maximum_fusion.1 = (bf16[18,129,768]{2,1,0:T(8,128)(2,1)S(1)}, bf16[18,129,768]{2,1,0:T(8,128)(2,1)S(1)}) fusion(bf16[1,128,768]{2,1,0:T(8,128)(2,1)} %collective-permute-done.13, bf16[16,128,768]{2,1,0:T(8,128)(2,1)} %bitcast.138, bf16[1,128,768]{2,1,0:T(8,128)(2,1)S(1)} %collective-permute-done.12, ...), kind=kLoop, calls=%fused_computation.13 | loop fusion | flops 28532736 | bytes 10727424 | tf_op jit(solution)/shard_map/concatenate | solution.py:17
  181.2 9.9 %multiply_add_fusion = f32[16,128,256]{2,1,0:T(8,128)S(1)} fusion(bf16[18,129,768]{2,1,0:T(8,128)(2,1)S(1)} %get-tuple-element.10, bf16[18,129,768]{2,1,0:T(8,128)(2,1)S(1)} %get-tuple-element.9, bf16[1,128,768]{2,1,0:T(8,128)(2,1)} %collective-permute-done.13, bf16[16,128,768]{2,1,0:T(8,128)(2,1)S(1)} %bitcast.140, ...), kind=kLoop, calls=%fused_computation.106 | loop fusion | flops 41943040 | bytes 21536768 | tf_op jit(solution)/shard_map/add | solution.py:76
  191.1 2.7 fusion.50
  193.8 256.3 %all-reduce.3.cloned.1.call-done = (f32[1024,256]{1,0:T(8,128)}, f32[1024,256]{1,0:T(8,128)}) async-done(((f32[1024,256]{1,0:T(8,128)}, f32[1024,256]{1,0:T(8,128)}), (f32[1024,256]{1,0:T(8,128)}, f32[1024,256]{1,0:T(8,128)})) %all-reduce.3.cloned.1.call-update) | async-done | bytes 2097168 | tf_op jit(solution)/shard_map/psum | solution.py:118
  450.1 3.0 broadcast_multiply_fusion
  (199 shorter events, 2.8 us)
Async XLA Ops:
  7.2 14.4 %copy-start = (bf16[16,128,256]{2,1,0:T(8,128)(2,1)S(1)}, bf16[16,128,256]{2,1,0:T(8,128)(2,1)}, u32[]{:S(2)}) copy-start(bf16[16,128,256]{2,1,0:T(8,128)(2,1)} %param.9) | copy-start | bytes 3145732
  7.2 14.4 %copy-start.14 = (bf16[4,256,256]{2,1,0:T(8,128)(2,1)S(1)}, bf16[4,256,256]{2,1,0:T(8,128)(2,1)}, u32[]{:S(2)}) copy-start(bf16[4,256,256]{2,1,0:T(8,128)(2,1)} %param.8) | copy-start | bytes 1572868
  7.2 442.9 %all-reduce.3.cloned.1.call-start = ((), (), s32[]{:S(2)}) async-start(), calls=%async_computation | async-start | bytes 4194304 | tf_op jit(solution)/shard_map/psum | solution.py:118
  8.2 19.9 %collective-permute-start = (bf16[21,1,128]{2,1,0:T(2,128)(2,1)S(1)}, bf16[21,1,128]{2,1,0:T(2,128)(2,1)S(1)}, u32[]{:S(2)}, u32[]{:S(2)}) collective-permute-start(bf16[21,1,128]{2,1,0:T(2,128)(2,1)S(1)} %get-tuple-element.71), channel_id=1, source_target_pairs={{0,16},{16,32},{32,48},{48,64},{64,80},{80,96},{96,112},{112,128},... | collective-permute-start | bytes 16136 | tf_op jit(solution)/shard_map/ppermute | solution.py:19
  12.6 15.5 %collective-permute-start.1 = (bf16[21,1,128]{2,1,0:T(2,128)(2,1)S(1)}, bf16[21,1,128]{2,1,0:T(2,128)(2,1)S(1)}, u32[]{:S(2)}, u32[]{:S(2)}) collective-permute-start(bf16[21,1,128]{2,1,0:T(2,128)(2,1)S(1)} %get-tuple-element.72), channel_id=1, source_target_pairs={{16,0},{32,16},{48,32},{64,48},{80,64},{96,80},{112,96},{128,112},... | collective-permute-start | bytes 16136 | tf_op jit(solution)/shard_map/ppermute | solution.py:21
  15.5 24.2 %collective-permute-start.9 = (bf16[1,128,256]{1,2,0:T(8,128)(2,1)S(1)}, bf16[1,128,256]{1,2,0:T(8,128)(2,1)S(1)}, u32[]{:S(2)}, u32[]{:S(2)}) collective-permute-start(bf16[1,128,256]{1,2,0:T(8,128)(2,1)S(1)} %get-tuple-element.25), channel_id=1, source_target_pairs={{16,0},{32,16},{48,32},{64,48},{80,64},{96,80},{112,96},{128,112},... | collective-permute-start | bytes 196616 | tf_op jit(solution)/shard_map/ppermute | solution.py:21
  16.8 22.9 %collective-permute-start.8 = (bf16[1,128,256]{1,2,0:T(8,128)(2,1)S(1)}, bf16[1,128,256]{1,2,0:T(8,128)(2,1)S(1)}, u32[]{:S(2)}, u32[]{:S(2)}) collective-permute-start(bf16[1,128,256]{1,2,0:T(8,128)(2,1)S(1)} %get-tuple-element.26), channel_id=1, source_target_pairs={{0,16},{16,32},{32,48},{48,64},{64,80},{80,96},{96,112},{112,128},... | collective-permute-start | bytes 196616 | tf_op jit(solution)/shard_map/ppermute | solution.py:19
  21.6 5.7 %copy-start.8 = (bf16[3,7,16,128]{3,2,1,0:T(8,128)(2,1)S(1)}, bf16[3,7,16,128]{3,2,1,0:T(8,128)(2,1)}, u32[]{:S(2)}) copy-start(bf16[3,7,16,128]{3,2,1,0:T(8,128)(2,1)} %param.6) | copy-start | bytes 258052
  22.9 10.9 %copy-start.5 = (bf16[2048,1024]{1,0:T(8,128)(2,1)}, bf16[2048,1024]{1,0:T(8,128)(2,1)S(1)}, u32[]{:S(2)}) copy-start(bf16[2048,1024]{1,0:T(8,128)(2,1)S(1)} %convolution_convert_fusion.1) | copy-start | bytes 12582916
  23.8 53.6 %collective-permute-start.4 = (bf16[1,128,768]{2,1,0:T(8,128)(2,1)}, bf16[1,128,768]{2,1,0:T(8,128)(2,1)S(1)}, u32[]{:S(2)}, u32[]{:S(2)}) collective-permute-start(bf16[1,128,768]{2,1,0:T(8,128)(2,1)} %get-tuple-element.7), channel_id=1, source_target_pairs={{0,16},{16,32},{32,48},{48,64},{64,80},{80,96},{96,112},{112,128},... | collective-permute-start | bytes 589832 | tf_op jit(solution)/shard_map/ppermute | solution.py:19
  28.3 5.5 %collective-permute-start.2 = (bf16[21,18,1]{2,1,0:T(8,128)(2,1)S(1)}, bf16[21,18,1]{2,1,0:T(8,128)(2,1)S(1)}, u32[]{:S(2)}, u32[]{:S(2)}) collective-permute-start(bf16[21,18,1]{2,1,0:T(8,128)(2,1)S(1)} %get-tuple-element.69), channel_id=1, source_target_pairs={{0,1},{1,2},{2,3},{3,4},{4,5},{5,6},{6,7},{7,8},{8,9},{9,10},{10,1... | collective-permute-start | bytes 2276 | tf_op jit(solution)/shard_map/ppermute | solution.py:19
  31.2 4.4 collective-permute-start.3
  33.8 43.6 %collective-permute-start.5 = (bf16[1,128,768]{2,1,0:T(8,128)(2,1)}, bf16[1,128,768]{2,1,0:T(8,128)(2,1)}, u32[]{:S(2)}, u32[]{:S(2)}) collective-permute-start(bf16[1,128,768]{2,1,0:T(8,128)(2,1)} %get-tuple-element.8), channel_id=1, source_target_pairs={{16,0},{32,16},{48,32},{64,48},{80,64},{96,80},{112,96},{128,112},... | collective-permute-start | bytes 589832 | tf_op jit(solution)/shard_map/ppermute | solution.py:21
  46.0 14.7 %collective-permute-start.10 = (bf16[18,1,256]{2,0,1:T(8,128)(2,1)}, bf16[18,1,256]{2,0,1:T(8,128)(2,1)}, u32[]{:S(2)}, u32[]{:S(2)}) collective-permute-start(bf16[18,1,256]{2,0,1:T(8,128)(2,1)} %copy.45), channel_id=1, source_target_pairs={{1,0},{2,1},{3,2},{4,3},{5,4},{6,5},{7,6},{8,7},{9,8},{10,9},{11,1... | collective-permute-start | bytes 27656 | tf_op jit(solution)/shard_map/ppermute | solution.py:21
  53.6 5.8 %collective-permute-start.11 = (bf16[18,1,256]{2,0,1:T(8,128)(2,1)S(1)}, bf16[18,1,256]{2,0,1:T(8,128)(2,1)}, u32[]{:S(2)}, u32[]{:S(2)}) collective-permute-start(bf16[18,1,256]{2,0,1:T(8,128)(2,1)S(1)} %copy.47), channel_id=1, source_target_pairs={{0,1},{1,2},{2,3},{3,4},{4,5},{5,6},{6,7},{7,8},{8,9},{9,10},{10,1... | collective-permute-start | bytes 27656 | tf_op jit(solution)/shard_map/ppermute | solution.py:19
  63.0 5.9 %copy-start.7 = (bf16[18,1,256]{1,2,0:T(8,128)(2,1)S(1)}, bf16[18,1,256]{1,2,0:T(8,128)(2,1)}, u32[]{:S(2)}) copy-start(bf16[18,1,256]{1,2,0:T(8,128)(2,1)} %copy.46) | copy-start | bytes 27652
  63.0 5.9 %copy-start.13 = (bf16[1,128,256]{1,2,0:T(8,128)(2,1)S(1)}, bf16[1,128,256]{1,2,0:T(8,128)(2,1)}, u32[]{:S(2)}) copy-start(bf16[1,128,256]{1,2,0:T(8,128)(2,1)} %copy-done.12) | copy-start | bytes 196612
  63.0 5.9 %copy-start.68 = (f32[16,128]{1,0:T(8,128)S(1)}, f32[16,128]{1,0:T(8,128)}, u32[]{:S(2)}) copy-start(f32[16,128]{1,0:T(8,128)} %get-tuple-element.48) | copy-start | bytes 24580
  63.0 5.9 %copy-start.70 = (f32[16,128]{1,0:T(8,128)S(1)}, f32[16,128]{1,0:T(8,128)}, u32[]{:S(2)}) copy-start(f32[16,128]{1,0:T(8,128)} %get-tuple-element.63) | copy-start | bytes 24580
  63.0 5.9 %copy-start.72 = (f32[16,128]{1,0:T(8,128)S(1)}, f32[16,128]{1,0:T(8,128)}, u32[]{:S(2)}) copy-start(f32[16,128]{1,0:T(8,128)} %get-tuple-element.64) | copy-start | bytes 24580
  63.0 5.9 %copy-start.74 = (f32[16,128]{1,0:T(8,128)S(1)}, f32[16,128]{1,0:T(8,128)}, u32[]{:S(2)}) copy-start(f32[16,128]{1,0:T(8,128)} %get-tuple-element.65) | copy-start | bytes 24580
  63.0 5.9 %copy-start.76 = (f32[16,128]{1,0:T(8,128)S(1)}, f32[16,128]{1,0:T(8,128)}, u32[]{:S(2)}) copy-start(f32[16,128]{1,0:T(8,128)} %get-tuple-element.66) | copy-start | bytes 24580
  63.0 5.9 %copy-start.78 = (f32[16,128]{1,0:T(8,128)S(1)}, f32[16,128]{1,0:T(8,128)}, u32[]{:S(2)}) copy-start(f32[16,128]{1,0:T(8,128)} %get-tuple-element.67) | copy-start | bytes 24580
  63.0 5.9 %copy-start.80 = (f32[16,128]{1,0:T(8,128)S(1)}, f32[16,128]{1,0:T(8,128)}, u32[]{:S(2)}) copy-start(f32[16,128]{1,0:T(8,128)} %get-tuple-element.68) | copy-start | bytes 24580
  78.2 17.4 %collective-permute-start.6 = (bf16[18,1,768]{2,1,0:T(2,128)(2,1)S(1)}, bf16[18,1,768]{2,1,0:T(2,128)(2,1)S(1)}, u32[]{:S(2)}, u32[]{:S(2)}) collective-permute-start(bf16[18,1,768]{2,1,0:T(2,128)(2,1)S(1)} %get-tuple-element.15), channel_id=1, source_target_pairs={{0,1},{1,2},{2,3},{3,4},{4,5},{5,6},{6,7},{7,8},{8,9},{9,10},{10,1... | collective-permute-start | bytes 82952 | tf_op jit(solution)/shard_map/ppermute | solution.py:19
  78.3 17.3 %collective-permute-start.7 = (bf16[18,1,768]{2,1,0:T(2,128)(2,1)S(1)}, bf16[18,1,768]{2,1,0:T(2,128)(2,1)S(1)}, u32[]{:S(2)}, u32[]{:S(2)}) collective-permute-start(bf16[18,1,768]{2,1,0:T(2,128)(2,1)S(1)} %get-tuple-element.16), channel_id=1, source_target_pairs={{1,0},{2,1},{3,2},{4,3},{5,4},{6,5},{7,6},{8,7},{9,8},{10,9},{11,1... | collective-permute-start | bytes 82952 | tf_op jit(solution)/shard_map/ppermute | solution.py:21
  100.8 10.0 %copy-start.9 = (bf16[16,128,1024]{2,1,0:T(8,128)(2,1)S(1)}, bf16[16,128,1024]{2,1,0:T(8,128)(2,1)}, u32[]{:S(2)}) copy-start(bf16[16,128,1024]{2,1,0:T(8,128)(2,1)} %copy.52) | copy-start | bytes 12582916
  100.8 10.0 %copy-start.15 = (bf16[4,256,256]{2,1,0:T(8,128)(2,1)S(1)}, bf16[4,256,256]{2,1,0:T(8,128)(2,1)}, u32[]{:S(2)}) copy-start(bf16[4,256,256]{2,1,0:T(8,128)(2,1)} %param.7) | copy-start | bytes 1572868
  116.4 9.7 %collective-permute-start.17 = (bf16[1,128,256]{2,1,0:T(8,128)(2,1)S(1)}, bf16[1,128,256]{2,1,0:T(8,128)(2,1)S(1)}, u32[]{:S(2)}, u32[]{:S(2)}) collective-permute-start(bf16[1,128,256]{2,1,0:T(8,128)(2,1)S(1)} %get-tuple-element.23), channel_id=1, source_target_pairs={{16,0},{32,16},{48,32},{64,48},{80,64},{96,80},{112,96},{128,112},... | collective-permute-start | bytes 196616 | tf_op jit(solution)/shard_map/ppermute | solution.py:21
  117.7 8.6 %collective-permute-start.16 = (bf16[1,128,256]{2,1,0:T(8,128)(2,1)S(1)}, bf16[1,128,256]{2,1,0:T(8,128)(2,1)S(1)}, u32[]{:S(2)}, u32[]{:S(2)}) collective-permute-start(bf16[1,128,256]{2,1,0:T(8,128)(2,1)S(1)} %get-tuple-element.24), channel_id=1, source_target_pairs={{0,16},{16,32},{32,48},{48,64},{64,80},{80,96},{96,112},{112,128},... | collective-permute-start | bytes 196616 | tf_op jit(solution)/shard_map/ppermute | solution.py:19
  132.2 22.4 %collective-permute-start.18 = (bf16[18,1,256]{2,0,1:T(8,128)(2,1)}, bf16[18,1,256]{2,0,1:T(8,128)(2,1)}, u32[]{:S(2)}, u32[]{:S(2)}) collective-permute-start(bf16[18,1,256]{2,0,1:T(8,128)(2,1)} %copy.57), channel_id=1, source_target_pairs={{1,0},{2,1},{3,2},{4,3},{5,4},{6,5},{7,6},{8,7},{9,8},{10,9},{11,1... | collective-permute-start | bytes 27656 | tf_op jit(solution)/shard_map/ppermute | solution.py:21
  140.2 13.0 %collective-permute-start.19 = (bf16[18,1,256]{2,0,1:T(8,128)(2,1)}, bf16[18,1,256]{2,0,1:T(8,128)(2,1)}, u32[]{:S(2)}, u32[]{:S(2)}) collective-permute-start(bf16[18,1,256]{2,0,1:T(8,128)(2,1)} %copy.59), channel_id=1, source_target_pairs={{0,1},{1,2},{2,3},{3,4},{4,5},{5,6},{6,7},{7,8},{8,9},{9,10},{10,1... | collective-permute-start | bytes 27656 | tf_op jit(solution)/shard_map/ppermute | solution.py:19
  145.8 25.4 %collective-permute-start.12 = (bf16[1,128,768]{2,1,0:T(8,128)(2,1)}, bf16[1,128,768]{2,1,0:T(8,128)(2,1)S(1)}, u32[]{:S(2)}, u32[]{:S(2)}) collective-permute-start(bf16[1,128,768]{2,1,0:T(8,128)(2,1)} %get-tuple-element.5), channel_id=1, source_target_pairs={{0,16},{16,32},{32,48},{48,64},{64,80},{80,96},{96,112},{112,128},... | collective-permute-start | bytes 589832 | tf_op jit(solution)/shard_map/ppermute | solution.py:19
  152.0 19.3 %collective-permute-start.13 = (bf16[1,128,768]{2,1,0:T(8,128)(2,1)}, bf16[1,128,768]{2,1,0:T(8,128)(2,1)}, u32[]{:S(2)}, u32[]{:S(2)}) collective-permute-start(bf16[1,128,768]{2,1,0:T(8,128)(2,1)} %get-tuple-element.6), channel_id=1, source_target_pairs={{16,0},{32,16},{48,32},{64,48},{80,64},{96,80},{112,96},{128,112},... | collective-permute-start | bytes 589832 | tf_op jit(solution)/shard_map/ppermute | solution.py:21
  156.8 5.8 %copy-start.6 = (bf16[18,1,256]{1,2,0:T(8,128)(2,1)S(1)}, bf16[18,1,256]{1,2,0:T(8,128)(2,1)}, u32[]{:S(2)}) copy-start(bf16[18,1,256]{1,2,0:T(8,128)(2,1)} %copy.58) | copy-start | bytes 27652
  156.8 5.9 %copy-start.11 = (bf16[1,128,256]{1,2,0:T(8,128)(2,1)S(1)}, bf16[1,128,256]{1,2,0:T(8,128)(2,1)}, u32[]{:S(2)}) copy-start(bf16[1,128,256]{1,2,0:T(8,128)(2,1)} %copy-done.10) | copy-start | bytes 196612
  156.8 5.9 %copy-start.69 = (f32[16,128]{1,0:T(8,128)S(1)}, f32[16,128]{1,0:T(8,128)}, u32[]{:S(2)}) copy-start(f32[16,128]{1,0:T(8,128)} %get-tuple-element.48) | copy-start | bytes 24580
  156.8 5.9 %copy-start.71 = (f32[16,128]{1,0:T(8,128)S(1)}, f32[16,128]{1,0:T(8,128)}, u32[]{:S(2)}) copy-start(f32[16,128]{1,0:T(8,128)} %get-tuple-element.63) | copy-start | bytes 24580
  156.8 5.9 %copy-start.73 = (f32[16,128]{1,0:T(8,128)S(1)}, f32[16,128]{1,0:T(8,128)}, u32[]{:S(2)}) copy-start(f32[16,128]{1,0:T(8,128)} %get-tuple-element.64) | copy-start | bytes 24580
  156.8 5.9 %copy-start.75 = (f32[16,128]{1,0:T(8,128)S(1)}, f32[16,128]{1,0:T(8,128)}, u32[]{:S(2)}) copy-start(f32[16,128]{1,0:T(8,128)} %get-tuple-element.65) | copy-start | bytes 24580
  156.8 5.9 %copy-start.77 = (f32[16,128]{1,0:T(8,128)S(1)}, f32[16,128]{1,0:T(8,128)}, u32[]{:S(2)}) copy-start(f32[16,128]{1,0:T(8,128)} %get-tuple-element.66) | copy-start | bytes 24580
  156.8 5.9 %copy-start.79 = (f32[16,128]{1,0:T(8,128)S(1)}, f32[16,128]{1,0:T(8,128)}, u32[]{:S(2)}) copy-start(f32[16,128]{1,0:T(8,128)} %get-tuple-element.67) | copy-start | bytes 24580
  156.8 5.9 %copy-start.81 = (f32[16,128]{1,0:T(8,128)S(1)}, f32[16,128]{1,0:T(8,128)}, u32[]{:S(2)}) copy-start(f32[16,128]{1,0:T(8,128)} %get-tuple-element.68) | copy-start | bytes 24580
  172.1 3.7 collective-permute-start.14
  172.2 3.9 collective-permute-start.15
  175.5 5.5 %copy-start.17 = (f32[16,128]{1,0:T(8,128)S(1)}, f32[16,128]{1,0:T(8,128)}, u32[]{:S(2)}) copy-start(f32[16,128]{1,0:T(8,128)} %get-tuple-element.44) | copy-start | bytes 24580
  175.5 5.5 %copy-start.19 = (f32[16,128]{1,0:T(8,128)S(1)}, f32[16,128]{1,0:T(8,128)}, u32[]{:S(2)}) copy-start(f32[16,128]{1,0:T(8,128)} %get-tuple-element.39) | copy-start | bytes 24580
  175.5 5.5 %copy-start.21 = (f32[16,128]{1,0:T(8,128)S(1)}, f32[16,128]{1,0:T(8,128)}, u32[]{:S(2)}) copy-start(f32[16,128]{1,0:T(8,128)} %get-tuple-element.40) | copy-start | bytes 24580
  175.6 5.5 %copy-start.23 = (f32[16,128]{1,0:T(8,128)S(1)}, f32[16,128]{1,0:T(8,128)}, u32[]{:S(2)}) copy-start(f32[16,128]{1,0:T(8,128)} %get-tuple-element.41) | copy-start | bytes 24580
  175.6 5.5 %copy-start.25 = (f32[16,128]{1,0:T(8,128)S(1)}, f32[16,128]{1,0:T(8,128)}, u32[]{:S(2)}) copy-start(f32[16,128]{1,0:T(8,128)} %get-tuple-element.36) | copy-start | bytes 24580
  175.6 5.5 %copy-start.27 = (f32[16,128]{1,0:T(8,128)S(1)}, f32[16,128]{1,0:T(8,128)}, u32[]{:S(2)}) copy-start(f32[16,128]{1,0:T(8,128)} %get-tuple-element.37) | copy-start | bytes 24580
  175.6 5.5 %copy-start.29 = (f32[16,128]{1,0:T(8,128)S(1)}, f32[16,128]{1,0:T(8,128)}, u32[]{:S(2)}) copy-start(f32[16,128]{1,0:T(8,128)} %get-tuple-element.38) | copy-start | bytes 24580
  175.6 5.5 %copy-start.31 = (f32[16,128]{1,0:T(8,128)S(1)}, f32[16,128]{1,0:T(8,128)}, u32[]{:S(2)}) copy-start(f32[16,128]{1,0:T(8,128)} %get-tuple-element.33) | copy-start | bytes 24580
  175.6 5.5 %copy-start.33 = (f32[16,128]{1,0:T(8,128)S(1)}, f32[16,128]{1,0:T(8,128)}, u32[]{:S(2)}) copy-start(f32[16,128]{1,0:T(8,128)} %get-tuple-element.34) | copy-start | bytes 24580
  175.6 5.5 %copy-start.35 = (f32[16,128]{1,0:T(8,128)S(1)}, f32[16,128]{1,0:T(8,128)}, u32[]{:S(2)}) copy-start(f32[16,128]{1,0:T(8,128)} %get-tuple-element.35) | copy-start | bytes 24580
  175.6 5.5 %copy-start.37 = (f32[16,128]{1,0:T(8,128)S(1)}, f32[16,128]{1,0:T(8,128)}, u32[]{:S(2)}) copy-start(f32[16,128]{1,0:T(8,128)} %get-tuple-element.30) | copy-start | bytes 24580
  175.6 5.5 %copy-start.39 = (f32[16,128]{1,0:T(8,128)S(1)}, f32[16,128]{1,0:T(8,128)}, u32[]{:S(2)}) copy-start(f32[16,128]{1,0:T(8,128)} %get-tuple-element.31) | copy-start | bytes 24580
  175.6 5.5 %copy-start.41 = (f32[16,128]{1,0:T(8,128)S(1)}, f32[16,128]{1,0:T(8,128)}, u32[]{:S(2)}) copy-start(f32[16,128]{1,0:T(8,128)} %get-tuple-element.32) | copy-start | bytes 24580
  175.7 5.5 %copy-start.43 = (f32[16,128]{1,0:T(8,128)S(1)}, f32[16,128]{1,0:T(8,128)}, u32[]{:S(2)}) copy-start(f32[16,128]{1,0:T(8,128)} %get-tuple-element.27) | copy-start | bytes 24580
  175.7 5.5 %copy-start.45 = (f32[16,128]{1,0:T(8,128)S(1)}, f32[16,128]{1,0:T(8,128)}, u32[]{:S(2)}) copy-start(f32[16,128]{1,0:T(8,128)} %get-tuple-element.28) | copy-start | bytes 24580
  175.7 5.5 %copy-start.47 = (f32[16,128]{1,0:T(8,128)S(1)}, f32[16,128]{1,0:T(8,128)}, u32[]{:S(2)}) copy-start(f32[16,128]{1,0:T(8,128)} %get-tuple-element.29) | copy-start | bytes 24580
  175.7 5.5 %copy-start.49 = (f32[16,128]{1,0:T(8,128)S(1)}, f32[16,128]{1,0:T(8,128)}, u32[]{:S(2)}) copy-start(f32[16,128]{1,0:T(8,128)} %get-tuple-element.45) | copy-start | bytes 24580
  175.7 5.5 %copy-start.51 = (f32[16,128]{1,0:T(8,128)S(1)}, f32[16,128]{1,0:T(8,128)}, u32[]{:S(2)}) copy-start(f32[16,128]{1,0:T(8,128)} %get-tuple-element.46) | copy-start | bytes 24580
  175.7 5.5 %copy-start.53 = (f32[16,128]{1,0:T(8,128)S(1)}, f32[16,128]{1,0:T(8,128)}, u32[]{:S(2)}) copy-start(f32[16,128]{1,0:T(8,128)} %get-tuple-element.47) | copy-start | bytes 24580
  (39 other events, 178.4 us)
Sparse Core Ops, SparseCore 0:
  175.6 274.3 all-reduce.2
where the time goes:
time: 462 us; the launch traced here: 460 us
  waiting for transfers between devices  262 us (57%)
  other arithmetic  72.7 us (16%)
  starting transfers between devices  58.2 us (13%)
  local copies, waits for them, and re-layouts  38.9 us (8%)
  between operations  15.6 us (3%)
  matrix products  12.3 us (3%)
    psum x1, waiting for transfers between devices, body(): first_total = lax.psum(weight_grad(first_flat, pre_grad), ('row', 'col'))  256 us
    ppermute x10, starting transfers between devices, extended_2(): lax.ppermute(head, axis, [((i + 1) % count, i) for i in range(ends)])  31.7 us
    convert_element_type x6, other arithmetic, feature_stack(): stencil_apply(extended, coefficients[operator], height, breadth)  28.2 us
    ppermute x10, starting transfers between devices, extended_2(): lax.ppermute(tail, axis, [(i, (i + 1) % count) for i in range(ends)])  26.4 us
    add x2, other arithmetic, apply_transposed(): accumulated = addend if accumulated is None else accumulated + addend  19.9 us
    slice x8, local copies, waits for them, and re-layouts, extended_2(): lax.slice_in_dim(cells, cells.shape[dim] - width, cells.shape[dim], axis=...  11.4 us
    concatenate x5, other arithmetic, extended_2(): jnp.concatenate([lax.ppermute(tail, axis, [(i, (i + 1) % count) for i in...  10.2 us
  transfers between devices with their start and end apart: 21, of which 4 were waited for; matrix products, arithmetic and copies ran while one was open for 20% of the time, Pallas kernels for 0%

commit v1 on v0

v1 whole, which is shorter than its diff:
```python
import functools
import math

import jax
import jax.numpy as jnp
from jax import lax
from jax.experimental import pallas as pl
from jax.experimental.pallas import tpu as pltpu
from jax.sharding import PartitionSpec as P

F32 = jnp.float32
BF16 = jnp.bfloat16
BOTH = ("row", "col")
SLOTS = 32
VMEM_LIMIT = 56 * 1024 * 1024


def dot(lhs, rhs, lhs_dim, rhs_dim):
    return lax.dot_general(
        lhs, rhs, (((lhs_dim,), (rhs_dim,)), ((), ())), preferred_element_type=F32
    )


def iota(shape, dim):
    return lax.broadcasted_iota(jnp.int32, shape, dim)


def as_mask(condition):
    return jnp.where(condition, 1.0, 0.0).astype(BF16)


def halves(value):
    return jnp.concatenate([value[:, :128], value[:, 128:]], axis=0)


def whole(ref, start, rows):
    return jnp.concatenate([ref[start : start + rows], ref[start + rows : start + 2 * rows]], axis=1)


def pack_kernel(f_ref, c_ref, st_ref, stt_ref, up_ref, down_ref, left_ref, right_ref, ul_ref, dr_ref):
    height, breadth, _ = f_ref.shape
    for row, out in ((0, up_ref), (height - 1, down_ref)):
        out[0 : 2 * breadth] = halves(f_ref[row])
        out[2 * breadth : 4 * breadth] = halves(c_ref[row])
        out[4 * breadth : 4 * breadth + SLOTS] = stt_ref[row]
    for col, first, out in ((0, (2, 6), left_ref), (breadth - 1, (1, 5), right_ref)):
        base = 0 if col == 0 else breadth - 16
        for which, ref in enumerate((f_ref, c_ref)):
            edge = ref[:, base : base + 16, :].astype(F32)[:, col - base, :]
            out[which * 2 * height : (which + 1) * 2 * height] = halves(edge).astype(BF16)
        for which, slot in enumerate(first):
            for k in range(3):
                start = 4 * height + (which * 3 + k) * height
                out[start : start + height] = st_ref[7 * k + slot]
    for row, col, slot, out in ((0, 0, 6, ul_ref), (height - 1, breadth - 1, 5, dr_ref)):
        base = 0 if col == 0 else breadth - 16
        lines = []
        for ref in (f_ref, c_ref):
            edge = ref[row, base : base + 16, :].astype(F32)[col - base : col - base + 1]
            lines += [edge[:, :128], edge[:, 128:]]
        weights = stt_ref[row].astype(F32)
        lines += [weights[7 * k + slot : 7 * k + slot + 1] for k in range(3)]
        lines.append(jnp.zeros((16 - len(lines), 128), F32))
        out[...] = jnp.concatenate(lines, axis=0).astype(BF16)


def pack(features, cotangent, stencil, stencil_t):
    height, breadth, _ = features.shape
    sizes = (4 * breadth + SLOTS,) * 2 + (10 * height,) * 2 + (16, 16)
    return pl.pallas_call(
        pack_kernel,
        out_shape=[jax.ShapeDtypeStruct((n, 128), BF16) for n in sizes],
        compiler_params=pltpu.CompilerParams(vmem_limit_bytes=VMEM_LIMIT),
        name="pack_rims",
    )(features, cotangent, stencil, stencil_t)


def exchange(messages, joint):
    up, down, left, right, up_left, down_right = messages
    rows, cols = lax.axis_size("row"), lax.axis_size("col")
    index = lambda r, c: r * cols + c % cols
    below = lax.ppermute(up, "row", [(i + 1, i) for i in range(rows - 1)])
    above = lax.ppermute(down, "row", [(i, i + 1) for i in range(rows - 1)])
    right_rim = lax.ppermute(left, "col", [((i + 1) % cols, i) for i in range(cols)])
    left_rim = lax.ppermute(right, "col", [(i, (i + 1) % cols) for i in range(cols)])
    corner_br = lax.ppermute(
        up_left, BOTH, [(index(r + 1, c + 1), index(r, c)) for r in range(rows - 1) for c in range(cols)]
    )
    corner_tl = lax.ppermute(
        down_right, BOTH, [(index(r, c), index(r + 1, c + 1)) for r in range(rows - 1) for c in range(cols)]
    )
    return above, below, left_rim, right_rim, corner_tl, corner_br


def fill_masks(mask_ref):
    j, c = iota((128, 128), 0), iota((128, 128), 1)
    mask_ref[0] = as_mask(j == c)
    mask_ref[1] = as_mask(j == c + 1)
    mask_ref[2] = as_mask(j == c - 1)
    mask_ref[3] = as_mask(((j == 0) & (c < 2)) | ((j == 127) & ((c == 2) | (c == 3))))
    e, l = iota((16, 128), 0), iota((16, 128), 1)
    spots = ((0, 0), (1, 0), (2, 127), (3, 127))
    for number, (edge, lane) in enumerate(spots):
        mask_ref[4, 16 * number : 16 * number + 16] = as_mask((e == edge) & (l == lane))


def fill_weights(stt_ref, above_ref, below_ref, left_ref, right_ref, tl_ref, br_ref, wx_ref, we_ref):
    height, _, breadth = stt_ref.shape
    base = 4 * breadth
    wx_ref[0] = above_ref[base : base + SLOTS].astype(F32)
    for r in range(height):
        wx_ref[1 + r] = stt_ref[r].astype(F32)
    wx_ref[height + 1] = below_ref[base : base + SLOTS].astype(F32)
    lane = iota((height, 128), 1)

    def spot(value, shift, place):
        rolled = pltpu.roll(value.astype(F32), shift, 1)
        return jnp.where(lane[: value.shape[0]] == place, rolled, 0.0)

    for k in range(3):
        near = 4 * height + k * height
        far = near + 3 * height
        we_ref[0, k, 8 : 8 + height] = spot(left_ref[near : near + height], 1, 0) + spot(
            right_ref[near : near + height], 2, 2
        )
        we_ref[1, k, 8 : 8 + height] = spot(left_ref[far : far + height], 2, 1)
        we_ref[1, k, 0:8] = jnp.broadcast_to(spot(tl_ref[...], 2, 1)[4 + k : 5 + k], (8, 128))
        we_ref[2, k, 8 : 8 + height] = spot(right_ref[far : far + height], 3, 3)
        we_ref[2, k, 8 + height : 16 + height] = jnp.broadcast_to(
            spot(br_ref[...], 3, 3)[4 + k : 5 + k], (8, 128)
        )


def fill_sides(left, right, tl, br, lx_ref, rx_ref):
    height = left.shape[0]
    lx_ref[0:8] = jnp.broadcast_to(tl.astype(F32), (8, tl.shape[1]))
    lx_ref[8 : 8 + height] = left.astype(F32)
    rx_ref[0:height] = right.astype(F32)
    rx_ref[height : height + 8] = jnp.broadcast_to(br.astype(F32), (8, br.shape[1]))


def line(weights, slot):
    return jnp.broadcast_to(weights[slot : slot + 1], (16, 128)).astype(BF16)


def tall(value):
    return jnp.concatenate([value] * 8, axis=0)


def field_block(ext_ref, lx_ref, rx_ref, r):
    channels = ext_ref.shape[2]
    e = iota((16, channels), 0)
    edge = jnp.where(e == 0, lx_ref[pl.ds(r + 8, 1)], 0.0)
    edge = jnp.where(e == 1, lx_ref[pl.ds(r + 7, 1)], edge)
    edge = jnp.where(e == 2, rx_ref[pl.ds(r, 1)], edge)
    edge = jnp.where(e == 3, rx_ref[pl.ds(r + 1, 1)], edge)
    rows = ext_ref[pl.ds(r, 3)].reshape(384, channels)
    return jnp.concatenate([rows, edge.astype(BF16), jnp.zeros((112, channels), BF16)], axis=0)


def forward_band(wx_ref, mask_ref, r):
    weights = wx_ref[r + 1]
    same, ahead, back = mask_ref[0], mask_ref[1], mask_ref[2]
    bands = []
    for k in range(3):
        w = [line(weights, 7 * k + s) for s in range(7)]
        t = [tall(x) for x in w]
        spots = [mask_ref[4, 16 * n : 16 * n + 16] for n in range(4)]
        edge = spots[0] * w[2] + spots[1] * w[6] + spots[2] * w[1] + spots[3] * w[5]
        bands.append(
            jnp.concatenate(
                [
                    same * t[4] + back * t[6],
                    same * t[0] + ahead * t[1] + back * t[2],
                    same * t[3] + ahead * t[5],
                    edge,
                    jnp.zeros((112, 128), BF16),
                ],
                axis=0,
            )
        )
    return jnp.concatenate(bands, axis=1)


def transposed_band(wx_ref, we_ref, mask_ref, r):
    before, here, after = wx_ref[r], wx_ref[r + 1], wx_ref[r + 2]
    same, ahead, back = mask_ref[0], mask_ref[1], mask_ref[2]
    bands = []
    for k in range(3):
        at = lambda weights, slot: tall(line(weights, 7 * k + slot))
        beside = (
            we_ref[0, k, pl.ds(r + 8, 1)] + we_ref[1, k, pl.ds(r + 7, 1)] + we_ref[2, k, pl.ds(r + 9, 1)]
        )
        beside = jnp.broadcast_to(beside, (16, 128)).astype(BF16)
        bands.append(
            jnp.concatenate(
                [
                    same * at(before, 3) + ahead * at(before, 5),
                    same * at(here, 0) + ahead * at(here, 1) + back * at(here, 2),
                    same * at(after, 4) + back * at(after, 6),
                    mask_ref[3] * tall(beside),
                ],
                axis=1,
            )
        )
    return jnp.concatenate(bands, axis=0)


def spread(products):
    return [products[128 * k : 128 * k + 128].astype(BF16) for k in range(3)]


def gradient_kernel(
    ids_ref, f_ref, c_ref, stt_ref, above_ref, below_ref, left_ref, right_ref, tl_ref, br_ref,
    w1_ref, w2_ref,
    g_ref, up_ref, down_ref, gl_ref, gr_ref, ul_ref, dr_ref, keep_ref, send_ref,
    fext_ref, cext_ref, ff_ref, tt_ref, wx_ref, we_ref, flx_ref, frx_ref, clx_ref, crx_ref,
    mask_ref, total_ref, glx_ref, grx_ref,
):
    height, breadth, channels = f_ref.shape
    fill_masks(mask_ref)
    fill_weights(
        stt_ref, above_ref, below_ref, left_ref, right_ref, tl_ref, br_ref, wx_ref, we_ref
    )
    for which, (src, ext, lx, rx) in enumerate(
        ((f_ref, fext_ref, flx_ref, frx_ref), (c_ref, cext_ref, clx_ref, crx_ref))
    ):
        start = which * 2 * breadth
        ext[0] = whole(above_ref, start, breadth)
        ext[1 : 1 + height] = src[...]
        ext[1 + height] = whole(below_ref, start, breadth)
        side = which * 2 * height
        corner = lambda ref: jnp.concatenate(
            [ref[...].astype(F32)[2 * which : 2 * which + 1], ref[...].astype(F32)[2 * which + 1 : 2 * which + 2]],
            axis=1,
        )
        fill_sides(
            whole(left_ref, side, height), whole(right_ref, side, height), corner(tl_ref), corner(br_ref), lx, rx
        )

    @pl.loop(0, height)
    def _(r):
        rows = pl.ds(pl.multiple_of(r * 128, 128), 128)
        forward = dot(forward_band(wx_ref, mask_ref, r), field_block(fext_ref, flx_ref, frx_ref, r), 0, 0)
        ff_ref[rows] = jnp.concatenate([fext_ref[r + 1]] + spread(forward), axis=1)
        turned = dot(
            transposed_band(wx_ref, we_ref, mask_ref, r), field_block(cext_ref, clx_ref, crx_ref, r), 1, 0
        )
        tt_ref[rows] = jnp.concatenate([cext_ref[r + 1]] + spread(turned), axis=1)

    total_ref[...] = jnp.zeros_like(total_ref)
    batch = 4

    @pl.loop(0, height // batch)
    def _(i):
        rows = pl.ds(pl.multiple_of(i * batch * 128, batch * 128), batch * 128)
        pre = dot(ff_ref[rows], w1_ref[...], 1, 0)
        hidden_grad = dot(tt_ref[rows], w2_ref[...], 1, 0)
        gate = jax.nn.sigmoid(pre)
        hidden = (pre * gate).astype(BF16)
        grad = hidden_grad * gate * (1.0 + pre * (1.0 - gate))
        for q in range(batch):
            g_ref[i * batch + q] = grad[q * 128 : q * 128 + 128].astype(BF16)
            glx_ref[pl.ds(i * batch + q, 1)] = grad[q * 128 : q * 128 + 1]
            grx_ref[pl.ds(i * batch + q, 1)] = grad[q * 128 + 127 : q * 128 + 128]
        second = dot(hidden, tt_ref[rows], 0, 0)
        for k in range(4):
            total_ref[0, 4 * k : 4 * k + 4] += second[:, k * channels : (k + 1) * channels].reshape(
                4, channels // 4, channels
            )
        first = dot(ff_ref[rows], grad.astype(BF16), 0, 0)
        total_ref[1] += first.reshape(16, channels // 4, channels)

    up_ref[...] = g_ref[0]
    down_ref[...] = g_ref[height - 1]
    gl_ref[...] = glx_ref[...].astype(BF16)
    gr_ref[...] = grx_ref[...].astype(BF16)
    ul_ref[...] = jnp.broadcast_to(glx_ref[0:1], (16, channels)).astype(BF16)
    dr_ref[...] = jnp.broadcast_to(grx_ref[height - 1 : height], (16, channels)).astype(BF16)
    core, x, y = ids_ref[0], ids_ref[1], ids_ref[2]
    for dx in range(4):
        for dy in range(4):
            chunk = jnp.bitwise_xor(x, dx) * 4 + jnp.bitwise_xor(y, dy)
            keep_ref[4 * dx + dy] = total_ref[core, chunk]
            send_ref[4 * dx + dy] = total_ref[1 - core, chunk]


def input_kernel(
    g_ref, gabove_ref, gbelow_ref, gleft_ref, gright_ref, gtl_ref, gbr_ref,
    stt_ref, above_ref, below_ref, left_ref, right_ref, tl_ref, br_ref, w1t_ref,
    out_ref,
    gext_ref, tt_ref, wx_ref, we_ref, lx_ref, rx_ref, mask_ref,
):
    height, breadth, channels = g_ref.shape
    fill_masks(mask_ref)
    fill_weights(
        stt_ref, above_ref, below_ref, left_ref, right_ref, tl_ref, br_ref, wx_ref, we_ref
    )
    gext_ref[0] = gabove_ref[...]
    gext_ref[1 : 1 + height] = g_ref[...]
    gext_ref[1 + height] = gbelow_ref[...]
    fill_sides(
        gleft_ref[...], gright_ref[...], gtl_ref[...].astype(F32)[0:1], gbr_ref[...].astype(F32)[0:1], lx_ref, rx_ref
    )

    @pl.loop(0, height)
    def _(r):
        rows = pl.ds(pl.multiple_of(r * 128, 128), 128)
        turned = dot(
            transposed_band(wx_ref, we_ref, mask_ref, r), field_block(gext_ref, lx_ref, rx_ref, r), 1, 0
        )
        tt_ref[rows] = jnp.concatenate([gext_ref[r + 1]] + spread(turned), axis=1)

    batch = 4

    @pl.loop(0, height // batch)
    def _(i):
        rows = pl.ds(pl.multiple_of(i * batch * 128, batch * 128), batch * 128)
        result = dot(tt_ref[rows], w1t_ref[...], 1, 0).astype(BF16)
        for q in range(batch):
            out_ref[i * batch + q] = result[q * 128 : q * 128 + 128]


def final_kernel(scale, ids_ref, *refs):
    mine, theirs, out_refs = refs[:4], refs[4:8], refs[8:]
    core, x, y = ids_ref[0], ids_ref[1], ids_ref[2]
    first_core = core == 0
    for dx in range(4):
        for dy in range(4):
            chunk = jnp.bitwise_xor(x, dx) * 4 + jnp.bitwise_xor(y, dy)
            a = mine[dx][dy].astype(F32) * scale
            b = theirs[dx][dy].astype(F32) * scale
            out_refs[0][chunk] = jnp.where(first_core, a, b)
            out_refs[1][chunk] = jnp.where(first_core, b, a)


SMEM_SPEC = pl.BlockSpec(memory_space=pltpu.SMEM)
VMEM_SPEC = pl.BlockSpec(memory_space=pltpu.VMEM)


def gradients(ids, features, cotangent, stencil_t, rims, w1, w2t):
    height, breadth, channels = features.shape
    shape = jax.ShapeDtypeStruct
    totals = (16, channels // 4, channels)
    vertices = height * breadth
    return pl.pallas_call(
        gradient_kernel,
        out_shape=[
            shape((height, breadth, channels), BF16),
            shape((breadth, channels), BF16),
            shape((breadth, channels), BF16),
            shape((height, channels), BF16),
            shape((height, channels), BF16),
            shape((16, channels), BF16),
            shape((16, channels), BF16),
            shape(totals, F32),
            shape(totals, F32),
        ],
        in_specs=[SMEM_SPEC] + [VMEM_SPEC] * 11,
        scratch_shapes=[
            pltpu.VMEM((height + 2, breadth, channels), BF16),
            pltpu.VMEM((height + 2, breadth, channels), BF16),
            pltpu.VMEM((vertices, 4 * channels), BF16),
            pltpu.VMEM((vertices, 4 * channels), BF16),
            pltpu.VMEM((height + 2, SLOTS, 128), F32),
            pltpu.VMEM((3, 3, height + 16, 128), F32),
        ]
        + [pltpu.VMEM((height + 8, channels), F32)] * 4
        + [
            pltpu.VMEM((5, 128, 128), BF16),
            pltpu.VMEM((2,) + totals, F32),
            pltpu.VMEM((height, channels), F32),
            pltpu.VMEM((height, channels), F32),
        ],
        compiler_params=pltpu.CompilerParams(vmem_limit_bytes=VMEM_LIMIT),
        cost_estimate=pl.CostEstimate(flops=9 * 10**9, bytes_accessed=9 * 10**6, transcendentals=vertices * channels),
        name="weight_gradients",
    )(ids, features, cotangent, stencil_t, *rims, w1, w2t)


def input_gradient(grad, grad_rims, stencil_t, rims, w1t):
    height, breadth, channels = grad.shape
    return pl.pallas_call(
        input_kernel,
        out_shape=jax.ShapeDtypeStruct((height, breadth, channels), BF16),
        in_specs=[VMEM_SPEC] * 15,
        scratch_shapes=[
            pltpu.VMEM((height + 2, breadth, channels), BF16),
            pltpu.VMEM((height * breadth, 4 * channels), BF16),
            pltpu.VMEM((height + 2, SLOTS, 128), F32),
            pltpu.VMEM((3, 3, height + 16, 128), F32),
            pltpu.VMEM((height + 8, channels), F32),
            pltpu.VMEM((height + 8, channels), F32),
            pltpu.VMEM((5, 128, 128), BF16),
        ],
        compiler_params=pltpu.CompilerParams(vmem_limit_bytes=VMEM_LIMIT),
        cost_estimate=pl.CostEstimate(flops=3 * 10**9, bytes_accessed=3 * 10**6, transcendentals=0),
        name="input_gradient",
    )(grad, *grad_rims, stencil_t, *rims, w1t)


def swap(value, row_bits, col_bits):
    rows, cols = lax.axis_size("row"), lax.axis_size("col")
    pairs = [
        (r * cols + c, (r ^ row_bits) * cols + (c ^ col_bits)) for r in range(rows) for c in range(cols)
    ]
    return lax.ppermute(value, BOTH, pairs)


def reduce_both(keep, send):
    total = keep + swap(send, 0, 1)
    parts = [total[4 * d : 4 * d + 4] for d in range(4)]
    came = [swap(parts[d].astype(BF16), 4 * d, 0) for d in (1, 2, 3)]
    total = parts[0] + sum(v.astype(F32) for v in came)
    parts = [total[d] for d in range(4)]
    came = [swap(parts[d].astype(BF16), 0, 2 * d) for d in (1, 2, 3)]
    total = parts[0] + sum(v.astype(F32) for v in came)
    came = [swap(total, d, 0) for d in (1, 2, 3)]
    total = (total + came[0]) + (came[1] + came[2])
    total = (total + swap(total, 0, 8)).astype(BF16)
    gathered = jnp.stack([total] + [swap(total, 0, 2 * d) for d in (1, 2, 3)])
    mine = [gathered] + [swap(gathered, 4 * d, 0) for d in (1, 2, 3)]
    theirs = [swap(v, 0, 1) for v in mine]
    return mine, theirs


def body(features_in, stencil, weights_first, weights_second, cotangent):
    height, breadth, channels = features_in.shape
    scale = 1.0 / math.sqrt(height * breadth * lax.axis_size("row") * lax.axis_size("col"))
    flat = stencil.reshape(21, height, breadth)
    stencil_t = jnp.pad(flat.transpose(1, 0, 2), ((0, 0), (0, SLOTS - 21), (0, 0)))
    row, col = lax.axis_index("row"), lax.axis_index("col")
    ids = jnp.stack([col % 2, row // 4, (col // 2) % 4]).astype(jnp.int32)
    w1 = weights_first.reshape(4 * channels, channels)
    w1t = weights_first.transpose(0, 2, 1).reshape(4 * channels, channels)
    w2t = weights_second.transpose(0, 2, 1).reshape(4 * channels, channels)

    rims = exchange(pack(features_in, cotangent, flat, stencil_t), BOTH)
    grad, *messages, keep, send = gradients(ids, features_in, cotangent, stencil_t, rims, w1, w2t)
    mine, theirs = reduce_both(keep, send)
    input_grad = input_gradient(grad, exchange(messages, BOTH), stencil_t, rims, w1t)
    totals = jax.ShapeDtypeStruct((16, channels // 4, channels), F32)
    second, first = pl.pallas_call(
        functools.partial(final_kernel, scale),
        out_shape=[totals, totals],
        in_specs=[SMEM_SPEC] + [VMEM_SPEC] * 8,
        compiler_params=pltpu.CompilerParams(vmem_limit_bytes=VMEM_LIMIT),
        name="place_totals",
    )(ids, *mine, *theirs)
    shape = (4, channels, channels)
    return input_grad, first.reshape(shape), second.reshape(shape)


def solution(mesh):
    return jax.shard_map(
        body,
        mesh=mesh,
        in_specs=(
            P("row", "col", None),
            P(None, None, "row", "col"),
            P(),
            P(),
            P("row", "col", None),
        ),
        out_specs=(P("row", "col", None), P(), P()),
        check_vma=False,
    )
```

time: 462 us -> 153 us (0.33)
  the two profiles are of different devices: /device:TPU:1 before, /device:TPU:7 now
where the time goes in v1:
time: 153 us
  starting transfers between devices  87.3 us (57%)
  Pallas kernels  30.3 us (20%)
  waiting for transfers between devices  24.8 us (16%)
  local copies, waits for them, and re-layouts  7.13 us (5%)
  other arithmetic  2.19 us (1%)
    ppermute x21, starting transfers between devices, swap(): return lax.ppermute(value, BOTH, pairs)  37.8 us
    ppermute x21, waiting for transfers between devices, swap(): return lax.ppermute(value, BOTH, pairs)  22.4 us
    pallas_call x1, Pallas kernels, gradients(): pl.pallas_call(gradient_kernel, out_shape=[shape((height, breadth, channe...  16.4 us
    ppermute x2, starting transfers between devices, exchange(): lax.ppermute(up_left, BOTH, [(index(r + 1, c + 1), index(r, c)) for r in...  13.5 us
    ppermute x2, starting transfers between devices, exchange(): lax.ppermute(right, 'col', [(i, (i + 1) % cols) for i in range(cols)])  12.1 us
    ppermute x2, starting transfers between devices, exchange(): below = lax.ppermute(up, 'row', [(i + 1, i) for i in range(rows - 1)])  10 us
    pallas_call x1, Pallas kernels, input_gradient(): pl.pallas_call(input_kernel, out_shape=jax.ShapeDtypeStruct((height, brea...  8.7 us
    ppermute x2, starting transfers between devices, exchange(): lax.ppermute(down_right, BOTH, [(index(r, c), index(r + 1, c + 1)) for r...  7.33 us
  transfers between devices with their start and end apart: 33, of which 13 were waited for; matrix products, arithmetic and copies ran while one was open for 2% of the time, Pallas kernels for 6%

profile of v1, /device:TPU:7, one launch (start us, length us, event | category | flops | bytes accessed | tf_op | source)
XLA Modules:
  0.0 152.7 jit_solution(10908639521477483397)
XLA Ops:
  0.6 0.9 copy.16
  1.5 0.7 pad.4.stt_ref
  2.2 2.4 %pack_rims.1 = (bf16[544,128]{1,0:T(8,128)(2,1)}, bf16[544,128]{1,0:T(8,128)(2,1)}, bf16[160,128]{1,0:T(8,128)(2,1)}, bf16[160,128]{1,0:T(8,128)(2,1)}, bf16[16,...) custom-call(bf16[16,128,256]{2,1,0:T(8,128)(2,1)} %f_ref.3, bf16[16,128,256]{2,1,0:T(8,128)(2,1)} %c_ref.3, ...), custom_call_target="tpu_custom_call" | custom-call | tf_op jit(solution)/shard_map/pack_rims/pallas_call | solution.py:70
  4.6 3.5 %collective-permute-start = (bf16[544,128]{1,0:T(8,128)(2,1)}, bf16[544,128]{1,0:T(8,128)(2,1)S(1)}, u32[]{:S(2)}, u32[]{:S(2)}) collective-permute-start(bf16[544,128]{1,0:T(8,128)(2,1)} %get-tuple-element.20), channel_id=1, source_target_pairs={{0,16},{16,32},{32,48},{48,64},{64,80},{80,96},{96,112},{112,128},... | collective-permute-start | bytes 417800 | tf_op jit(solution)/shard_map/ppermute | solution.py:83
  8.1 4.9 %collective-permute-start.1 = (bf16[544,128]{1,0:T(8,128)(2,1)}, bf16[544,128]{1,0:T(8,128)(2,1)S(1)}, u32[]{:S(2)}, u32[]{:S(2)}) collective-permute-start(bf16[544,128]{1,0:T(8,128)(2,1)} %get-tuple-element.21), channel_id=1, source_target_pairs={{16,0},{32,16},{48,32},{64,48},{80,64},{96,80},{112,96},{128,112},... | collective-permute-start | bytes 417800 | tf_op jit(solution)/shard_map/ppermute | solution.py:82
  13.0 2.5 %collective-permute-start.4 = (bf16[16,128]{1,0:T(8,128)(2,1)}, bf16[16,128]{1,0:T(8,128)(2,1)S(1)}, u32[]{:S(2)}, u32[]{:S(2)}) collective-permute-start(bf16[16,128]{1,0:T(8,128)(2,1)} %get-tuple-element.24), channel_id=1, source_target_pairs={{0,17},{1,18},{2,19},{3,20},{4,21},{5,22},{6,23},{7,24},{8,25},{9,... | collective-permute-start | bytes 12296 | tf_op jit(solution)/shard_map/ppermute | solution.py:89
  15.6 5.7 %collective-permute-start.5 = (bf16[16,128]{1,0:T(8,128)(2,1)S(1)}, bf16[16,128]{1,0:T(8,128)(2,1)S(1)}, u32[]{:S(2)}, u32[]{:S(2)}) collective-permute-start(bf16[16,128]{1,0:T(8,128)(2,1)S(1)} %copy-done.29), channel_id=1, source_target_pairs={{17,0},{18,1},{19,2},{20,3},{21,4},{22,5},{23,6},{24,7},{25,8},{26... | collective-permute-start | bytes 12296 | tf_op jit(solution)/shard_map/ppermute | solution.py:86
  21.3 3.1 %collective-permute-start.2 = (bf16[160,128]{1,0:T(8,128)(2,1)}, bf16[160,128]{1,0:T(8,128)(2,1)S(1)}, u32[]{:S(2)}, u32[]{:S(2)}) collective-permute-start(bf16[160,128]{1,0:T(8,128)(2,1)} %get-tuple-element.22), channel_id=1, source_target_pairs={{0,1},{1,2},{2,3},{3,4},{4,5},{5,6},{6,7},{7,8},{8,9},{9,10},{10,1... | collective-permute-start | bytes 122888 | tf_op jit(solution)/shard_map/ppermute | solution.py:85
  24.4 0.8 copy-done.18
  25.2 0.7 pad_add_fusion.ids_ref
  25.9 1.0 copy.13
  26.9 1.7 %collective-permute-done.3.right_ref = bf16[160,128]{1,0:T(8,128)(2,1)S(1)} collective-permute-done((bf16[160,128]{1,0:T(8,128)(2,1)S(1)}, bf16[160,128]{1,0:T(8,128)(2,1)S(1)}, u32[]{:S(2)}, u32[]{:S(2)}) %collective-permute-start.3) | collective-permute-done | bytes 40992 | tf_op jit(solution)/shard_map/ppermute | solution.py:84
  28.7 0.6 copy-done.17
  29.3 0.1 copy-done.10
  29.3 0.0 copy-done.11
  29.4 16.4 %weight_gradients.1 = (bf16[16,128,256]{2,1,0:T(8,128)(2,1)}, bf16[128,256]{1,0:T(8,128)(2,1)}, bf16[128,256]{1,0:T(8,128)(2,1)}, bf16[16,256]{1,0:T(8,128)(2,1)...) custom-call(s32[3]{0:T(128)} %pad_add_fusion.ids_ref, ...), custom_call_target="tpu_custom_call" | custom-call | flops 8999999488 | bytes 9000000 | tf_op jit(solution)/shard_map/weight_gradients/pallas_call | solution.py:346
  45.8 5.6 %collective-permute-start.12 = (f32[16,64,256]{2,1,0:T(8,128)}, f32[16,64,256]{2,1,0:T(8,128)S(1)}, u32[]{:S(2)}, u32[]{:S(2)}) collective-permute-start(f32[16,64,256]{2,1,0:T(8,128)} %get-tuple-element.34), channel_id=1, source_target_pairs={{0,1},{1,0},{2,3},{3,2},{4,5},{5,4},{6,7},{7,6},{8,9},{9,8},{10,11... | collective-permute-start | bytes 3145736 | tf_op jit(solution)/shard_map/ppermute | solution.py:407
  51.3 2.5 %collective-permute-done.12 = f32[16,64,256]{2,1,0:T(8,128)S(1)} collective-permute-done((f32[16,64,256]{2,1,0:T(8,128)}, f32[16,64,256]{2,1,0:T(8,128)S(1)}, u32[]{:S(2)}, u32[]{:S(2)}) %collective-permute-start.12) | collective-permute-done | bytes 1048608 | tf_op jit(solution)/shard_map/ppermute | solution.py:407
  53.8 1.4 fusion.2
  55.3 0.5 collective-permute-start.13
  55.8 0.8 collective-permute-start.15
  56.6 2.0 %collective-permute-start.14 = (bf16[4,64,256]{2,1,0:T(8,128)(2,1)S(1)}, bf16[4,64,256]{2,1,0:T(8,128)(2,1)S(1)}, u32[]{:S(2)}, u32[]{:S(2)}) collective-permute-start(bf16[4,64,256]{2,1,0:T(8,128)(2,1)S(1)} %get-tuple-element.43), channel_id=1, source_target_pairs={{0,128},{1,129},{2,130},{3,131},{4,132},{5,133},{6,134},{7,135},{8... | collective-permute-start | bytes 393224 | tf_op jit(solution)/shard_map/ppermute | solution.py:407
  58.6 1.5 collective-permute-done.13
  60.1 4.1 %collective-permute-done.15 = bf16[4,64,256]{2,1,0:T(8,128)(2,1)S(1)} collective-permute-done((bf16[4,64,256]{2,1,0:T(8,128)(2,1)S(1)}, bf16[4,64,256]{2,1,0:T(8,128)(2,1)S(1)}, u32[]{:S(2)}, u32[]{:S(2)}) %collective-permute-start.15) | collective-permute-done | bytes 131104 | tf_op jit(solution)/shard_map/ppermute | solution.py:407
  64.2 0.1 fusion.1
  64.3 0.1 collective-permute-start.16
  64.4 9.9 %collective-permute-start.18 = (bf16[64,256]{1,0:T(8,128)(2,1)S(1)}, bf16[64,256]{1,0:T(8,128)(2,1)S(1)}, u32[]{:S(2)}, u32[]{:S(2)}) collective-permute-start(bf16[64,256]{1,0:T(8,128)(2,1)S(1)} %get-tuple-element.45), channel_id=1, source_target_pairs={{0,6},{1,7},{2,4},{3,5},{4,2},{5,3},{6,0},{7,1},{8,14},{9,15},{10,... | collective-permute-start | bytes 98312 | tf_op jit(solution)/shard_map/ppermute | solution.py:407
  74.3 1.1 collective-permute-start.17
  75.3 0.2 collective-permute-done.18
  75.6 3.2 %collective-permute-done.17 = bf16[64,256]{1,0:T(8,128)(2,1)S(1)} collective-permute-done((bf16[64,256]{1,0:T(8,128)(2,1)S(1)}, bf16[64,256]{1,0:T(8,128)(2,1)S(1)}, u32[]{:S(2)}, u32[]{:S(2)}) %collective-permute-start.17) | collective-permute-done | bytes 32800 | tf_op jit(solution)/shard_map/ppermute | solution.py:407
  78.7 0.4 collective-permute-start.21
  79.2 3.2 %collective-permute-start.19 = (f32[64,256]{1,0:T(8,128)S(1)}, f32[64,256]{1,0:T(8,128)S(1)}, u32[]{:S(2)}, u32[]{:S(2)}) collective-permute-start(f32[64,256]{1,0:T(8,128)S(1)} %fusion), channel_id=1, source_target_pairs={{0,16},{1,17},{2,18},{3,19},{4,20},{5,21},{6,22},{7,23},{8,24},{9,... | collective-permute-start | bytes 196616 | tf_op jit(solution)/shard_map/ppermute | solution.py:407
  82.4 1.5 collective-permute-done.21
  83.9 1.1 collective-permute-done.20
  85.0 0.7 collective-permute-start.22
  85.8 6.6 %collective-permute-done.22 = f32[64,256]{1,0:T(8,128)S(1)} collective-permute-done((f32[64,256]{1,0:T(8,128)S(1)}, f32[64,256]{1,0:T(8,128)S(1)}, u32[]{:S(2)}, u32[]{:S(2)}) %collective-permute-start.22) | collective-permute-done | bytes 65568 | tf_op jit(solution)/shard_map/ppermute | solution.py:407
  92.4 0.1 collective-permute-start.25
  92.5 1.7 %collective-permute-start.24 = (bf16[64,256]{1,0:T(8,128)(2,1)S(1)}, bf16[64,256]{1,0:T(8,128)(2,1)S(1)}, u32[]{:S(2)}, u32[]{:S(2)}) collective-permute-start(bf16[64,256]{1,0:T(8,128)(2,1)S(1)} %add_convert_fusion), channel_id=1, source_target_pairs={{0,4},{1,5},{2,6},{3,7},{4,0},{5,1},{6,2},{7,3},{8,12},{9,13},{10,... | collective-permute-start | bytes 98312 | tf_op jit(solution)/shard_map/ppermute | solution.py:407
  94.2 1.5 collective-permute-start.23
  95.7 1.0 collective-permute-done.25
  96.8 0.4 collective-permute-done.24
  97.2 0.3 collective-permute-done.23
  97.5 1.3 collective-permute-start.28
  98.8 0.2 collective-permute-start.27
  99.0 1.9 %collective-permute-start.26 = (bf16[4,64,256]{2,1,0:T(8,128)(2,1)S(1)}, bf16[4,64,256]{2,1,0:T(8,128)(2,1)S(1)}, u32[]{:S(2)}, u32[]{:S(2)}) collective-permute-start(bf16[4,64,256]{2,1,0:T(8,128)(2,1)S(1)} %pad_maximum_fusion.refs_0_), channel_id=1, source_target_pairs={{0,64},{1,65},{2,66},{3,67},{4,68},{5,69},{6,70},{7,71},{8,72},{9,... | collective-permute-start | bytes 393224 | tf_op jit(solution)/shard_map/ppermute | solution.py:407
  100.8 9.0 %collective-permute-start.8 = (bf16[16,256]{1,0:T(8,128)(2,1)S(1)}, bf16[16,256]{1,0:T(8,128)(2,1)S(1)}, u32[]{:S(2)}, u32[]{:S(2)}) collective-permute-start(bf16[16,256]{1,0:T(8,128)(2,1)S(1)} %copy-done.22), channel_id=1, source_target_pairs={{0,1},{1,2},{2,3},{3,4},{4,5},{5,6},{6,7},{7,8},{8,9},{9,10},{10,1... | collective-permute-start | bytes 24584 | tf_op jit(solution)/shard_map/ppermute | solution.py:85
  109.8 0.1 collective-permute-start.9
  109.9 0.7 collective-permute-done.8.gleft_ref
  110.6 4.8 %collective-permute-start.10 = (bf16[16,256]{1,0:T(8,128)(2,1)S(1)}, bf16[16,256]{1,0:T(8,128)(2,1)S(1)}, u32[]{:S(2)}, u32[]{:S(2)}) collective-permute-start(bf16[16,256]{1,0:T(8,128)(2,1)S(1)} %copy-done.20), channel_id=1, source_target_pairs={{0,17},{1,18},{2,19},{3,20},{4,21},{5,22},{6,23},{7,24},{8,25},{9,... | collective-permute-start | bytes 24584 | tf_op jit(solution)/shard_map/ppermute | solution.py:89
  115.5 7.8 %collective-permute-start.11 = (bf16[16,256]{1,0:T(8,128)(2,1)S(1)}, bf16[16,256]{1,0:T(8,128)(2,1)S(1)}, u32[]{:S(2)}, u32[]{:S(2)}) collective-permute-start(bf16[16,256]{1,0:T(8,128)(2,1)S(1)} %copy-done.19), channel_id=1, source_target_pairs={{17,0},{18,1},{19,2},{20,3},{21,4},{22,5},{23,6},{24,7},{25,8},{26... | collective-permute-start | bytes 24584 | tf_op jit(solution)/shard_map/ppermute | solution.py:86
  123.3 2.9 %collective-permute-start.6 = (bf16[128,256]{1,0:T(8,128)(2,1)S(1)}, bf16[128,256]{1,0:T(8,128)(2,1)S(1)}, u32[]{:S(2)}, u32[]{:S(2)}) collective-permute-start(bf16[128,256]{1,0:T(8,128)(2,1)S(1)} %copy-done.13), channel_id=1, source_target_pairs={{0,16},{16,32},{32,48},{48,64},{64,80},{80,96},{96,112},{112,128},... | collective-permute-start | bytes 196616 | tf_op jit(solution)/shard_map/ppermute | solution.py:83
  126.1 5.1 %collective-permute-start.7 = (bf16[128,256]{1,0:T(8,128)(2,1)S(1)}, bf16[128,256]{1,0:T(8,128)(2,1)S(1)}, u32[]{:S(2)}, u32[]{:S(2)}) collective-permute-start(bf16[128,256]{1,0:T(8,128)(2,1)S(1)} %copy-done.12), channel_id=1, source_target_pairs={{16,0},{32,16},{48,32},{64,48},{80,64},{96,80},{112,96},{128,112},... | collective-permute-start | bytes 196616 | tf_op jit(solution)/shard_map/ppermute | solution.py:82
  131.3 1.0 copy.14
  132.3 6.2 %collective-permute-start.29 = (bf16[4,64,256]{2,1,0:T(8,128)(2,1)S(1)}, bf16[4,64,256]{2,1,0:T(8,128)(2,1)S(1)}, u32[]{:S(2)}, u32[]{:S(2)}) collective-permute-start(bf16[4,64,256]{2,1,0:T(8,128)(2,1)S(1)} %pad_maximum_fusion.refs_0_), channel_id=1, source_target_pairs={{0,1},{1,0},{2,3},{3,2},{4,5},{5,4},{6,7},{7,6},{8,9},{9,8},{10,11... | collective-permute-start | bytes 393224 | tf_op jit(solution)/shard_map/ppermute | solution.py:407
  138.5 0.1 collective-permute-start.32
  138.7 0.4 collective-permute-start.31
  139.1 0.1 collective-permute-start.30
  139.2 0.6 copy-done.15
  139.8 8.7 %input_gradient.1 = bf16[16,128,256]{2,1,0:T(8,128)(2,1)} custom-call(bf16[16,128,256]{2,1,0:T(8,128)(2,1)} %get-tuple-element.26.g_ref, bf16[128,256]{1,0:T(8,128)(2,1)} %copy-done.14, bf16[128,256]{1,0:T(8,128)(2,1)} %copy-done.15, bf16[16,256]{1,0:T(8,128)(2,1)} %copy-done.23, bf16[16,256]{1,0:T(8,128)(2,1)} %copy-done.24, bf16[16,256]{1,0:T(8,128)(2,1)} %copy-done.25, ...), custom_call_target="tpu_custom_call" | custom-call | flops 3000000000 | bytes 3000000 | tf_op jit(solution)/shard_map/input_gradient/pallas_call | solution.py:383
  148.6 0.6 copy-done.6
  149.2 0.0 copy-done.7
  149.2 0.1 copy-done.8
  149.3 0.6 copy-done.9
  149.9 2.8 %place_totals.1 = (f32[16,64,256]{2,1,0:T(8,128)}, f32[16,64,256]{2,1,0:T(8,128)}) custom-call(s32[3]{0:T(128)} %pad_add_fusion.ids_ref, bf16[4,64,256]{2,1,0:T(8,128)(2,1)} %copy-done.2, bf16[4,64,256]{2,1,0:T(8,128)(2,1)} %copy-done.5, bf16[4,64,256]{2,1,0:T(8,128)(2,1)} %copy-done.4, bf16[4,64,256]{2,1,0:T(8,128)(2,1)} %copy-done.3, ...), custom_call_target="tpu_custom_call" | custom-call | tf_op jit(solution)/shard_map/place_totals/pallas_call | solution.py:443
  (79 shorter events, 0.3 us)
Async XLA Ops:
  2.2 23.7 %copy-start = (bf16[4,256,256]{2,1,0:T(8,128)(2,1)S(1)}, bf16[4,256,256]{2,1,0:T(8,128)(2,1)}, u32[]{:S(2)}) copy-start(bf16[4,256,256]{2,1,0:T(8,128)(2,1)} %param.8) | copy-start | bytes 1572868
  4.6 11.0 %copy-start.29 = (bf16[16,128]{1,0:T(8,128)(2,1)S(1)}, bf16[16,128]{1,0:T(8,128)(2,1)}, u32[]{:S(2)}) copy-start(bf16[16,128]{1,0:T(8,128)(2,1)} %get-tuple-element.25) | copy-start | bytes 12292
  4.6 24.1 %collective-permute-start = (bf16[544,128]{1,0:T(8,128)(2,1)}, bf16[544,128]{1,0:T(8,128)(2,1)S(1)}, u32[]{:S(2)}, u32[]{:S(2)}) collective-permute-start(bf16[544,128]{1,0:T(8,128)(2,1)} %get-tuple-element.20), channel_id=1, source_target_pairs={{0,16},{16,32},{32,48},{48,64},{64,80},{80,96},{96,112},{112,128},... | collective-permute-start | bytes 417800 | tf_op jit(solution)/shard_map/ppermute | solution.py:83
  8.1 20.5 %collective-permute-start.1 = (bf16[544,128]{1,0:T(8,128)(2,1)}, bf16[544,128]{1,0:T(8,128)(2,1)S(1)}, u32[]{:S(2)}, u32[]{:S(2)}) collective-permute-start(bf16[544,128]{1,0:T(8,128)(2,1)} %get-tuple-element.21), channel_id=1, source_target_pairs={{16,0},{32,16},{48,32},{64,48},{80,64},{96,80},{112,96},{128,112},... | collective-permute-start | bytes 417800 | tf_op jit(solution)/shard_map/ppermute | solution.py:82
  13.0 11.4 %collective-permute-start.4 = (bf16[16,128]{1,0:T(8,128)(2,1)}, bf16[16,128]{1,0:T(8,128)(2,1)S(1)}, u32[]{:S(2)}, u32[]{:S(2)}) collective-permute-start(bf16[16,128]{1,0:T(8,128)(2,1)} %get-tuple-element.24), channel_id=1, source_target_pairs={{0,17},{1,18},{2,19},{3,20},{4,21},{5,22},{6,23},{7,24},{8,25},{9,... | collective-permute-start | bytes 12296 | tf_op jit(solution)/shard_map/ppermute | solution.py:89
  15.6 11.3 %collective-permute-start.5 = (bf16[16,128]{1,0:T(8,128)(2,1)S(1)}, bf16[16,128]{1,0:T(8,128)(2,1)S(1)}, u32[]{:S(2)}, u32[]{:S(2)}) collective-permute-start(bf16[16,128]{1,0:T(8,128)(2,1)S(1)} %copy-done.29), channel_id=1, source_target_pairs={{17,0},{18,1},{19,2},{20,3},{21,4},{22,5},{23,6},{24,7},{25,8},{26... | collective-permute-start | bytes 12296 | tf_op jit(solution)/shard_map/ppermute | solution.py:86
  21.3 5.6 %collective-permute-start.2 = (bf16[160,128]{1,0:T(8,128)(2,1)}, bf16[160,128]{1,0:T(8,128)(2,1)S(1)}, u32[]{:S(2)}, u32[]{:S(2)}) collective-permute-start(bf16[160,128]{1,0:T(8,128)(2,1)} %get-tuple-element.22), channel_id=1, source_target_pairs={{0,1},{1,2},{2,3},{3,4},{4,5},{5,6},{6,7},{7,8},{8,9},{9,10},{10,1... | collective-permute-start | bytes 122888 | tf_op jit(solution)/shard_map/ppermute | solution.py:85
  24.4 0.8 copy-start.18
  24.4 1.4 copy-start.27
  25.2 3.4 %collective-permute-start.3 = (bf16[160,128]{1,0:T(8,128)(2,1)S(1)}, bf16[160,128]{1,0:T(8,128)(2,1)S(1)}, u32[]{:S(2)}, u32[]{:S(2)}) collective-permute-start(bf16[160,128]{1,0:T(8,128)(2,1)S(1)} %copy-done.18), channel_id=1, source_target_pairs={{1,0},{2,1},{3,2},{4,3},{5,4},{6,5},{7,6},{8,7},{9,8},{10,9},{11,1... | collective-permute-start | bytes 122888 | tf_op jit(solution)/shard_map/ppermute | solution.py:84
  26.9 1.8 %copy-start.28 = (bf16[16,128]{1,0:T(8,128)(2,1)}, bf16[16,128]{1,0:T(8,128)(2,1)S(1)}, u32[]{:S(2)}) copy-start(bf16[16,128]{1,0:T(8,128)(2,1)S(1)} %collective-permute-done.5.br_ref) | copy-start | bytes 12292
  26.9 1.8 %copy-start.16 = (bf16[160,128]{1,0:T(8,128)(2,1)}, bf16[160,128]{1,0:T(8,128)(2,1)S(1)}, u32[]{:S(2)}) copy-start(bf16[160,128]{1,0:T(8,128)(2,1)S(1)} %collective-permute-done.2.left_ref) | copy-start | bytes 122884
  28.7 0.6 copy-start.17
  28.7 0.7 copy-start.10
  28.7 0.7 copy-start.11
  45.8 8.1 %collective-permute-start.12 = (f32[16,64,256]{2,1,0:T(8,128)}, f32[16,64,256]{2,1,0:T(8,128)S(1)}, u32[]{:S(2)}, u32[]{:S(2)}) collective-permute-start(f32[16,64,256]{2,1,0:T(8,128)} %get-tuple-element.34), channel_id=1, source_target_pairs={{0,1},{1,0},{2,3},{3,2},{4,5},{5,4},{6,7},{7,6},{8,9},{9,8},{10,11... | collective-permute-start | bytes 3145736 | tf_op jit(solution)/shard_map/ppermute | solution.py:407
  55.3 4.8 %collective-permute-start.13 = (bf16[4,64,256]{2,1,0:T(8,128)(2,1)S(1)}, bf16[4,64,256]{2,1,0:T(8,128)(2,1)S(1)}, u32[]{:S(2)}, u32[]{:S(2)}) collective-permute-start(bf16[4,64,256]{2,1,0:T(8,128)(2,1)S(1)} %get-tuple-element.41), channel_id=1, source_target_pairs={{0,64},{1,65},{2,66},{3,67},{4,68},{5,69},{6,70},{7,71},{8,72},{9,... | collective-permute-start | bytes 393224 | tf_op jit(solution)/shard_map/ppermute | solution.py:407
  55.8 8.4 %collective-permute-start.15 = (bf16[4,64,256]{2,1,0:T(8,128)(2,1)S(1)}, bf16[4,64,256]{2,1,0:T(8,128)(2,1)S(1)}, u32[]{:S(2)}, u32[]{:S(2)}) collective-permute-start(bf16[4,64,256]{2,1,0:T(8,128)(2,1)S(1)} %get-tuple-element.42), channel_id=1, source_target_pairs={{0,192},{1,193},{2,194},{3,195},{4,196},{5,197},{6,198},{7,199},{8... | collective-permute-start | bytes 393224 | tf_op jit(solution)/shard_map/ppermute | solution.py:407
  56.6 7.6 %collective-permute-start.14 = (bf16[4,64,256]{2,1,0:T(8,128)(2,1)S(1)}, bf16[4,64,256]{2,1,0:T(8,128)(2,1)S(1)}, u32[]{:S(2)}, u32[]{:S(2)}) collective-permute-start(bf16[4,64,256]{2,1,0:T(8,128)(2,1)S(1)} %get-tuple-element.43), channel_id=1, source_target_pairs={{0,128},{1,129},{2,130},{3,131},{4,132},{5,133},{6,134},{7,135},{8... | collective-permute-start | bytes 393224 | tf_op jit(solution)/shard_map/ppermute | solution.py:407
  64.3 67.0 %copy-start.1 = (bf16[4,256,256]{2,1,0:T(8,128)(2,1)S(1)}, bf16[4,256,256]{2,1,0:T(8,128)(2,1)}, u32[]{:S(2)}) copy-start(bf16[4,256,256]{2,1,0:T(8,128)(2,1)} %param.7) | copy-start | bytes 1572868
  64.3 11.0 %collective-permute-start.16 = (bf16[64,256]{1,0:T(8,128)(2,1)S(1)}, bf16[64,256]{1,0:T(8,128)(2,1)S(1)}, u32[]{:S(2)}, u32[]{:S(2)}) collective-permute-start(bf16[64,256]{1,0:T(8,128)(2,1)S(1)} %get-tuple-element.44), channel_id=1, source_target_pairs={{0,2},{1,3},{2,0},{3,1},{4,6},{5,7},{6,4},{7,5},{8,10},{9,11},{10,... | collective-permute-start | bytes 98312 | tf_op jit(solution)/shard_map/ppermute | solution.py:407
  64.4 11.2 %collective-permute-start.18 = (bf16[64,256]{1,0:T(8,128)(2,1)S(1)}, bf16[64,256]{1,0:T(8,128)(2,1)S(1)}, u32[]{:S(2)}, u32[]{:S(2)}) collective-permute-start(bf16[64,256]{1,0:T(8,128)(2,1)S(1)} %get-tuple-element.45), channel_id=1, source_target_pairs={{0,6},{1,7},{2,4},{3,5},{4,2},{5,3},{6,0},{7,1},{8,14},{9,15},{10,... | collective-permute-start | bytes 98312 | tf_op jit(solution)/shard_map/ppermute | solution.py:407
  74.3 4.5 %collective-permute-start.17 = (bf16[64,256]{1,0:T(8,128)(2,1)S(1)}, bf16[64,256]{1,0:T(8,128)(2,1)S(1)}, u32[]{:S(2)}, u32[]{:S(2)}) collective-permute-start(bf16[64,256]{1,0:T(8,128)(2,1)S(1)} %get-tuple-element.46), channel_id=1, source_target_pairs={{0,4},{1,5},{2,6},{3,7},{4,0},{5,1},{6,2},{7,3},{8,12},{9,13},{10,... | collective-permute-start | bytes 98312 | tf_op jit(solution)/shard_map/ppermute | solution.py:407
  78.7 5.2 %collective-permute-start.21 = (f32[64,256]{1,0:T(8,128)S(1)}, f32[64,256]{1,0:T(8,128)S(1)}, u32[]{:S(2)}, u32[]{:S(2)}) collective-permute-start(f32[64,256]{1,0:T(8,128)S(1)} %fusion), channel_id=1, source_target_pairs={{0,48},{1,49},{2,50},{3,51},{4,52},{5,53},{6,54},{7,55},{8,56},{9,... | collective-permute-start | bytes 196616 | tf_op jit(solution)/shard_map/ppermute | solution.py:407
  79.2 5.8 %collective-permute-start.20 = (f32[64,256]{1,0:T(8,128)S(1)}, f32[64,256]{1,0:T(8,128)S(1)}, u32[]{:S(2)}, u32[]{:S(2)}) collective-permute-start(f32[64,256]{1,0:T(8,128)S(1)} %fusion), channel_id=1, source_target_pairs={{0,32},{1,33},{2,34},{3,35},{4,36},{5,37},{6,38},{7,39},{8,40},{9,... | collective-permute-start | bytes 196616 | tf_op jit(solution)/shard_map/ppermute | solution.py:407
  79.2 5.8 %collective-permute-start.19 = (f32[64,256]{1,0:T(8,128)S(1)}, f32[64,256]{1,0:T(8,128)S(1)}, u32[]{:S(2)}, u32[]{:S(2)}) collective-permute-start(f32[64,256]{1,0:T(8,128)S(1)} %fusion), channel_id=1, source_target_pairs={{0,16},{1,17},{2,18},{3,19},{4,20},{5,21},{6,22},{7,23},{8,24},{9,... | collective-permute-start | bytes 196616 | tf_op jit(solution)/shard_map/ppermute | solution.py:407
  85.0 7.4 %collective-permute-start.22 = (f32[64,256]{1,0:T(8,128)S(1)}, f32[64,256]{1,0:T(8,128)S(1)}, u32[]{:S(2)}, u32[]{:S(2)}) collective-permute-start(f32[64,256]{1,0:T(8,128)S(1)} %add_add_fusion), channel_id=1, source_target_pairs={{0,8},{1,9},{2,10},{3,11},{4,12},{5,13},{6,14},{7,15},{8,0},{9,1},... | collective-permute-start | bytes 196616 | tf_op jit(solution)/shard_map/ppermute | solution.py:407
  92.4 4.4 %collective-permute-start.25 = (bf16[64,256]{1,0:T(8,128)(2,1)S(1)}, bf16[64,256]{1,0:T(8,128)(2,1)S(1)}, u32[]{:S(2)}, u32[]{:S(2)}) collective-permute-start(bf16[64,256]{1,0:T(8,128)(2,1)S(1)} %add_convert_fusion), channel_id=1, source_target_pairs={{0,6},{1,7},{2,4},{3,5},{4,2},{5,3},{6,0},{7,1},{8,14},{9,15},{10,... | collective-permute-start | bytes 98312 | tf_op jit(solution)/shard_map/ppermute | solution.py:407
  92.5 4.7 %collective-permute-start.24 = (bf16[64,256]{1,0:T(8,128)(2,1)S(1)}, bf16[64,256]{1,0:T(8,128)(2,1)S(1)}, u32[]{:S(2)}, u32[]{:S(2)}) collective-permute-start(bf16[64,256]{1,0:T(8,128)(2,1)S(1)} %add_convert_fusion), channel_id=1, source_target_pairs={{0,4},{1,5},{2,6},{3,7},{4,0},{5,1},{6,2},{7,3},{8,12},{9,13},{10,... | collective-permute-start | bytes 98312 | tf_op jit(solution)/shard_map/ppermute | solution.py:407
  94.2 3.2 %collective-permute-start.23 = (bf16[64,256]{1,0:T(8,128)(2,1)S(1)}, bf16[64,256]{1,0:T(8,128)(2,1)S(1)}, u32[]{:S(2)}, u32[]{:S(2)}) collective-permute-start(bf16[64,256]{1,0:T(8,128)(2,1)S(1)} %add_convert_fusion), channel_id=1, source_target_pairs={{0,2},{1,3},{2,0},{3,1},{4,6},{5,7},{6,4},{7,5},{8,10},{9,11},{10,... | collective-permute-start | bytes 98312 | tf_op jit(solution)/shard_map/ppermute | solution.py:407
  97.4 3.4 %copy-start.22 = (bf16[16,256]{1,0:T(8,128)(2,1)S(1)}, bf16[16,256]{1,0:T(8,128)(2,1)}, u32[]{:S(2)}) copy-start(bf16[16,256]{1,0:T(8,128)(2,1)} %get-tuple-element.29) | copy-start | bytes 24580
  97.4 12.4 %copy-start.21 = (bf16[16,256]{1,0:T(8,128)(2,1)S(1)}, bf16[16,256]{1,0:T(8,128)(2,1)}, u32[]{:S(2)}) copy-start(bf16[16,256]{1,0:T(8,128)(2,1)} %get-tuple-element.30) | copy-start | bytes 24580
  97.4 13.2 %copy-start.20 = (bf16[16,256]{1,0:T(8,128)(2,1)S(1)}, bf16[16,256]{1,0:T(8,128)(2,1)}, u32[]{:S(2)}) copy-start(bf16[16,256]{1,0:T(8,128)(2,1)} %get-tuple-element.31) | copy-start | bytes 24580
  97.4 18.0 %copy-start.19 = (bf16[16,256]{1,0:T(8,128)(2,1)S(1)}, bf16[16,256]{1,0:T(8,128)(2,1)}, u32[]{:S(2)}) copy-start(bf16[16,256]{1,0:T(8,128)(2,1)} %get-tuple-element.32) | copy-start | bytes 24580
  97.4 25.8 %copy-start.13 = (bf16[128,256]{1,0:T(8,128)(2,1)S(1)}, bf16[128,256]{1,0:T(8,128)(2,1)}, u32[]{:S(2)}) copy-start(bf16[128,256]{1,0:T(8,128)(2,1)} %get-tuple-element.27) | copy-start | bytes 196612
  97.4 28.7 %copy-start.12 = (bf16[128,256]{1,0:T(8,128)(2,1)S(1)}, bf16[128,256]{1,0:T(8,128)(2,1)}, u32[]{:S(2)}) copy-start(bf16[128,256]{1,0:T(8,128)(2,1)} %get-tuple-element.28) | copy-start | bytes 196612
  97.5 34.8 %copy-start.2 = (bf16[4,64,256]{2,1,0:T(8,128)(2,1)}, bf16[4,64,256]{2,1,0:T(8,128)(2,1)S(1)}, u32[]{:S(2)}) copy-start(bf16[4,64,256]{2,1,0:T(8,128)(2,1)S(1)} %pad_maximum_fusion.refs_0_) | copy-start | bytes 393220
  97.5 41.0 %collective-permute-start.28 = (bf16[4,64,256]{2,1,0:T(8,128)(2,1)S(1)}, bf16[4,64,256]{2,1,0:T(8,128)(2,1)S(1)}, u32[]{:S(2)}, u32[]{:S(2)}) collective-permute-start(bf16[4,64,256]{2,1,0:T(8,128)(2,1)S(1)} %pad_maximum_fusion.refs_0_), channel_id=1, source_target_pairs={{0,192},{1,193},{2,194},{3,195},{4,196},{5,197},{6,198},{7,199},{8... | collective-permute-start | bytes 393224 | tf_op jit(solution)/shard_map/ppermute | solution.py:407
  98.8 39.9 %collective-permute-start.27 = (bf16[4,64,256]{2,1,0:T(8,128)(2,1)S(1)}, bf16[4,64,256]{2,1,0:T(8,128)(2,1)S(1)}, u32[]{:S(2)}, u32[]{:S(2)}) collective-permute-start(bf16[4,64,256]{2,1,0:T(8,128)(2,1)S(1)} %pad_maximum_fusion.refs_0_), channel_id=1, source_target_pairs={{0,128},{1,129},{2,130},{3,131},{4,132},{5,133},{6,134},{7,135},{8... | collective-permute-start | bytes 393224 | tf_op jit(solution)/shard_map/ppermute | solution.py:407
  99.0 40.1 %collective-permute-start.26 = (bf16[4,64,256]{2,1,0:T(8,128)(2,1)S(1)}, bf16[4,64,256]{2,1,0:T(8,128)(2,1)S(1)}, u32[]{:S(2)}, u32[]{:S(2)}) collective-permute-start(bf16[4,64,256]{2,1,0:T(8,128)(2,1)S(1)} %pad_maximum_fusion.refs_0_), channel_id=1, source_target_pairs={{0,64},{1,65},{2,66},{3,67},{4,68},{5,69},{6,70},{7,71},{8,72},{9,... | collective-permute-start | bytes 393224 | tf_op jit(solution)/shard_map/ppermute | solution.py:407
  100.8 9.8 %collective-permute-start.8 = (bf16[16,256]{1,0:T(8,128)(2,1)S(1)}, bf16[16,256]{1,0:T(8,128)(2,1)S(1)}, u32[]{:S(2)}, u32[]{:S(2)}) collective-permute-start(bf16[16,256]{1,0:T(8,128)(2,1)S(1)} %copy-done.22), channel_id=1, source_target_pairs={{0,1},{1,2},{2,3},{3,4},{4,5},{5,6},{6,7},{7,8},{8,9},{9,10},{10,1... | collective-permute-start | bytes 24584 | tf_op jit(solution)/shard_map/ppermute | solution.py:85
  109.8 5.6 %collective-permute-start.9 = (bf16[16,256]{1,0:T(8,128)(2,1)S(1)}, bf16[16,256]{1,0:T(8,128)(2,1)S(1)}, u32[]{:S(2)}, u32[]{:S(2)}) collective-permute-start(bf16[16,256]{1,0:T(8,128)(2,1)S(1)} %copy-done.21), channel_id=1, source_target_pairs={{1,0},{2,1},{3,2},{4,3},{5,4},{6,5},{7,6},{8,7},{9,8},{10,9},{11,1... | collective-permute-start | bytes 24584 | tf_op jit(solution)/shard_map/ppermute | solution.py:84
  110.6 21.7 %copy-start.23 = (bf16[16,256]{1,0:T(8,128)(2,1)}, bf16[16,256]{1,0:T(8,128)(2,1)S(1)}, u32[]{:S(2)}) copy-start(bf16[16,256]{1,0:T(8,128)(2,1)S(1)} %collective-permute-done.8.gleft_ref) | copy-start | bytes 24580
  110.6 12.6 %collective-permute-start.10 = (bf16[16,256]{1,0:T(8,128)(2,1)S(1)}, bf16[16,256]{1,0:T(8,128)(2,1)S(1)}, u32[]{:S(2)}, u32[]{:S(2)}) collective-permute-start(bf16[16,256]{1,0:T(8,128)(2,1)S(1)} %copy-done.20), channel_id=1, source_target_pairs={{0,17},{1,18},{2,19},{3,20},{4,21},{5,22},{6,23},{7,24},{8,25},{9,... | collective-permute-start | bytes 24584 | tf_op jit(solution)/shard_map/ppermute | solution.py:89
  115.4 16.9 %copy-start.24 = (bf16[16,256]{1,0:T(8,128)(2,1)}, bf16[16,256]{1,0:T(8,128)(2,1)S(1)}, u32[]{:S(2)}) copy-start(bf16[16,256]{1,0:T(8,128)(2,1)S(1)} %collective-permute-done.9.gright_ref) | copy-start | bytes 24580
  115.5 10.7 %collective-permute-start.11 = (bf16[16,256]{1,0:T(8,128)(2,1)S(1)}, bf16[16,256]{1,0:T(8,128)(2,1)S(1)}, u32[]{:S(2)}, u32[]{:S(2)}) collective-permute-start(bf16[16,256]{1,0:T(8,128)(2,1)S(1)} %copy-done.19), channel_id=1, source_target_pairs={{17,0},{18,1},{19,2},{20,3},{21,4},{22,5},{23,6},{24,7},{25,8},{26... | collective-permute-start | bytes 24584 | tf_op jit(solution)/shard_map/ppermute | solution.py:86
  123.2 9.1 %copy-start.25 = (bf16[16,256]{1,0:T(8,128)(2,1)}, bf16[16,256]{1,0:T(8,128)(2,1)S(1)}, u32[]{:S(2)}) copy-start(bf16[16,256]{1,0:T(8,128)(2,1)S(1)} %collective-permute-done.10.gtl_ref) | copy-start | bytes 24580
  123.3 9.1 %collective-permute-start.6 = (bf16[128,256]{1,0:T(8,128)(2,1)S(1)}, bf16[128,256]{1,0:T(8,128)(2,1)S(1)}, u32[]{:S(2)}, u32[]{:S(2)}) collective-permute-start(bf16[128,256]{1,0:T(8,128)(2,1)S(1)} %copy-done.13), channel_id=1, source_target_pairs={{0,16},{16,32},{32,48},{48,64},{64,80},{80,96},{96,112},{112,128},... | collective-permute-start | bytes 196616 | tf_op jit(solution)/shard_map/ppermute | solution.py:83
  126.1 6.2 %copy-start.26 = (bf16[16,256]{1,0:T(8,128)(2,1)}, bf16[16,256]{1,0:T(8,128)(2,1)S(1)}, u32[]{:S(2)}) copy-start(bf16[16,256]{1,0:T(8,128)(2,1)S(1)} %collective-permute-done.11.gbr_ref) | copy-start | bytes 24580
  126.1 13.0 %collective-permute-start.7 = (bf16[128,256]{1,0:T(8,128)(2,1)S(1)}, bf16[128,256]{1,0:T(8,128)(2,1)S(1)}, u32[]{:S(2)}, u32[]{:S(2)}) collective-permute-start(bf16[128,256]{1,0:T(8,128)(2,1)S(1)} %copy-done.12), channel_id=1, source_target_pairs={{16,0},{32,16},{48,32},{64,48},{80,64},{96,80},{112,96},{128,112},... | collective-permute-start | bytes 196616 | tf_op jit(solution)/shard_map/ppermute | solution.py:82
  132.3 6.9 %copy-start.14 = (bf16[128,256]{1,0:T(8,128)(2,1)}, bf16[128,256]{1,0:T(8,128)(2,1)S(1)}, u32[]{:S(2)}) copy-start(bf16[128,256]{1,0:T(8,128)(2,1)S(1)} %collective-permute-done.6.gabove_ref) | copy-start | bytes 196612
  132.3 16.2 %collective-permute-start.29 = (bf16[4,64,256]{2,1,0:T(8,128)(2,1)S(1)}, bf16[4,64,256]{2,1,0:T(8,128)(2,1)S(1)}, u32[]{:S(2)}, u32[]{:S(2)}) collective-permute-start(bf16[4,64,256]{2,1,0:T(8,128)(2,1)S(1)} %pad_maximum_fusion.refs_0_), channel_id=1, source_target_pairs={{0,1},{1,0},{2,3},{3,2},{4,5},{5,4},{6,7},{7,6},{8,9},{9,8},{10,11... | collective-permute-start | bytes 393224 | tf_op jit(solution)/shard_map/ppermute | solution.py:407
  138.5 10.0 %copy-start.3 = (bf16[4,64,256]{2,1,0:T(8,128)(2,1)}, bf16[4,64,256]{2,1,0:T(8,128)(2,1)S(1)}, u32[]{:S(2)}) copy-start(bf16[4,64,256]{2,1,0:T(8,128)(2,1)S(1)} %collective-permute-done.28.refs_3_) | copy-start | bytes 393220
  138.5 10.0 %collective-permute-start.32 = (bf16[4,64,256]{2,1,0:T(8,128)(2,1)S(1)}, bf16[4,64,256]{2,1,0:T(8,128)(2,1)S(1)}, u32[]{:S(2)}, u32[]{:S(2)}) collective-permute-start(bf16[4,64,256]{2,1,0:T(8,128)(2,1)S(1)} %collective-permute-done.28.refs_3_), channel_id=1, source_target_pairs={{0,1},{1,0},{2,3},{3,2},{4,5},{5,4},{6,7},{7,6},{8,9},{9,8},{10,11... | collective-permute-start | bytes 393224 | tf_op jit(solution)/shard_map/ppermute | solution.py:407
  138.7 9.8 %copy-start.4 = (bf16[4,64,256]{2,1,0:T(8,128)(2,1)}, bf16[4,64,256]{2,1,0:T(8,128)(2,1)S(1)}, u32[]{:S(2)}) copy-start(bf16[4,64,256]{2,1,0:T(8,128)(2,1)S(1)} %collective-permute-done.27.refs_2_) | copy-start | bytes 393220
  138.7 9.9 %collective-permute-start.31 = (bf16[4,64,256]{2,1,0:T(8,128)(2,1)S(1)}, bf16[4,64,256]{2,1,0:T(8,128)(2,1)S(1)}, u32[]{:S(2)}, u32[]{:S(2)}) collective-permute-start(bf16[4,64,256]{2,1,0:T(8,128)(2,1)S(1)} %collective-permute-done.27.refs_2_), channel_id=1, source_target_pairs={{0,1},{1,0},{2,3},{3,2},{4,5},{5,4},{6,7},{7,6},{8,9},{9,8},{10,11... | collective-permute-start | bytes 393224 | tf_op jit(solution)/shard_map/ppermute | solution.py:407
  139.1 9.4 %copy-start.5 = (bf16[4,64,256]{2,1,0:T(8,128)(2,1)}, bf16[4,64,256]{2,1,0:T(8,128)(2,1)S(1)}, u32[]{:S(2)}) copy-start(bf16[4,64,256]{2,1,0:T(8,128)(2,1)S(1)} %collective-permute-done.26.refs_1_) | copy-start | bytes 393220
  139.1 9.5 %collective-permute-start.30 = (bf16[4,64,256]{2,1,0:T(8,128)(2,1)S(1)}, bf16[4,64,256]{2,1,0:T(8,128)(2,1)S(1)}, u32[]{:S(2)}, u32[]{:S(2)}) collective-permute-start(bf16[4,64,256]{2,1,0:T(8,128)(2,1)S(1)} %collective-permute-done.26.refs_1_), channel_id=1, source_target_pairs={{0,1},{1,0},{2,3},{3,2},{4,5},{5,4},{6,7},{7,6},{8,9},{9,8},{10,11... | collective-permute-start | bytes 393224 | tf_op jit(solution)/shard_map/ppermute | solution.py:407
  139.2 0.6 copy-start.15
  148.5 0.6 copy-start.6
  148.5 0.7 copy-start.7
  148.6 0.7 copy-start.8
  149.3 0.6 copy-start.9

commit v2 on v1

--- a/solution.py
+++ b/solution.py
@@ -1,4 +1,3 @@
-import functools
 import math
 
 import jax
@@ -37,59 +36,106 @@
     return jnp.concatenate([ref[start : start + rows], ref[start + rows : start + 2 * rows]], axis=1)
 
 
-def pack_kernel(f_ref, c_ref, st_ref, stt_ref, up_ref, down_ref, left_ref, right_ref, ul_ref, dr_ref):
+def even(axis):
+    return lax.axis_index(axis) % 2 == 0
+
+
+def choose(condition, value, other):
+    return jnp.where(condition, value, other), jnp.where(condition, other, value)
+
+
+def pack_kernel(f_ref, c_ref, st_ref, row0_ref, row1_ref, col0_ref, col1_ref):
     height, breadth, _ = f_ref.shape
-    for row, out in ((0, up_ref), (height - 1, down_ref)):
+    last = height - 1
+    weights = st_ref[...].astype(F32)
+    bottom_first = even("row")
+    for out, first in ((row0_ref, True), (row1_ref, False)):
+        row = jnp.where(bottom_first == first, last, 0)
         out[0 : 2 * breadth] = halves(f_ref[row])
         out[2 * breadth : 4 * breadth] = halves(c_ref[row])
-        out[4 * breadth : 4 * breadth + SLOTS] = stt_ref[row]
-    for col, first, out in ((0, (2, 6), left_ref), (breadth - 1, (1, 5), right_ref)):
+    slots = [
+        jnp.concatenate([weights[:, row, :], jnp.zeros((SLOTS - 21, 128), F32)], axis=0).astype(BF16)
+        for row in (last, 0)
+    ]
+    ordered = choose(bottom_first, *slots)
+    row0_ref[4 * breadth : 4 * breadth + SLOTS] = ordered[0]
+    row1_ref[4 * breadth : 4 * breadth + SLOTS] = ordered[1]
+    sides = []
+    for col, first in ((breadth - 1, (1, 5)), (0, (2, 6))):
         base = 0 if col == 0 else breadth - 16
-        for which, ref in enumerate((f_ref, c_ref)):
-            edge = ref[:, base : base + 16, :].astype(F32)[:, col - base, :]
-            out[which * 2 * height : (which + 1) * 2 * height] = halves(edge).astype(BF16)
-        for which, slot in enumerate(first):
-            for k in range(3):
-                start = 4 * height + (which * 3 + k) * height
-                out[start : start + height] = st_ref[7 * k + slot]
-    for row, col, slot, out in ((0, 0, 6, ul_ref), (height - 1, breadth - 1, 5, dr_ref)):
-        base = 0 if col == 0 else breadth - 16
-        lines = []
+        parts = []
         for ref in (f_ref, c_ref):
-            edge = ref[row, base : base + 16, :].astype(F32)[col - base : col - base + 1]
-            lines += [edge[:, :128], edge[:, 128:]]
-        weights = stt_ref[row].astype(F32)
-        lines += [weights[7 * k + slot : 7 * k + slot + 1] for k in range(3)]
-        lines.append(jnp.zeros((16 - len(lines), 128), F32))
-        out[...] = jnp.concatenate(lines, axis=0).astype(BF16)
-
-
-def pack(features, cotangent, stencil, stencil_t):
+            parts.append(halves(ref[:, base : base + 16, :].astype(F32)[:, col - base, :]).astype(BF16))
+        parts += [st_ref[7 * k + slot] for slot in first for k in range(3)]
+        sides.append(parts)
+    start = 0
+    for right, left in zip(*sides):
+        rows = right.shape[0]
+        col0_ref[start : start + rows], col1_ref[start : start + rows] = choose(even("col"), right, left)
+        start += rows
+
+
+def pack(features, cotangent, stencil):
     height, breadth, _ = features.shape
-    sizes = (4 * breadth + SLOTS,) * 2 + (10 * height,) * 2 + (16, 16)
+    sizes = (4 * breadth + SLOTS,) * 2 + (10 * height,) * 2
     return pl.pallas_call(
         pack_kernel,
         out_shape=[jax.ShapeDtypeStruct((n, 128), BF16) for n in sizes],
         compiler_params=pltpu.CompilerParams(vmem_limit_bytes=VMEM_LIMIT),
         name="pack_rims",
-    )(features, cotangent, stencil, stencil_t)
-
-
-def exchange(messages, joint):
-    up, down, left, right, up_left, down_right = messages
+    )(features, cotangent, stencil)
+
+
+def corner_kernel(row0_ref, row1_ref, col0_ref, col1_ref, out0_ref, out1_ref):
+    size = col0_ref.shape[0]
+    below, above = choose(even("row"), row0_ref[...].astype(F32), row1_ref[...].astype(F32))
+    corners = []
+    for rim, col, slot in ((above, 127, 5), (below, 0, 6)):
+        lines = [rim[128 * n + col : 128 * n + col + 1] for n in range(4)]
+        lines += [rim[512 + 7 * k + slot : 513 + 7 * k + slot] for k in range(3)]
+        corners.append(jnp.concatenate(lines + [jnp.zeros((9, 128), F32)], axis=0).astype(BF16))
+    out0_ref[0:size], out1_ref[0:size] = col0_ref[...], col1_ref[...]
+    out0_ref[size : size + 16], out1_ref[size : size + 16] = choose(even("col"), *corners)
+
+
+def grad_corner_kernel(row0_ref, row1_ref, col0_ref, col1_ref, out0_ref, out1_ref):
+    size, channels = col0_ref.shape
+    edges = []
+    for ref in (row0_ref, row1_ref):
+        value = ref[...].astype(F32)
+        edges.append((value[0:1], value[127:128]))
+    below = jnp.where(even("row"), edges[0][0], edges[1][0])
+    above = jnp.where(even("row"), edges[1][1], edges[0][1])
+    corners = [jnp.broadcast_to(v, (16, channels)).astype(BF16) for v in (above, below)]
+    out0_ref[0:size], out1_ref[0:size] = col0_ref[...], col1_ref[...]
+    out0_ref[size : size + 16], out1_ref[size : size + 16] = choose(even("col"), *corners)
+
+
+def pair_swap(value, axis, offset):
     rows, cols = lax.axis_size("row"), lax.axis_size("col")
-    index = lambda r, c: r * cols + c % cols
-    below = lax.ppermute(up, "row", [(i + 1, i) for i in range(rows - 1)])
-    above = lax.ppermute(down, "row", [(i, i + 1) for i in range(rows - 1)])
-    right_rim = lax.ppermute(left, "col", [((i + 1) % cols, i) for i in range(cols)])
-    left_rim = lax.ppermute(right, "col", [(i, (i + 1) % cols) for i in range(cols)])
-    corner_br = lax.ppermute(
-        up_left, BOTH, [(index(r + 1, c + 1), index(r, c)) for r in range(rows - 1) for c in range(cols)]
-    )
-    corner_tl = lax.ppermute(
-        down_right, BOTH, [(index(r, c), index(r + 1, c + 1)) for r in range(rows - 1) for c in range(cols)]
-    )
-    return above, below, left_rim, right_rim, corner_tl, corner_br
+    pairs = []
+    for r in range(rows):
+        for c in range(cols):
+            place = r if axis == "row" else c
+            step = 1 if place % 2 == offset else -1
+            to_r, to_c = (r + step, c) if axis == "row" else (r, (c + step) % cols)
+            if 0 <= to_r < rows:
+                pairs.append((r * cols + c, to_r * cols + to_c))
+    return lax.ppermute(value, BOTH, pairs)
+
+
+def exchange(row0, row1, col0, col1, kernel, name):
+    row0, row1 = pair_swap(row0, "row", 0), pair_swap(row1, "row", 1)
+    shape = (col0.shape[0] + 16, col0.shape[1])
+    col0, col1 = pl.pallas_call(
+        kernel, out_shape=[jax.ShapeDtypeStruct(shape, BF16)] * 2, name=name
+    )(row0, row1, col0, col1)
+    return row0, row1, pair_swap(col0, "col", 0), pair_swap(col1, "col", 1)
+
+
+def place_rims(row0_ref, row1_ref, col0_ref, col1_ref, above_ref, below_ref, left_ref, right_ref):
+    below_ref[...], above_ref[...] = choose(even("row"), row0_ref[...], row1_ref[...])
+    right_ref[...], left_ref[...] = choose(even("col"), col0_ref[...], col1_ref[...])
 
 
 def fill_masks(mask_ref):
@@ -104,7 +150,7 @@
         mask_ref[4, 16 * number : 16 * number + 16] = as_mask((e == edge) & (l == lane))
 
 
-def fill_weights(stt_ref, above_ref, below_ref, left_ref, right_ref, tl_ref, br_ref, wx_ref, we_ref):
+def fill_weights(stt_ref, above_ref, below_ref, left_ref, right_ref, wx_ref, we_ref):
     height, _, breadth = stt_ref.shape
     base = 4 * breadth
     wx_ref[0] = above_ref[base : base + SLOTS].astype(F32)
@@ -112,6 +158,7 @@
         wx_ref[1 + r] = stt_ref[r].astype(F32)
     wx_ref[height + 1] = below_ref[base : base + SLOTS].astype(F32)
     lane = iota((height, 128), 1)
+    tl, br = left_ref[10 * height :], right_ref[10 * height :]
 
     def spot(value, shift, place):
         rolled = pltpu.roll(value.astype(F32), shift, 1)
@@ -124,10 +171,10 @@
             right_ref[near : near + height], 2, 2
         )
         we_ref[1, k, 8 : 8 + height] = spot(left_ref[far : far + height], 2, 1)
-        we_ref[1, k, 0:8] = jnp.broadcast_to(spot(tl_ref[...], 2, 1)[4 + k : 5 + k], (8, 128))
+        we_ref[1, k, 0:8] = jnp.broadcast_to(spot(tl, 2, 1)[4 + k : 5 + k], (8, 128))
         we_ref[2, k, 8 : 8 + height] = spot(right_ref[far : far + height], 3, 3)
         we_ref[2, k, 8 + height : 16 + height] = jnp.broadcast_to(
-            spot(br_ref[...], 3, 3)[4 + k : 5 + k], (8, 128)
+            spot(br, 3, 3)[4 + k : 5 + k], (8, 128)
         )
 
 
@@ -211,17 +258,16 @@
 
 
 def gradient_kernel(
-    ids_ref, f_ref, c_ref, stt_ref, above_ref, below_ref, left_ref, right_ref, tl_ref, br_ref,
-    w1_ref, w2_ref,
-    g_ref, up_ref, down_ref, gl_ref, gr_ref, ul_ref, dr_ref, keep_ref, send_ref,
+    f_ref, c_ref, stt_ref, row0_ref, row1_ref, col0_ref, col1_ref, w1_ref, w2_ref,
+    g_ref, grow0_ref, grow1_ref, gcol0_ref, gcol1_ref, keep_ref, send_ref,
+    above_ref, below_ref, left_ref, right_ref,
     fext_ref, cext_ref, ff_ref, tt_ref, wx_ref, we_ref, flx_ref, frx_ref, clx_ref, crx_ref,
     mask_ref, total_ref, glx_ref, grx_ref,
 ):
     height, breadth, channels = f_ref.shape
     fill_masks(mask_ref)
-    fill_weights(
-        stt_ref, above_ref, below_ref, left_ref, right_ref, tl_ref, br_ref, wx_ref, we_ref
-    )
+    place_rims(row0_ref, row1_ref, col0_ref, col1_ref, above_ref, below_ref, left_ref, right_ref)
+    fill_weights(stt_ref, above_ref, below_ref, left_ref, right_ref, wx_ref, we_ref)
     for which, (src, ext, lx, rx) in enumerate(
         ((f_ref, fext_ref, flx_ref, frx_ref), (c_ref, cext_ref, clx_ref, crx_ref))
     ):
@@ -230,12 +276,10 @@
         ext[1 : 1 + height] = src[...]
         ext[1 + height] = whole(below_ref, start, breadth)
         side = which * 2 * height
-        corner = lambda ref: jnp.concatenate(
-            [ref[...].astype(F32)[2 * which : 2 * which + 1], ref[...].astype(F32)[2 * which + 1 : 2 * which + 2]],
-            axis=1,
-        )
+        lines = lambda ref: ref[10 * height :].astype(F32)[2 * which : 2 * which + 2]
+        corner = lambda ref: jnp.concatenate([lines(ref)[0:1], lines(ref)[1:2]], axis=1)
         fill_sides(
-            whole(left_ref, side, height), whole(right_ref, side, height), corner(tl_ref), corner(br_ref), lx, rx
+            whole(left_ref, side, height), whole(right_ref, side, height), corner(left_ref), corner(right_ref), lx, rx
         )
 
     @pl.loop(0, height)
@@ -271,37 +315,31 @@
         first = dot(ff_ref[rows], grad.astype(BF16), 0, 0)
         total_ref[1] += first.reshape(16, channels // 4, channels)
 
-    up_ref[...] = g_ref[0]
-    down_ref[...] = g_ref[height - 1]
-    gl_ref[...] = glx_ref[...].astype(BF16)
-    gr_ref[...] = grx_ref[...].astype(BF16)
-    ul_ref[...] = jnp.broadcast_to(glx_ref[0:1], (16, channels)).astype(BF16)
-    dr_ref[...] = jnp.broadcast_to(grx_ref[height - 1 : height], (16, channels)).astype(BF16)
-    core, x, y = ids_ref[0], ids_ref[1], ids_ref[2]
-    for dx in range(4):
-        for dy in range(4):
-            chunk = jnp.bitwise_xor(x, dx) * 4 + jnp.bitwise_xor(y, dy)
-            keep_ref[4 * dx + dy] = total_ref[core, chunk]
-            send_ref[4 * dx + dy] = total_ref[1 - core, chunk]
+    grow0_ref[...], grow1_ref[...] = choose(even("row"), g_ref[height - 1], g_ref[0])
+    gcol0_ref[...], gcol1_ref[...] = choose(
+        even("col"), grx_ref[...].astype(BF16), glx_ref[...].astype(BF16)
+    )
+    core = lax.axis_index("col") % 2
+    keep_ref[...] = total_ref[core]
+    send_ref[...] = total_ref[1 - core]
 
 
 def input_kernel(
-    g_ref, gabove_ref, gbelow_ref, gleft_ref, gright_ref, gtl_ref, gbr_ref,
-    stt_ref, above_ref, below_ref, left_ref, right_ref, tl_ref, br_ref, w1t_ref,
+    g_ref, grow0_ref, grow1_ref, gcol0_ref, gcol1_ref,
+    stt_ref, row0_ref, row1_ref, col0_ref, col1_ref, w1t_ref,
     out_ref,
+    above_ref, below_ref, left_ref, right_ref,
     gext_ref, tt_ref, wx_ref, we_ref, lx_ref, rx_ref, mask_ref,
 ):
     height, breadth, channels = g_ref.shape
     fill_masks(mask_ref)
-    fill_weights(
-        stt_ref, above_ref, below_ref, left_ref, right_ref, tl_ref, br_ref, wx_ref, we_ref
-    )
-    gext_ref[0] = gabove_ref[...]
+    place_rims(row0_ref, row1_ref, col0_ref, col1_ref, above_ref, below_ref, left_ref, right_ref)
+    fill_weights(stt_ref, above_ref, below_ref, left_ref, right_ref, wx_ref, we_ref)
+    gext_ref[1 + height], gext_ref[0] = choose(even("row"), grow0_ref[...], grow1_ref[...])
     gext_ref[1 : 1 + height] = g_ref[...]
-    gext_ref[1 + height] = gbelow_ref[...]
-    fill_sides(
-        gleft_ref[...], gright_ref[...], gtl_ref[...].astype(F32)[0:1], gbr_ref[...].astype(F32)[0:1], lx_ref, rx_ref
-    )
+    right, left = choose(even("col"), gcol0_ref[...], gcol1_ref[...])
+    corner = lambda value: value[height:].astype(F32)[0:1]
+    fill_sides(left[:height], right[:height], corner(left), corner(right), lx_ref, rx_ref)
 
     @pl.loop(0, height)
     def _(r):
@@ -321,24 +359,10 @@
             out_ref[i * batch + q] = result[q * 128 : q * 128 + 128]
 
 
-def final_kernel(scale, ids_ref, *refs):
-    mine, theirs, out_refs = refs[:4], refs[4:8], refs[8:]
-    core, x, y = ids_ref[0], ids_ref[1], ids_ref[2]
-    first_core = core == 0
-    for dx in range(4):
-        for dy in range(4):
-            chunk = jnp.bitwise_xor(x, dx) * 4 + jnp.bitwise_xor(y, dy)
-            a = mine[dx][dy].astype(F32) * scale
-            b = theirs[dx][dy].astype(F32) * scale
-            out_refs[0][chunk] = jnp.where(first_core, a, b)
-            out_refs[1][chunk] = jnp.where(first_core, b, a)
-
-
-SMEM_SPEC = pl.BlockSpec(memory_space=pltpu.SMEM)
 VMEM_SPEC = pl.BlockSpec(memory_space=pltpu.VMEM)
 
 
-def gradients(ids, features, cotangent, stencil_t, rims, w1, w2t):
+def gradients(features, cotangent, stencil_t, rims, w1, w2t):
     height, breadth, channels = features.shape
     shape = jax.ShapeDtypeStruct
     totals = (16, channels // 4, channels)
@@ -351,13 +375,12 @@
             shape((breadth, channels), BF16),
             shape((height, channels), BF16),
             shape((height, channels), BF16),
-            shape((16, channels), BF16),
-            shape((16, channels), BF16),
             shape(totals, F32),
             shape(totals, F32),
         ],
-        in_specs=[SMEM_SPEC] + [VMEM_SPEC] * 11,
-        scratch_shapes=[
+        in_specs=[VMEM_SPEC] * 9,
+        scratch_shapes=[pltpu.VMEM(v.shape, BF16) for v in rims]
+        + [
             pltpu.VMEM((height + 2, breadth, channels), BF16),
             pltpu.VMEM((height + 2, breadth, channels), BF16),
             pltpu.VMEM((vertices, 4 * channels), BF16),
@@ -375,7 +398,7 @@
         compiler_params=pltpu.CompilerParams(vmem_limit_bytes=VMEM_LIMIT),
         cost_estimate=pl.CostEstimate(flops=9 * 10**9, bytes_accessed=9 * 10**6, transcendentals=vertices * channels),
         name="weight_gradients",
-    )(ids, features, cotangent, stencil_t, *rims, w1, w2t)
+    )(features, cotangent, stencil_t, *rims, w1, w2t)
 
 
 def input_gradient(grad, grad_rims, stencil_t, rims, w1t):
@@ -383,8 +406,9 @@
     return pl.pallas_call(
         input_kernel,
         out_shape=jax.ShapeDtypeStruct((height, breadth, channels), BF16),
-        in_specs=[VMEM_SPEC] * 15,
-        scratch_shapes=[
+        in_specs=[VMEM_SPEC] * 11,
+        scratch_shapes=[pltpu.VMEM(v.shape, BF16) for v in rims]
+        + [
             pltpu.VMEM((height + 2, breadth, channels), BF16),
             pltpu.VMEM((height * breadth, 4 * channels), BF16),
             pltpu.VMEM((height + 2, SLOTS, 128), F32),
@@ -408,20 +432,20 @@
 
 
 def reduce_both(keep, send):
-    total = keep + swap(send, 0, 1)
-    parts = [total[4 * d : 4 * d + 4] for d in range(4)]
-    came = [swap(parts[d].astype(BF16), 4 * d, 0) for d in (1, 2, 3)]
-    total = parts[0] + sum(v.astype(F32) for v in came)
-    parts = [total[d] for d in range(4)]
-    came = [swap(parts[d].astype(BF16), 0, 2 * d) for d in (1, 2, 3)]
-    total = parts[0] + sum(v.astype(F32) for v in came)
+    cols = lax.axis_size("col")
+    planes = [
+        [cols * (4 * x + z) + 8 * h + 2 * y + core for x in range(4) for y in range(4)]
+        for z in range(4)
+        for h in range(2)
+        for core in range(2)
+    ]
+    trade = lambda v: lax.all_to_all(v, BOTH, 0, 0, axis_index_groups=planes, tiled=True)
+    total = trade((keep + swap(send, 0, 1)).astype(BF16)).astype(F32).sum(0)
     came = [swap(total, d, 0) for d in (1, 2, 3)]
     total = (total + came[0]) + (came[1] + came[2])
-    total = (total + swap(total, 0, 8)).astype(BF16)
-    gathered = jnp.stack([total] + [swap(total, 0, 2 * d) for d in (1, 2, 3)])
-    mine = [gathered] + [swap(gathered, 4 * d, 0) for d in (1, 2, 3)]
-    theirs = [swap(v, 0, 1) for v in mine]
-    return mine, theirs
+    total = (total + swap(total, 3, 8)).astype(BF16)
+    mine = trade(jnp.broadcast_to(total[None], keep.shape))
+    return mine, swap(mine, 0, 1)
 
 
 def body(features_in, stencil, weights_first, weights_second, cotangent):
@@ -429,26 +453,19 @@
     scale = 1.0 / math.sqrt(height * breadth * lax.axis_size("row") * lax.axis_size("col"))
     flat = stencil.reshape(21, height, breadth)
     stencil_t = jnp.pad(flat.transpose(1, 0, 2), ((0, 0), (0, SLOTS - 21), (0, 0)))
-    row, col = lax.axis_index("row"), lax.axis_index("col")
-    ids = jnp.stack([col % 2, row // 4, (col // 2) % 4]).astype(jnp.int32)
     w1 = weights_first.reshape(4 * channels, channels)
     w1t = weights_first.transpose(0, 2, 1).reshape(4 * channels, channels)
     w2t = weights_second.transpose(0, 2, 1).reshape(4 * channels, channels)
 
-    rims = exchange(pack(features_in, cotangent, flat, stencil_t), BOTH)
-    grad, *messages, keep, send = gradients(ids, features_in, cotangent, stencil_t, rims, w1, w2t)
+    rims = exchange(*pack(features_in, cotangent, flat), corner_kernel, "pack_corners")
+    grad, *messages, keep, send = gradients(features_in, cotangent, stencil_t, rims, w1, w2t)
     mine, theirs = reduce_both(keep, send)
-    input_grad = input_gradient(grad, exchange(messages, BOTH), stencil_t, rims, w1t)
-    totals = jax.ShapeDtypeStruct((16, channels // 4, channels), F32)
-    second, first = pl.pallas_call(
-        functools.partial(final_kernel, scale),
-        out_shape=[totals, totals],
-        in_specs=[SMEM_SPEC] + [VMEM_SPEC] * 8,
-        compiler_params=pltpu.CompilerParams(vmem_limit_bytes=VMEM_LIMIT),
-        name="place_totals",
-    )(ids, *mine, *theirs)
-    shape = (4, channels, channels)
-    return input_grad, first.reshape(shape), second.reshape(shape)
+    grad_rims = exchange(*messages, grad_corner_kernel, "pack_grad_corners")
+    input_grad = input_gradient(grad, grad_rims, stencil_t, rims, w1t)
+    mine, theirs = mine.astype(F32) * scale, theirs.astype(F32) * scale
+    second = jnp.where(even("col"), mine, theirs).reshape(4, channels, channels)
+    first = jnp.where(even("col"), theirs, mine).reshape(4, channels, channels)
+    return input_grad, first, second
 
 
 def solution(mesh):

time: 153 us -> 128 us (0.84)
  the two profiles are of different devices: /device:TPU:7 before, /device:TPU:224 now
where the time goes in v2:
time: 128 us
  waiting for transfers between devices  36.7 us (29%)
  blocking collectives  32.2 us (25%)
  Pallas kernels  30.7 us (24%)
  starting transfers between devices  18.9 us (15%)
  local copies, waits for them, and re-layouts  5.25 us (4%)
  other arithmetic  3.05 us (2%)
    all_to_all x2, blocking collectives, reduce_both(): lax.all_to_all(v, BOTH, 0, 0, axis_index_groups=planes, tiled=True)  32.2 us
    ppermute x8, waiting for transfers between devices, pair_swap(): return lax.ppermute(value, BOTH, pairs)  22.4 us
    pallas_call x1, Pallas kernels, gradients(): pl.pallas_call(gradient_kernel, out_shape=[shape((height, breadth, channe...  16.5 us
    ppermute x8, starting transfers between devices, pair_swap(): return lax.ppermute(value, BOTH, pairs)  15.2 us
    ppermute x6, waiting for transfers between devices, swap(): return lax.ppermute(value, BOTH, pairs)  14.4 us
    pallas_call x1, Pallas kernels, input_gradient(): pl.pallas_call(input_kernel, out_shape=jax.ShapeDtypeStruct((height, brea...  8.75 us
    ppermute x6, starting transfers between devices, swap(): return lax.ppermute(value, BOTH, pairs)  3.75 us
    pallas_call x2, Pallas kernels, exchange(): pl.pallas_call(kernel, out_shape=[jax.ShapeDtypeStruct(shape, BF16)] * 2,...  3.12 us
  transfers between devices with their start and end apart: 14, of which 9 were waited for; matrix products, arithmetic and copies ran while one was open for 2% of the time, Pallas kernels for 8%

profile of v2, /device:TPU:224, one launch (start us, length us, event | category | flops | bytes accessed | tf_op | source)
XLA Modules:
  0.0 127.6 jit_solution(2592288028870679124)
XLA Ops:
  0.6 0.0 copy-start.2
  0.6 2.3 %pack_rims.1 = (bf16[544,128]{1,0:T(8,128)(2,1)}, bf16[544,128]{1,0:T(8,128)(2,1)}, bf16[160,128]{1,0:T(8,128)(2,1)}, bf16[160,128]{1,0:T(8,128)(2,1)}) custom-call(bf16[16,128,256]{2,1,0:T(8,128)(2,1)} %f_ref.3, bf16[16,128,256]{2,1,0:T(8,128)(2,1)} %c_ref.3, bf16[21,16,128]{2,1,0:T(8,128)(2,1)} %bitcast.19), custom_call_target="tpu_custom_call" | custom-call | tf_op jit(solution)/shard_map/pack_rims/pallas_call | solution.py:81
  3.0 0.0 copy-start
  3.0 1.0 collective-permute-start
  4.0 4.7 %collective-permute-start.1 = (bf16[544,128]{1,0:T(8,128)(2,1)}, bf16[544,128]{1,0:T(8,128)(2,1)S(1)}, u32[]{:S(2)}, u32[]{:S(2)}) collective-permute-start(bf16[544,128]{1,0:T(8,128)(2,1)} %get-tuple-element.19), channel_id=1, source_target_pairs={{16,32},{17,33},{18,34},{19,35},{20,36},{21,37},{22,38},{23,39},{2... | collective-permute-start | bytes 417800 | tf_op jit(solution)/shard_map/ppermute | solution.py:124
  8.7 0.0 collective-permute-done.row0_ref
  8.7 0.0 copy-start.3
  8.7 5.3 %collective-permute-done.1.row1_ref = bf16[544,128]{1,0:T(8,128)(2,1)S(1)} collective-permute-done((bf16[544,128]{1,0:T(8,128)(2,1)}, bf16[544,128]{1,0:T(8,128)(2,1)S(1)}, u32[]{:S(2)}, u32[]{:S(2)}) %collective-permute-start.1) | collective-permute-done | bytes 139296 | tf_op jit(solution)/shard_map/ppermute | solution.py:124
  14.0 0.0 copy-start.4
  14.0 0.0 copy-done.3
  14.0 0.7 copy-done.4
  14.7 1.6 %pack_corners.1 = (bf16[176,128]{1,0:T(8,128)(2,1)}, bf16[176,128]{1,0:T(8,128)(2,1)}) custom-call(bf16[544,128]{1,0:T(8,128)(2,1)} %copy-done.3, bf16[544,128]{1,0:T(8,128)(2,1)} %copy-done.4, bf16[160,128]{1,0:T(8,128)(2,1)} %get-tuple-element.20.col0_ref, bf16[160,128]{1,0:T(8,128)(2,1)} %get-tuple-element.21.col1_ref), custom_call_target="tpu_custom_call" | custom-call | tf_op jit(solution)/shard_map/pack_corners/pallas_call | solution.py:130
  16.3 0.0 collective-permute-start.2
  16.3 3.4 %collective-permute-start.3 = (bf16[176,128]{1,0:T(8,128)(2,1)}, bf16[176,128]{1,0:T(8,128)(2,1)S(1)}, u32[]{:S(2)}, u32[]{:S(2)}) collective-permute-start(bf16[176,128]{1,0:T(8,128)(2,1)} %get-tuple-element.23), channel_id=1, source_target_pairs={{0,15},{1,2},{2,1},{3,4},{4,3},{5,6},{6,5},{7,8},{8,7},{9,10},{10,... | collective-permute-start | bytes 135176 | tf_op jit(solution)/shard_map/ppermute | solution.py:124
  19.7 0.0 copy-done.2
  19.8 0.0 copy-done
  19.8 1.0 copy.13
  20.8 0.7 pad.4.stt_ref
  21.4 0.0 collective-permute-done.2.col0_ref
  21.4 0.0 copy-start.9
  21.5 4.6 %collective-permute-done.3.col1_ref = bf16[176,128]{1,0:T(8,128)(2,1)S(1)} collective-permute-done((bf16[176,128]{1,0:T(8,128)(2,1)}, bf16[176,128]{1,0:T(8,128)(2,1)S(1)}, u32[]{:S(2)}, u32[]{:S(2)}) %collective-permute-start.3) | collective-permute-done | bytes 45088 | tf_op jit(solution)/shard_map/ppermute | solution.py:124
  26.0 0.0 copy-start.10
  26.0 0.0 copy-done.9
  26.0 0.6 copy-done.10
  26.6 16.5 %weight_gradients.1 = (bf16[16,128,256]{2,1,0:T(8,128)(2,1)}, bf16[128,256]{1,0:T(8,128)(2,1)}, bf16[128,256]{1,0:T(8,128)(2,1)}, bf16[16,256]{1,0:T(8,128)(2,1)...) custom-call(bf16[16,128,256]{2,1,0:T(8,128)(2,1)} %f_ref.3, ...), custom_call_target="tpu_custom_call" | custom-call | flops 8999999488 | bytes 9000000 | tf_op jit(solution)/shard_map/weight_gradients/pallas_call | solution.py:370
  43.1 0.0 collective-permute-start.8
  43.1 2.9 %collective-permute-done.8 = f32[16,64,256]{2,1,0:T(8,128)S(1)} collective-permute-done((f32[16,64,256]{2,1,0:T(8,128)}, f32[16,64,256]{2,1,0:T(8,128)S(1)}, u32[]{:S(2)}, u32[]{:S(2)}) %collective-permute-start.8) | collective-permute-done | bytes 1048608 | tf_op jit(solution)/shard_map/ppermute | solution.py:431
  46.0 1.3 %add_convert_fusion = bf16[16,64,256]{2,1,0:T(8,128)(2,1)S(1)} fusion(f32[16,64,256]{2,1,0:T(8,128)} %get-tuple-element.31, f32[16,64,256]{2,1,0:T(8,128)S(1)} %collective-permute-done.8), kind=kLoop, calls=%fused_computation.5 | loop fusion | flops 524288 | bytes 2621440 | tf_op jit(solution)/shard_map/convert_element_type | solution.py:443
  47.3 18.8 %all_to_all.10 = bf16[16,64,256]{2,1,0:T(8,128)(2,1)S(1)} all-to-all(bf16[16,64,256]{2,1,0:T(8,128)(2,1)S(1)} %add_convert_fusion), channel_id=1, replica_groups={{0,2,4,6,64,66,68,70,128,130,132,134,192,194,196,198},{1,3,5,7,65,67,69..., dimensions={0} | all-to-all | bytes 1048576 | tf_op jit(solution)/shard_map/all_to_all | solution.py:442
  66.1 0.1 convert_reduce_fusion
  66.2 1.7 %collective-permute-start.10 = (f32[64,256]{1,0:T(8,128)S(1)}, f32[64,256]{1,0:T(8,128)S(1)}, u32[]{:S(2)}, u32[]{:S(2)}) collective-permute-start(f32[64,256]{1,0:T(8,128)S(1)} %convert_reduce_fusion), channel_id=1, source_target_pairs={{0,32},{1,33},{2,34},{3,35},{4,36},{5,37},{6,38},{7,39},{8,40},{9,... | collective-permute-start | bytes 196616 | tf_op jit(solution)/shard_map/ppermute | solution.py:431
  67.9 1.9 %collective-permute-start.11 = (f32[64,256]{1,0:T(8,128)S(1)}, f32[64,256]{1,0:T(8,128)S(1)}, u32[]{:S(2)}, u32[]{:S(2)}) collective-permute-start(f32[64,256]{1,0:T(8,128)S(1)} %convert_reduce_fusion), channel_id=1, source_target_pairs={{0,48},{1,49},{2,50},{3,51},{4,52},{5,53},{6,54},{7,55},{8,56},{9,... | collective-permute-start | bytes 196616 | tf_op jit(solution)/shard_map/ppermute | solution.py:431
  69.9 0.0 collective-permute-start.9
  69.9 2.6 %collective-permute-done.10 = f32[64,256]{1,0:T(8,128)S(1)} collective-permute-done((f32[64,256]{1,0:T(8,128)S(1)}, f32[64,256]{1,0:T(8,128)S(1)}, u32[]{:S(2)}, u32[]{:S(2)}) %collective-permute-start.10) | collective-permute-done | bytes 65568 | tf_op jit(solution)/shard_map/ppermute | solution.py:431
  72.4 1.7 %collective-permute-done.11 = f32[64,256]{1,0:T(8,128)S(1)} collective-permute-done((f32[64,256]{1,0:T(8,128)S(1)}, f32[64,256]{1,0:T(8,128)S(1)}, u32[]{:S(2)}, u32[]{:S(2)}) %collective-permute-start.11) | collective-permute-done | bytes 65568 | tf_op jit(solution)/shard_map/ppermute | solution.py:431
  74.1 1.2 collective-permute-done.9
  75.3 0.1 collective-permute-start.12
  75.4 6.0 %collective-permute-done.12 = f32[64,256]{1,0:T(8,128)S(1)} collective-permute-done((f32[64,256]{1,0:T(8,128)S(1)}, f32[64,256]{1,0:T(8,128)S(1)}, u32[]{:S(2)}, u32[]{:S(2)}) %collective-permute-start.12) | collective-permute-done | bytes 65568 | tf_op jit(solution)/shard_map/ppermute | solution.py:431
  81.5 0.0 copy-start.8
  81.6 0.0 copy-start.7
  81.6 0.0 copy-start.1
  81.6 13.4 %all_to_all.11 = bf16[16,64,256]{2,1,0:T(8,128)(2,1)S(1)} all-to-all(bf16[16,64,256]{2,1,0:T(8,128)(2,1)S(1)} %broadcast_in_dim.2), channel_id=1, replica_groups={{0,2,4,6,64,66,68,70,128,130,132,134,192,194,196,198},{1,3,5,7,65,67,69..., dimensions={0} | all-to-all | bytes 1048576 | tf_op jit(solution)/shard_map/all_to_all | solution.py:442
  95.0 0.0 collective-permute-start.13
  95.0 0.0 copy-done.8
  95.0 1.3 %collective-permute-start.4 = (bf16[128,256]{1,0:T(8,128)(2,1)S(1)}, bf16[128,256]{1,0:T(8,128)(2,1)S(1)}, u32[]{:S(2)}, u32[]{:S(2)}) collective-permute-start(bf16[128,256]{1,0:T(8,128)(2,1)S(1)} %copy-done.8), channel_id=1, source_target_pairs={{0,16},{1,17},{2,18},{3,19},{4,20},{5,21},{6,22},{7,23},{8,24},{9,... | collective-permute-start | bytes 196616 | tf_op jit(solution)/shard_map/ppermute | solution.py:124
  96.3 0.0 copy-done.7
  96.3 3.4 %collective-permute-start.5 = (bf16[128,256]{1,0:T(8,128)(2,1)S(1)}, bf16[128,256]{1,0:T(8,128)(2,1)S(1)}, u32[]{:S(2)}, u32[]{:S(2)}) collective-permute-start(bf16[128,256]{1,0:T(8,128)(2,1)S(1)} %copy-done.7), channel_id=1, source_target_pairs={{16,32},{17,33},{18,34},{19,35},{20,36},{21,37},{22,38},{23,39},{2... | collective-permute-start | bytes 196616 | tf_op jit(solution)/shard_map/ppermute | solution.py:124
  99.8 0.0 collective-permute-done.4.row0_ref.grow0_ref
  99.8 0.0 copy-start.5
  99.8 5.4 %collective-permute-done.5.row1_ref.grow1_ref = bf16[128,256]{1,0:T(8,128)(2,1)S(1)} collective-permute-done((bf16[128,256]{1,0:T(8,128)(2,1)S(1)}, bf16[128,256]{1,0:T(8,128)(2,1)S(1)}, u32[]{:S(2)}, u32[]{:S(2)}) %collective-permute-start.5) | collective-permute-done | bytes 65568 | tf_op jit(solution)/shard_map/ppermute | solution.py:124
  105.1 0.0 copy-done.5
  105.1 0.6 copy-done.6
  105.8 1.5 %pack_grad_corners.1 = (bf16[32,256]{1,0:T(8,128)(2,1)}, bf16[32,256]{1,0:T(8,128)(2,1)}) custom-call(bf16[128,256]{1,0:T(8,128)(2,1)} %copy-done.5, bf16[128,256]{1,0:T(8,128)(2,1)} %copy-done.6, bf16[16,256]{1,0:T(8,128)(2,1)} %get-tuple-element.27.col0_ref, bf16[16,256]{1,0:T(8,128)(2,1)} %get-tuple-element.28.col1_ref), custom_call_target="tpu_custom_call" | custom-call | tf_op jit(solution)/shard_map/pack_grad_corners/pallas_call | solution.py:130
  107.3 0.0 collective-permute-start.6
  107.3 1.2 collective-permute-start.7
  108.5 0.0 copy-done.1
  108.5 1.0 copy.14
  109.5 0.0 collective-permute-done.6.gcol0_ref
  109.5 7.2 %collective-permute-done.7.gcol1_ref = bf16[32,256]{1,0:T(8,128)(2,1)S(1)} collective-permute-done((bf16[32,256]{1,0:T(8,128)(2,1)}, bf16[32,256]{1,0:T(8,128)(2,1)S(1)}, u32[]{:S(2)}, u32[]{:S(2)}) %collective-permute-start.7) | collective-permute-done | bytes 16416 | tf_op jit(solution)/shard_map/ppermute | solution.py:124
  116.7 0.0 copy-done.11
  116.7 0.6 copy-done.12
  117.2 8.7 %input_gradient.1 = bf16[16,128,256]{2,1,0:T(8,128)(2,1)} custom-call(bf16[16,128,256]{2,1,0:T(8,128)(2,1)} %get-tuple-element.24.g_ref, bf16[128,256]{1,0:T(8,128)(2,1)} %copy-done.5, bf16[128,256]{1,0:T(8,128)(2,1)} %copy-done.6, bf16[32,256]{1,0:T(8,128)(2,1)} %copy-done.11, bf16[32,256]{1,0:T(8,128)(2,1)} %copy-done.12, ...), custom_call_target="tpu_custom_call" | custom-call | flops 3000000000 | bytes 3000000 | tf_op jit(solution)/shard_map/input_gradient/pallas_call | solution.py:406
  126.0 0.0 collective-permute-done.13
  126.0 1.6 %fusion = (f32[16,64,256]{2,1,0:T(8,128)}, f32[16,64,256]{2,1,0:T(8,128)}) fusion(bf16[16,64,256]{2,1,0:T(8,128)(2,1)S(1)} %all_to_all.11, bf16[16,64,256]{2,1,0:T(8,128)(2,1)S(1)} %collective-permute-done.13, pred[]{:T(512)S(6)} %eq.7), kind=kLoop, calls=%fused_computation.1 | loop fusion | flops 1572864 | bytes 3145729 | tf_op jit(solution)/shard_map/jit(_where)/select_n | solution.py:466
  (7 shorter events, 0.1 us)
Async XLA Ops:
  0.6 19.1 %copy-start.2 = (bf16[3,7,16,128]{3,2,1,0:T(8,128)(2,1)S(1)}, bf16[3,7,16,128]{3,2,1,0:T(8,128)(2,1)}, u32[]{:S(2)}) copy-start(bf16[3,7,16,128]{3,2,1,0:T(8,128)(2,1)} %param.6) | copy-start | bytes 258052
  3.0 16.8 %copy-start = (bf16[4,256,256]{2,1,0:T(8,128)(2,1)S(1)}, bf16[4,256,256]{2,1,0:T(8,128)(2,1)}, u32[]{:S(2)}) copy-start(bf16[4,256,256]{2,1,0:T(8,128)(2,1)} %param.8) | copy-start | bytes 1572868
  3.0 5.7 %collective-permute-start = (bf16[544,128]{1,0:T(8,128)(2,1)}, bf16[544,128]{1,0:T(8,128)(2,1)S(1)}, u32[]{:S(2)}, u32[]{:S(2)}) collective-permute-start(bf16[544,128]{1,0:T(8,128)(2,1)} %get-tuple-element.18), channel_id=1, source_target_pairs={{0,16},{1,17},{2,18},{3,19},{4,20},{5,21},{6,22},{7,23},{8,24},{9,... | collective-permute-start | bytes 417800 | tf_op jit(solution)/shard_map/ppermute | solution.py:124
  4.0 10.0 %collective-permute-start.1 = (bf16[544,128]{1,0:T(8,128)(2,1)}, bf16[544,128]{1,0:T(8,128)(2,1)S(1)}, u32[]{:S(2)}, u32[]{:S(2)}) collective-permute-start(bf16[544,128]{1,0:T(8,128)(2,1)} %get-tuple-element.19), channel_id=1, source_target_pairs={{16,32},{17,33},{18,34},{19,35},{20,36},{21,37},{22,38},{23,39},{2... | collective-permute-start | bytes 417800 | tf_op jit(solution)/shard_map/ppermute | solution.py:124
  8.7 5.3 %copy-start.3 = (bf16[544,128]{1,0:T(8,128)(2,1)}, bf16[544,128]{1,0:T(8,128)(2,1)S(1)}, u32[]{:S(2)}) copy-start(bf16[544,128]{1,0:T(8,128)(2,1)S(1)} %collective-permute-done.row0_ref) | copy-start | bytes 417796
  14.0 0.7 copy-start.4
  16.3 5.1 %collective-permute-start.2 = (bf16[176,128]{1,0:T(8,128)(2,1)}, bf16[176,128]{1,0:T(8,128)(2,1)S(1)}, u32[]{:S(2)}, u32[]{:S(2)}) collective-permute-start(bf16[176,128]{1,0:T(8,128)(2,1)} %get-tuple-element.22), channel_id=1, source_target_pairs={{0,1},{1,0},{2,3},{3,2},{4,5},{5,4},{6,7},{7,6},{8,9},{9,8},{10,11... | collective-permute-start | bytes 135176 | tf_op jit(solution)/shard_map/ppermute | solution.py:124
  16.3 9.7 %collective-permute-start.3 = (bf16[176,128]{1,0:T(8,128)(2,1)}, bf16[176,128]{1,0:T(8,128)(2,1)S(1)}, u32[]{:S(2)}, u32[]{:S(2)}) collective-permute-start(bf16[176,128]{1,0:T(8,128)(2,1)} %get-tuple-element.23), channel_id=1, source_target_pairs={{0,15},{1,2},{2,1},{3,4},{4,3},{5,6},{6,5},{7,8},{8,7},{9,10},{10,... | collective-permute-start | bytes 135176 | tf_op jit(solution)/shard_map/ppermute | solution.py:124
  21.4 4.6 %copy-start.9 = (bf16[176,128]{1,0:T(8,128)(2,1)}, bf16[176,128]{1,0:T(8,128)(2,1)S(1)}, u32[]{:S(2)}) copy-start(bf16[176,128]{1,0:T(8,128)(2,1)S(1)} %collective-permute-done.2.col0_ref) | copy-start | bytes 135172
  26.0 0.6 copy-start.10
  43.1 2.9 %collective-permute-start.8 = (f32[16,64,256]{2,1,0:T(8,128)}, f32[16,64,256]{2,1,0:T(8,128)S(1)}, u32[]{:S(2)}, u32[]{:S(2)}) collective-permute-start(f32[16,64,256]{2,1,0:T(8,128)} %get-tuple-element.32), channel_id=1, source_target_pairs={{0,1},{1,0},{2,3},{3,2},{4,5},{5,4},{6,7},{7,6},{8,9},{9,8},{10,11... | collective-permute-start | bytes 3145736 | tf_op jit(solution)/shard_map/ppermute | solution.py:431
  66.2 6.2 %collective-permute-start.10 = (f32[64,256]{1,0:T(8,128)S(1)}, f32[64,256]{1,0:T(8,128)S(1)}, u32[]{:S(2)}, u32[]{:S(2)}) collective-permute-start(f32[64,256]{1,0:T(8,128)S(1)} %convert_reduce_fusion), channel_id=1, source_target_pairs={{0,32},{1,33},{2,34},{3,35},{4,36},{5,37},{6,38},{7,39},{8,40},{9,... | collective-permute-start | bytes 196616 | tf_op jit(solution)/shard_map/ppermute | solution.py:431
  67.9 6.2 %collective-permute-start.11 = (f32[64,256]{1,0:T(8,128)S(1)}, f32[64,256]{1,0:T(8,128)S(1)}, u32[]{:S(2)}, u32[]{:S(2)}) collective-permute-start(f32[64,256]{1,0:T(8,128)S(1)} %convert_reduce_fusion), channel_id=1, source_target_pairs={{0,48},{1,49},{2,50},{3,51},{4,52},{5,53},{6,54},{7,55},{8,56},{9,... | collective-permute-start | bytes 196616 | tf_op jit(solution)/shard_map/ppermute | solution.py:431
  69.9 5.4 %collective-permute-start.9 = (f32[64,256]{1,0:T(8,128)S(1)}, f32[64,256]{1,0:T(8,128)S(1)}, u32[]{:S(2)}, u32[]{:S(2)}) collective-permute-start(f32[64,256]{1,0:T(8,128)S(1)} %convert_reduce_fusion), channel_id=1, source_target_pairs={{0,16},{1,17},{2,18},{3,19},{4,20},{5,21},{6,22},{7,23},{8,24},{9,... | collective-permute-start | bytes 196616 | tf_op jit(solution)/shard_map/ppermute | solution.py:431
  75.3 6.1 %collective-permute-start.12 = (f32[64,256]{1,0:T(8,128)S(1)}, f32[64,256]{1,0:T(8,128)S(1)}, u32[]{:S(2)}, u32[]{:S(2)}) collective-permute-start(f32[64,256]{1,0:T(8,128)S(1)} %add_add_fusion), channel_id=1, source_target_pairs={{0,56},{1,57},{2,58},{3,59},{4,60},{5,61},{6,62},{7,63},{8,48},{9,... | collective-permute-start | bytes 196616 | tf_op jit(solution)/shard_map/ppermute | solution.py:431
  81.5 13.4 %copy-start.8 = (bf16[128,256]{1,0:T(8,128)(2,1)S(1)}, bf16[128,256]{1,0:T(8,128)(2,1)}, u32[]{:S(2)}) copy-start(bf16[128,256]{1,0:T(8,128)(2,1)} %get-tuple-element.25) | copy-start | bytes 196612
  81.6 14.7 %copy-start.7 = (bf16[128,256]{1,0:T(8,128)(2,1)S(1)}, bf16[128,256]{1,0:T(8,128)(2,1)}, u32[]{:S(2)}) copy-start(bf16[128,256]{1,0:T(8,128)(2,1)} %get-tuple-element.26) | copy-start | bytes 196612
  81.6 26.9 %copy-start.1 = (bf16[4,256,256]{2,1,0:T(8,128)(2,1)S(1)}, bf16[4,256,256]{2,1,0:T(8,128)(2,1)}, u32[]{:S(2)}) copy-start(bf16[4,256,256]{2,1,0:T(8,128)(2,1)} %param.7) | copy-start | bytes 1572868
  95.0 31.0 %collective-permute-start.13 = (bf16[16,64,256]{2,1,0:T(8,128)(2,1)S(1)}, bf16[16,64,256]{2,1,0:T(8,128)(2,1)S(1)}, u32[]{:S(2)}, u32[]{:S(2)}) collective-permute-start(bf16[16,64,256]{2,1,0:T(8,128)(2,1)S(1)} %all_to_all.11), channel_id=1, source_target_pairs={{0,1},{1,0},{2,3},{3,2},{4,5},{5,4},{6,7},{7,6},{8,9},{9,8},{10,11... | collective-permute-start | bytes 1572872 | tf_op jit(solution)/shard_map/ppermute | solution.py:431
  95.0 4.8 %collective-permute-start.4 = (bf16[128,256]{1,0:T(8,128)(2,1)S(1)}, bf16[128,256]{1,0:T(8,128)(2,1)S(1)}, u32[]{:S(2)}, u32[]{:S(2)}) collective-permute-start(bf16[128,256]{1,0:T(8,128)(2,1)S(1)} %copy-done.8), channel_id=1, source_target_pairs={{0,16},{1,17},{2,18},{3,19},{4,20},{5,21},{6,22},{7,23},{8,24},{9,... | collective-permute-start | bytes 196616 | tf_op jit(solution)/shard_map/ppermute | solution.py:124
  96.3 8.8 %collective-permute-start.5 = (bf16[128,256]{1,0:T(8,128)(2,1)S(1)}, bf16[128,256]{1,0:T(8,128)(2,1)S(1)}, u32[]{:S(2)}, u32[]{:S(2)}) collective-permute-start(bf16[128,256]{1,0:T(8,128)(2,1)S(1)} %copy-done.7), channel_id=1, source_target_pairs={{16,32},{17,33},{18,34},{19,35},{20,36},{21,37},{22,38},{23,39},{2... | collective-permute-start | bytes 196616 | tf_op jit(solution)/shard_map/ppermute | solution.py:124
  99.8 5.4 %copy-start.5 = (bf16[128,256]{1,0:T(8,128)(2,1)}, bf16[128,256]{1,0:T(8,128)(2,1)S(1)}, u32[]{:S(2)}) copy-start(bf16[128,256]{1,0:T(8,128)(2,1)S(1)} %collective-permute-done.4.row0_ref.grow0_ref) | copy-start | bytes 196612
  105.1 0.6 copy-start.6
  107.3 2.2 %collective-permute-start.6 = (bf16[32,256]{1,0:T(8,128)(2,1)}, bf16[32,256]{1,0:T(8,128)(2,1)S(1)}, u32[]{:S(2)}, u32[]{:S(2)}) collective-permute-start(bf16[32,256]{1,0:T(8,128)(2,1)} %get-tuple-element.29), channel_id=1, source_target_pairs={{0,1},{1,0},{2,3},{3,2},{4,5},{5,4},{6,7},{7,6},{8,9},{9,8},{10,11... | collective-permute-start | bytes 49160 | tf_op jit(solution)/shard_map/ppermute | solution.py:124
  107.3 9.4 %collective-permute-start.7 = (bf16[32,256]{1,0:T(8,128)(2,1)}, bf16[32,256]{1,0:T(8,128)(2,1)S(1)}, u32[]{:S(2)}, u32[]{:S(2)}) collective-permute-start(bf16[32,256]{1,0:T(8,128)(2,1)} %get-tuple-element.30), channel_id=1, source_target_pairs={{0,15},{1,2},{2,1},{3,4},{4,3},{5,6},{6,5},{7,8},{8,7},{9,10},{10,... | collective-permute-start | bytes 49160 | tf_op jit(solution)/shard_map/ppermute | solution.py:124
  109.5 7.2 %copy-start.11 = (bf16[32,256]{1,0:T(8,128)(2,1)}, bf16[32,256]{1,0:T(8,128)(2,1)S(1)}, u32[]{:S(2)}) copy-start(bf16[32,256]{1,0:T(8,128)(2,1)S(1)} %collective-permute-done.6.gcol0_ref) | copy-start | bytes 49156
  116.7 0.6 copy-start.12

commit v3 on v2

--- a/solution.py
+++ b/solution.py
@@ -11,7 +11,7 @@
 BF16 = jnp.bfloat16
 BOTH = ("row", "col")
 SLOTS = 32
-VMEM_LIMIT = 56 * 1024 * 1024
+VMEM_LIMIT = 28 * 1024 * 1024
 
 
 def dot(lhs, rhs, lhs_dim, rhs_dim):
@@ -124,12 +124,16 @@
     return lax.ppermute(value, BOTH, pairs)
 
 
+def add_corners(row0, row1, col0, col1, kernel, name):
+    shape = (col0.shape[0] + 16, col0.shape[1])
+    return pl.pallas_call(kernel, out_shape=[jax.ShapeDtypeStruct(shape, BF16)] * 2, name=name)(
+        row0, row1, col0, col1
+    )
+
+
 def exchange(row0, row1, col0, col1, kernel, name):
     row0, row1 = pair_swap(row0, "row", 0), pair_swap(row1, "row", 1)
-    shape = (col0.shape[0] + 16, col0.shape[1])
-    col0, col1 = pl.pallas_call(
-        kernel, out_shape=[jax.ShapeDtypeStruct(shape, BF16)] * 2, name=name
-    )(row0, row1, col0, col1)
+    col0, col1 = add_corners(row0, row1, col0, col1, kernel, name)
     return row0, row1, pair_swap(col0, "col", 0), pair_swap(col1, "col", 1)
 
 
@@ -282,7 +286,7 @@
             whole(left_ref, side, height), whole(right_ref, side, height), corner(left_ref), corner(right_ref), lx, rx
         )
 
-    @pl.loop(0, height)
+    @pl.loop(0, height, unroll=8)
     def _(r):
         rows = pl.ds(pl.multiple_of(r * 128, 128), 128)
         forward = dot(forward_band(wx_ref, mask_ref, r), field_block(fext_ref, flx_ref, frx_ref, r), 0, 0)
@@ -341,7 +345,7 @@
     corner = lambda value: value[height:].astype(F32)[0:1]
     fill_sides(left[:height], right[:height], corner(left), corner(right), lx_ref, rx_ref)
 
-    @pl.loop(0, height)
+    @pl.loop(0, height, unroll=8)
     def _(r):
         rows = pl.ds(pl.multiple_of(r * 128, 128), 128)
         turned = dot(
@@ -431,7 +435,7 @@
     return lax.ppermute(value, BOTH, pairs)
 
 
-def reduce_both(keep, send):
+def plane_trade(value):
     cols = lax.axis_size("col")
     planes = [
         [cols * (4 * x + z) + 8 * h + 2 * y + core for x in range(4) for y in range(4)]
@@ -439,13 +443,14 @@
         for h in range(2)
         for core in range(2)
     ]
-    trade = lambda v: lax.all_to_all(v, BOTH, 0, 0, axis_index_groups=planes, tiled=True)
-    total = trade((keep + swap(send, 0, 1)).astype(BF16)).astype(F32).sum(0)
-    came = [swap(total, d, 0) for d in (1, 2, 3)]
-    total = (total + came[0]) + (came[1] + came[2])
-    total = (total + swap(total, 3, 8)).astype(BF16)
-    mine = trade(jnp.broadcast_to(total[None], keep.shape))
-    return mine, swap(mine, 0, 1)
+    return lax.all_to_all(value, BOTH, 0, 0, axis_index_groups=planes, tiled=True)
+
+
+def sum_line(total):
+    total = total.astype(BF16)
+    came = [swap(total, d, 0).astype(F32) for d in (1, 2, 3)]
+    total = ((total.astype(F32) + came[0]) + (came[1] + came[2])).astype(BF16)
+    return total, swap(total, 3, 8)
 
 
 def body(features_in, stencil, weights_first, weights_second, cotangent):
@@ -459,9 +464,21 @@
 
     rims = exchange(*pack(features_in, cotangent, flat), corner_kernel, "pack_corners")
     grad, *messages, keep, send = gradients(features_in, cotangent, stencil_t, rims, w1, w2t)
-    mine, theirs = reduce_both(keep, send)
-    grad_rims = exchange(*messages, grad_corner_kernel, "pack_grad_corners")
-    input_grad = input_gradient(grad, grad_rims, stencil_t, rims, w1t)
+    row0, row1, col0, col1 = messages
+    row0, row1 = pair_swap(row0, "row", 0), pair_swap(row1, "row", 1)
+    half = (keep + swap(send, 0, 1)).astype(BF16)
+    half, row0, row1 = lax.optimization_barrier((half, row0, row1))
+    col0, col1 = add_corners(row0, row1, col0, col1, grad_corner_kernel, "pack_grad_corners")
+    col0, col1 = pair_swap(col0, "col", 0), pair_swap(col1, "col", 1)
+    part = plane_trade(half).astype(F32).sum(0)
+    part, col0, col1 = lax.optimization_barrier((part, col0, col1))
+    part, other = sum_line(part)
+    part = (part.astype(F32) + other.astype(F32)).astype(BF16)
+    part, grad = lax.optimization_barrier((part, grad))
+    input_grad = input_gradient(grad, (row0, row1, col0, col1), stencil_t, rims, w1t)
+    mine = plane_trade(jnp.broadcast_to(part[None], keep.shape))
+    mine, input_grad = lax.optimization_barrier((mine, input_grad))
+    theirs = swap(mine, 0, 1)
     mine, theirs = mine.astype(F32) * scale, theirs.astype(F32) * scale
     second = jnp.where(even("col"), mine, theirs).reshape(4, channels, channels)
     first = jnp.where(even("col"), theirs, mine).reshape(4, channels, channels)

time: 128 us -> 107 us (0.84)
  the two profiles are of different devices: /device:TPU:224 before, /device:TPU:1 now
where the time goes in v3:
time: 107 us; the launch traced here: 106 us
  starting transfers between devices  53.4 us (50%)
  Pallas kernels  19.5 us (18%)
  waiting for transfers between devices  18.2 us (17%)
  local copies, waits for them, and re-layouts  11.5 us (11%)
  other arithmetic  2.62 us (2%)
    all_to_all x2, starting transfers between devices, plane_trade(): lax.all_to_all(value, BOTH, 0, 0, axis_index_groups=planes, tiled=True)  21.9 us
    ppermute x8, starting transfers between devices, pair_swap(): return lax.ppermute(value, BOTH, pairs)  17.1 us
    ppermute x6, starting transfers between devices, swap(): return lax.ppermute(value, BOTH, pairs)  14.3 us
    pallas_call x1, Pallas kernels, gradients(): pl.pallas_call(gradient_kernel, out_shape=[shape((height, breadth, channe...  10.8 us
    all_to_all x2, waiting for transfers between devices, plane_trade(): lax.all_to_all(value, BOTH, 0, 0, axis_index_groups=planes, tiled=True)  9.39 us
    unnamed x44, local copies, waits for them, and re-layouts  7.53 us
    ppermute x6, waiting for transfers between devices, swap(): return lax.ppermute(value, BOTH, pairs)  5.6 us
    pallas_call x1, Pallas kernels, input_gradient(): pl.pallas_call(input_kernel, out_shape=jax.ShapeDtypeStruct((height, brea...  5.45 us
  transfers between devices with their start and end apart: 16, of which 10 were waited for; matrix products, arithmetic and copies ran while one was open for 4% of the time, Pallas kernels for 7%

profile of v3, /device:TPU:1, one launch (start us, length us, event | category | flops | bytes accessed | tf_op | source)
XLA Modules:
  0.0 106.1 jit_solution(14273302543647399391)
XLA Ops:
  0.6 0.0 copy-start
  0.6 1.2 %copy-done = bf16[16,128,256]{2,1,0:T(8,128)(2,1)S(1)} copy-done((bf16[16,128,256]{2,1,0:T(8,128)(2,1)S(1)}, bf16[16,128,256]{2,1,0:T(8,128)(2,1)}, u32[]{:S(2)}) %copy-start) | copy-done | bytes 1048600
  1.9 1.2 %copy-done.2 = bf16[16,128,256]{2,1,0:T(8,128)(2,1)S(1)} copy-done((bf16[16,128,256]{2,1,0:T(8,128)(2,1)S(1)}, bf16[16,128,256]{2,1,0:T(8,128)(2,1)}, u32[]{:S(2)}) %copy-start.2) | copy-done | bytes 1048600
  3.1 0.9 copy-done.5
  4.0 0.1 pack_rims.1
  4.1 0.0 copy-start.16
  4.1 0.6 copy-done.16
  4.7 0.6 copy-done.17
  5.3 2.5 %collective-permute-start = (bf16[544,128]{1,0:T(8,128)(2,1)S(1)}, bf16[544,128]{1,0:T(8,128)(2,1)S(1)}, u32[]{:S(2)}, u32[]{:S(2)}) collective-permute-start(bf16[544,128]{1,0:T(8,128)(2,1)S(1)} %get-tuple-element.28), channel_id=1, source_target_pairs={{0,16},{1,17},{2,18},{3,19},{4,20},{5,21},{6,22},{7,23},{8,24},{9,... | collective-permute-start | bytes 417800 | tf_op jit(solution)/shard_map/ppermute | solution.py:124
  7.8 0.7 collective-permute-start.1
  8.5 1.8 %collective-permute-done.row0_ref = bf16[544,128]{1,0:T(8,128)(2,1)S(1)} collective-permute-done((bf16[544,128]{1,0:T(8,128)(2,1)S(1)}, bf16[544,128]{1,0:T(8,128)(2,1)S(1)}, u32[]{:S(2)}, u32[]{:S(2)}) %collective-permute-start) | collective-permute-done | bytes 139296 | tf_op jit(solution)/shard_map/ppermute | solution.py:124
  10.2 0.0 collective-permute-done.1.row1_ref
  10.2 0.7 copy-done.7
  10.9 0.0 copy-done.9
  10.9 1.6 %pack_corners.1 = (bf16[176,128]{1,0:T(8,128)(2,1)}, bf16[176,128]{1,0:T(8,128)(2,1)}) custom-call(bf16[544,128]{1,0:T(8,128)(2,1)} %copy-done.7, bf16[544,128]{1,0:T(8,128)(2,1)} %copy-done.9, bf16[160,128]{1,0:T(8,128)(2,1)} %copy-done.16, bf16[160,128]{1,0:T(8,128)(2,1)} %copy-done.17), custom_call_target="tpu_custom_call" | custom-call | tf_op jit(solution)/shard_map/pack_corners/pallas_call | solution.py:129
  12.6 3.4 %collective-permute-start.2 = (bf16[176,128]{1,0:T(8,128)(2,1)}, bf16[176,128]{1,0:T(8,128)(2,1)S(1)}, u32[]{:S(2)}, u32[]{:S(2)}) collective-permute-start(bf16[176,128]{1,0:T(8,128)(2,1)} %get-tuple-element.32), channel_id=1, source_target_pairs={{0,1},{1,0},{2,3},{3,2},{4,5},{5,4},{6,7},{7,6},{8,9},{9,8},{10,11... | collective-permute-start | bytes 135176 | tf_op jit(solution)/shard_map/ppermute | solution.py:124
  16.0 0.0 collective-permute-start.3
  16.0 0.7 copy.16
  16.6 1.3 %copy.13 = bf16[4,256,256]{2,1,0:T(8,128)(2,1)S(1)} copy(bf16[4,256,256]{1,2,0:T(8,128)(2,1)} %bitcast.19) | data formatting | bytes 1048576 | tf_op jit(solution)/shard_map/transpose | solution.py:463
  17.9 0.0 copy-start.8
  18.0 0.9 pad.4.stt_ref
  18.9 0.0 collective-permute-done.2.col0_ref
  18.9 0.7 collective-permute-done.3.col1_ref
  19.6 0.0 copy-done.1
  19.7 0.0 copy-start.10
  19.7 0.9 copy-done.10
  20.6 10.8 %weight_gradients.1 = (bf16[16,128,256]{2,1,0:T(8,128)(2,1)S(1)}, bf16[128,256]{1,0:T(8,128)(2,1)S(1)}, bf16[128,256]{1,0:T(8,128)(2,1)S(1)}, bf16[16,256]{1,0:T...) custom-call(bf16[16,128,256]{2,1,0:T(8,128)(2,1)S(1)} %copy-done.1, ...), custom_call_target="tpu_custom_call" | custom-call | flops 8999999488 | bytes 9000000 | tf_op jit(solution)/shard_map/weight_gradients/pallas_call | solution.py:374
  31.4 0.0 copy-start.20
  31.4 7.8 %collective-permute-start.4 = (f32[16,64,256]{2,1,0:T(8,128)S(1)}, f32[16,64,256]{2,1,0:T(8,128)S(1)}, u32[]{:S(2)}, u32[]{:S(2)}) collective-permute-start(f32[16,64,256]{2,1,0:T(8,128)S(1)} %get-tuple-element.35), channel_id=1, source_target_pairs={{0,1},{1,0},{2,3},{3,2},{4,5},{5,4},{6,7},{7,6},{8,9},{9,8},{10,11... | collective-permute-start | bytes 3145736 | tf_op jit(solution)/shard_map/ppermute | solution.py:435
  39.2 6.3 %collective-permute-start.5 = (bf16[128,256]{1,0:T(8,128)(2,1)S(1)}, bf16[128,256]{1,0:T(8,128)(2,1)S(1)}, u32[]{:S(2)}, u32[]{:S(2)}) collective-permute-start(bf16[128,256]{1,0:T(8,128)(2,1)S(1)} %get-tuple-element.36), channel_id=1, source_target_pairs={{0,16},{1,17},{2,18},{3,19},{4,20},{5,21},{6,22},{7,23},{8,24},{9,... | collective-permute-start | bytes 196616 | tf_op jit(solution)/shard_map/ppermute | solution.py:124
  45.5 0.7 collective-permute-start.6
  46.1 0.0 collective-permute-done.4
  46.1 0.9 add_convert_fusion
  47.1 0.7 collective-permute-done.5.row0_ref.grow0_ref
  47.8 0.0 collective-permute-done.6.row1_ref.grow1_ref
  47.8 0.6 copy-done.12
  48.4 0.0 copy-done.14
  48.5 10.9 %all-to-all-start = ((bf16[16,64,256]{2,1,0:T(8,128)(2,1)}), bf16[16,64,256]{2,1,0:T(8,128)(2,1)S(1)}, u32[]{:S(2)}, u32[]{:S(2)}) async-start(bf16[16,64,256]{2,1,0:T(8,128)(2,1)} %add_convert_fusion), calls=%async_computation | async-start | bytes 1048576 | tf_op jit(solution)/shard_map/all_to_all | solution.py:446
  59.4 1.5 %pack_grad_corners.1 = (bf16[32,256]{1,0:T(8,128)(2,1)}, bf16[32,256]{1,0:T(8,128)(2,1)}) custom-call(bf16[128,256]{1,0:T(8,128)(2,1)} %copy-done.12, bf16[128,256]{1,0:T(8,128)(2,1)} %copy-done.14, bf16[16,256]{1,0:T(8,128)(2,1)} %copy-done.18, bf16[16,256]{1,0:T(8,128)(2,1)} %copy-done.19), custom_call_target="tpu_custom_call" | custom-call | tf_op jit(solution)/shard_map/pack_grad_corners/pallas_call | solution.py:129
  60.9 2.1 %collective-permute-start.7 = (bf16[32,256]{1,0:T(8,128)(2,1)}, bf16[32,256]{1,0:T(8,128)(2,1)S(1)}, u32[]{:S(2)}, u32[]{:S(2)}) collective-permute-start(bf16[32,256]{1,0:T(8,128)(2,1)} %get-tuple-element.43), channel_id=1, source_target_pairs={{0,1},{1,0},{2,3},{3,2},{4,5},{5,4},{6,7},{7,6},{8,9},{9,8},{10,11... | collective-permute-start | bytes 49160 | tf_op jit(solution)/shard_map/ppermute | solution.py:124
  63.0 1.5 %collective-permute-start.8 = (bf16[32,256]{1,0:T(8,128)(2,1)}, bf16[32,256]{1,0:T(8,128)(2,1)S(1)}, u32[]{:S(2)}, u32[]{:S(2)}) collective-permute-start(bf16[32,256]{1,0:T(8,128)(2,1)} %get-tuple-element.44), channel_id=1, source_target_pairs={{0,15},{1,2},{2,1},{3,4},{4,3},{5,6},{6,5},{7,8},{8,7},{9,10},{10,... | collective-permute-start | bytes 49160 | tf_op jit(solution)/shard_map/ppermute | solution.py:124
  64.6 4.1 %all-to-all-done = bf16[16,64,256]{2,1,0:T(8,128)(2,1)S(1)} async-done(((bf16[16,64,256]{2,1,0:T(8,128)(2,1)}), bf16[16,64,256]{2,1,0:T(8,128)(2,1)S(1)}, u32[]{:S(2)}, u32[]{:S(2)}) %all-to-all-start) | async-done | bytes 524320 | tf_op jit(solution)/shard_map/all_to_all | solution.py:446
  68.6 0.1 convert_reduce_fusion
  68.7 0.0 collective-permute-done.7.gcol0_ref
  68.7 0.0 collective-permute-done.8.gcol1_ref
  68.7 0.1 collective-permute-start.10
  68.8 2.5 %collective-permute-start.11 = (bf16[64,256]{1,0:T(8,128)(2,1)S(1)}, bf16[64,256]{1,0:T(8,128)(2,1)S(1)}, u32[]{:S(2)}, u32[]{:S(2)}) collective-permute-start(bf16[64,256]{1,0:T(8,128)(2,1)S(1)} %convert_reduce_fusion), channel_id=1, source_target_pairs={{0,48},{1,49},{2,50},{3,51},{4,52},{5,53},{6,54},{7,55},{8,56},{9,... | collective-permute-start | bytes 98312 | tf_op jit(solution)/shard_map/ppermute | solution.py:435
  71.4 0.2 collective-permute-start.9
  71.5 1.3 %collective-permute-done.10 = bf16[64,256]{1,0:T(8,128)(2,1)S(1)} collective-permute-done((bf16[64,256]{1,0:T(8,128)(2,1)S(1)}, bf16[64,256]{1,0:T(8,128)(2,1)S(1)}, u32[]{:S(2)}, u32[]{:S(2)}) %collective-permute-start.10) | collective-permute-done | bytes 32800 | tf_op jit(solution)/shard_map/ppermute | solution.py:435
  72.8 0.6 collective-permute-done.11
  73.5 0.8 collective-permute-done.9
  74.3 3.0 %collective-permute-start.12 = (bf16[64,256]{1,0:T(8,128)(2,1)S(1)}, bf16[64,256]{1,0:T(8,128)(2,1)S(1)}, u32[]{:S(2)}, u32[]{:S(2)}) collective-permute-start(bf16[64,256]{1,0:T(8,128)(2,1)S(1)} %add_convert_fusion.2), channel_id=1, source_target_pairs={{0,56},{1,57},{2,58},{3,59},{4,60},{5,61},{6,62},{7,63},{8,48},{9,... | collective-permute-start | bytes 98312 | tf_op jit(solution)/shard_map/ppermute | solution.py:435
  77.3 1.3 %collective-permute-done.12 = bf16[64,256]{1,0:T(8,128)(2,1)S(1)} collective-permute-done((bf16[64,256]{1,0:T(8,128)(2,1)S(1)}, bf16[64,256]{1,0:T(8,128)(2,1)S(1)}, u32[]{:S(2)}, u32[]{:S(2)}) %collective-permute-start.12) | collective-permute-done | bytes 32800 | tf_op jit(solution)/shard_map/ppermute | solution.py:435
  78.6 0.8 broadcast_in_dim.2
  79.5 11.0 %all-to-all-start.1 = ((bf16[16,64,256]{2,1,0:T(8,128)(2,1)}), bf16[16,64,256]{2,1,0:T(8,128)(2,1)S(1)}, u32[]{:S(2)}, u32[]{:S(2)}) async-start(bf16[16,64,256]{2,1,0:T(8,128)(2,1)} %broadcast_in_dim.2), calls=%async_computation.1 | async-start | bytes 1048576 | tf_op jit(solution)/shard_map/all_to_all | solution.py:446
  90.5 0.0 copy-start.11
  90.5 0.2 copy.14
  90.8 0.7 copy-done.11
  91.4 0.0 copy-done.15
  91.5 5.5 %input_gradient.1 = bf16[16,128,256]{2,1,0:T(8,128)(2,1)} custom-call(bf16[16,128,256]{2,1,0:T(8,128)(2,1)S(1)} %copy-done.21, bf16[128,256]{1,0:T(8,128)(2,1)S(1)} %copy-done.13, bf16[128,256]{1,0:T(8,128)(2,1)S(1)} %copy-done.15, bf16[32,256]{1,0:T(8,128)(2,1)S(1)} %collective-permute-done.7.gcol0_ref, ...), custom_call_target="tpu_custom_call" | custom-call | flops 3000000000 | bytes 3000000 | tf_op jit(solution)/shard_map/input_gradient/pallas_call | solution.py:410
  96.9 5.3 %all-to-all-done.1 = bf16[16,64,256]{2,1,0:T(8,128)(2,1)S(1)} async-done(((bf16[16,64,256]{2,1,0:T(8,128)(2,1)}), bf16[16,64,256]{2,1,0:T(8,128)(2,1)S(1)}, u32[]{:S(2)}, u32[]{:S(2)}) %all-to-all-start.1) | async-done | bytes 524320 | tf_op jit(solution)/shard_map/all_to_all | solution.py:446
  102.2 0.7 collective-permute-start.13
  102.9 1.5 %collective-permute-done.13 = bf16[16,64,256]{2,1,0:T(8,128)(2,1)S(1)} collective-permute-done((bf16[16,64,256]{2,1,0:T(8,128)(2,1)S(1)}, bf16[16,64,256]{2,1,0:T(8,128)(2,1)S(1)}, u32[]{:S(2)}, u32[]{:S(2)}) %collective-permute-start.13) | collective-permute-done | bytes 524320 | tf_op jit(solution)/shard_map/ppermute | solution.py:435
  104.5 1.6 %fusion = (f32[16,64,256]{2,1,0:T(8,128)}, f32[16,64,256]{2,1,0:T(8,128)}) fusion(bf16[16,64,256]{2,1,0:T(8,128)(2,1)S(1)} %all-to-all-done.1, bf16[16,64,256]{2,1,0:T(8,128)(2,1)S(1)} %collective-permute-done.13, pred[]{:T(512)S(6)} %eq.7), kind=kLoop, calls=%fused_computation.1 | loop fusion | flops 1572864 | bytes 3145729 | tf_op jit(solution)/shard_map/jit(_where)/select_n | solution.py:483
  (27 shorter events, 0.1 us)
Async XLA Ops:
  0.6 1.2 %copy-start = (bf16[16,128,256]{2,1,0:T(8,128)(2,1)S(1)}, bf16[16,128,256]{2,1,0:T(8,128)(2,1)}, u32[]{:S(2)}) copy-start(bf16[16,128,256]{2,1,0:T(8,128)(2,1)} %f_ref.3) | copy-start | bytes 3145732
  1.9 1.2 %copy-start.2 = (bf16[16,128,256]{2,1,0:T(8,128)(2,1)S(1)}, bf16[16,128,256]{2,1,0:T(8,128)(2,1)}, u32[]{:S(2)}) copy-start(bf16[16,128,256]{2,1,0:T(8,128)(2,1)} %c_ref.3) | copy-start | bytes 3145732
  3.1 0.9 copy-start.5
  4.0 12.0 %copy-start.6 = (bf16[3,7,16,128]{3,2,1,0:T(8,128)(2,1)S(1)}, bf16[3,7,16,128]{3,2,1,0:T(8,128)(2,1)}, u32[]{:S(2)}) copy-start(bf16[3,7,16,128]{3,2,1,0:T(8,128)(2,1)} %param.6) | copy-start | bytes 258052
  4.0 15.7 %copy-start.3 = (bf16[16,128,256]{2,1,0:T(8,128)(2,1)S(1)}, bf16[16,128,256]{2,1,0:T(8,128)(2,1)}, u32[]{:S(2)}) copy-start(bf16[16,128,256]{2,1,0:T(8,128)(2,1)} %c_ref.3) | copy-start | bytes 3145732
  4.1 0.6 copy-start.16
  4.7 0.6 copy-start.17
  5.3 14.3 %copy-start.1 = (bf16[16,128,256]{2,1,0:T(8,128)(2,1)S(1)}, bf16[16,128,256]{2,1,0:T(8,128)(2,1)}, u32[]{:S(2)}) copy-start(bf16[16,128,256]{2,1,0:T(8,128)(2,1)} %f_ref.3) | copy-start | bytes 3145732
  5.3 4.9 %collective-permute-start = (bf16[544,128]{1,0:T(8,128)(2,1)S(1)}, bf16[544,128]{1,0:T(8,128)(2,1)S(1)}, u32[]{:S(2)}, u32[]{:S(2)}) collective-permute-start(bf16[544,128]{1,0:T(8,128)(2,1)S(1)} %get-tuple-element.28), channel_id=1, source_target_pairs={{0,16},{1,17},{2,18},{3,19},{4,20},{5,21},{6,22},{7,23},{8,24},{9,... | collective-permute-start | bytes 417800 | tf_op jit(solution)/shard_map/ppermute | solution.py:124
  7.8 2.4 %collective-permute-start.1 = (bf16[544,128]{1,0:T(8,128)(2,1)S(1)}, bf16[544,128]{1,0:T(8,128)(2,1)S(1)}, u32[]{:S(2)}, u32[]{:S(2)}) collective-permute-start(bf16[544,128]{1,0:T(8,128)(2,1)S(1)} %get-tuple-element.29), channel_id=1, source_target_pairs={{16,32},{17,33},{18,34},{19,35},{20,36},{21,37},{22,38},{23,39},{2... | collective-permute-start | bytes 417800 | tf_op jit(solution)/shard_map/ppermute | solution.py:124
  10.2 0.7 copy-start.7
  10.2 0.7 copy-start.9
  12.6 6.3 %collective-permute-start.2 = (bf16[176,128]{1,0:T(8,128)(2,1)}, bf16[176,128]{1,0:T(8,128)(2,1)S(1)}, u32[]{:S(2)}, u32[]{:S(2)}) collective-permute-start(bf16[176,128]{1,0:T(8,128)(2,1)} %get-tuple-element.32), channel_id=1, source_target_pairs={{0,1},{1,0},{2,3},{3,2},{4,5},{5,4},{6,7},{7,6},{8,9},{9,8},{10,11... | collective-permute-start | bytes 135176 | tf_op jit(solution)/shard_map/ppermute | solution.py:124
  16.0 3.7 %collective-permute-start.3 = (bf16[176,128]{1,0:T(8,128)(2,1)}, bf16[176,128]{1,0:T(8,128)(2,1)S(1)}, u32[]{:S(2)}, u32[]{:S(2)}) collective-permute-start(bf16[176,128]{1,0:T(8,128)(2,1)} %get-tuple-element.33), channel_id=1, source_target_pairs={{0,15},{1,2},{2,1},{3,4},{4,3},{5,6},{6,5},{7,8},{8,7},{9,10},{10,... | collective-permute-start | bytes 135176 | tf_op jit(solution)/shard_map/ppermute | solution.py:124
  16.6 3.0 %copy-start.4 = (bf16[4,256,256]{2,1,0:T(8,128)(2,1)S(1)}, bf16[4,256,256]{2,1,0:T(8,128)(2,1)}, u32[]{:S(2)}) copy-start(bf16[4,256,256]{2,1,0:T(8,128)(2,1)} %param.7) | copy-start | bytes 1572868
  17.9 1.7 %copy-start.8 = (bf16[544,128]{1,0:T(8,128)(2,1)S(1)}, bf16[544,128]{1,0:T(8,128)(2,1)}, u32[]{:S(2)}) copy-start(bf16[544,128]{1,0:T(8,128)(2,1)} %copy-done.7) | copy-start | bytes 417796
  19.7 0.9 copy-start.10
  31.4 15.7 %copy-start.18 = (bf16[16,256]{1,0:T(8,128)(2,1)}, bf16[16,256]{1,0:T(8,128)(2,1)S(1)}, u32[]{:S(2)}) copy-start(bf16[16,256]{1,0:T(8,128)(2,1)S(1)} %get-tuple-element.41.col0_ref) | copy-start | bytes 24580
  31.4 15.7 %copy-start.19 = (bf16[16,256]{1,0:T(8,128)(2,1)}, bf16[16,256]{1,0:T(8,128)(2,1)S(1)}, u32[]{:S(2)}) copy-start(bf16[16,256]{1,0:T(8,128)(2,1)S(1)} %get-tuple-element.42.col1_ref) | copy-start | bytes 24580
  31.4 15.7 %copy-start.20 = (bf16[16,128,256]{2,1,0:T(8,128)(2,1)}, bf16[16,128,256]{2,1,0:T(8,128)(2,1)S(1)}, u32[]{:S(2)}) copy-start(bf16[16,128,256]{2,1,0:T(8,128)(2,1)S(1)} %get-tuple-element.48.g_ref) | copy-start | bytes 3145732
  31.4 14.7 %collective-permute-start.4 = (f32[16,64,256]{2,1,0:T(8,128)S(1)}, f32[16,64,256]{2,1,0:T(8,128)S(1)}, u32[]{:S(2)}, u32[]{:S(2)}) collective-permute-start(f32[16,64,256]{2,1,0:T(8,128)S(1)} %get-tuple-element.35), channel_id=1, source_target_pairs={{0,1},{1,0},{2,3},{3,2},{4,5},{5,4},{6,7},{7,6},{8,9},{9,8},{10,11... | collective-permute-start | bytes 3145736 | tf_op jit(solution)/shard_map/ppermute | solution.py:435
  39.2 8.6 %collective-permute-start.5 = (bf16[128,256]{1,0:T(8,128)(2,1)S(1)}, bf16[128,256]{1,0:T(8,128)(2,1)S(1)}, u32[]{:S(2)}, u32[]{:S(2)}) collective-permute-start(bf16[128,256]{1,0:T(8,128)(2,1)S(1)} %get-tuple-element.36), channel_id=1, source_target_pairs={{0,16},{1,17},{2,18},{3,19},{4,20},{5,21},{6,22},{7,23},{8,24},{9,... | collective-permute-start | bytes 196616 | tf_op jit(solution)/shard_map/ppermute | solution.py:124
  45.5 2.4 %collective-permute-start.6 = (bf16[128,256]{1,0:T(8,128)(2,1)S(1)}, bf16[128,256]{1,0:T(8,128)(2,1)S(1)}, u32[]{:S(2)}, u32[]{:S(2)}) collective-permute-start(bf16[128,256]{1,0:T(8,128)(2,1)S(1)} %get-tuple-element.37), channel_id=1, source_target_pairs={{16,32},{17,33},{18,34},{19,35},{20,36},{21,37},{22,38},{23,39},{2... | collective-permute-start | bytes 196616 | tf_op jit(solution)/shard_map/ppermute | solution.py:124
  47.8 0.6 copy-start.12
  47.8 0.6 copy-start.14
  48.5 20.2 %all-to-all-start = ((bf16[16,64,256]{2,1,0:T(8,128)(2,1)}), bf16[16,64,256]{2,1,0:T(8,128)(2,1)S(1)}, u32[]{:S(2)}, u32[]{:S(2)}) async-start(bf16[16,64,256]{2,1,0:T(8,128)(2,1)} %add_convert_fusion), calls=%async_computation | async-start | bytes 1048576 | tf_op jit(solution)/shard_map/all_to_all | solution.py:446
  60.9 7.8 %collective-permute-start.7 = (bf16[32,256]{1,0:T(8,128)(2,1)}, bf16[32,256]{1,0:T(8,128)(2,1)S(1)}, u32[]{:S(2)}, u32[]{:S(2)}) collective-permute-start(bf16[32,256]{1,0:T(8,128)(2,1)} %get-tuple-element.43), channel_id=1, source_target_pairs={{0,1},{1,0},{2,3},{3,2},{4,5},{5,4},{6,7},{7,6},{8,9},{9,8},{10,11... | collective-permute-start | bytes 49160 | tf_op jit(solution)/shard_map/ppermute | solution.py:124
  63.0 5.7 %collective-permute-start.8 = (bf16[32,256]{1,0:T(8,128)(2,1)}, bf16[32,256]{1,0:T(8,128)(2,1)S(1)}, u32[]{:S(2)}, u32[]{:S(2)}) collective-permute-start(bf16[32,256]{1,0:T(8,128)(2,1)} %get-tuple-element.44), channel_id=1, source_target_pairs={{0,15},{1,2},{2,1},{3,4},{4,3},{5,6},{6,5},{7,8},{8,7},{9,10},{10,... | collective-permute-start | bytes 49160 | tf_op jit(solution)/shard_map/ppermute | solution.py:124
  68.7 4.1 %collective-permute-start.10 = (bf16[64,256]{1,0:T(8,128)(2,1)S(1)}, bf16[64,256]{1,0:T(8,128)(2,1)S(1)}, u32[]{:S(2)}, u32[]{:S(2)}) collective-permute-start(bf16[64,256]{1,0:T(8,128)(2,1)S(1)} %convert_reduce_fusion), channel_id=1, source_target_pairs={{0,32},{1,33},{2,34},{3,35},{4,36},{5,37},{6,38},{7,39},{8,40},{9,... | collective-permute-start | bytes 98312 | tf_op jit(solution)/shard_map/ppermute | solution.py:435
  68.8 4.7 %collective-permute-start.11 = (bf16[64,256]{1,0:T(8,128)(2,1)S(1)}, bf16[64,256]{1,0:T(8,128)(2,1)S(1)}, u32[]{:S(2)}, u32[]{:S(2)}) collective-permute-start(bf16[64,256]{1,0:T(8,128)(2,1)S(1)} %convert_reduce_fusion), channel_id=1, source_target_pairs={{0,48},{1,49},{2,50},{3,51},{4,52},{5,53},{6,54},{7,55},{8,56},{9,... | collective-permute-start | bytes 98312 | tf_op jit(solution)/shard_map/ppermute | solution.py:435
  71.4 2.9 %collective-permute-start.9 = (bf16[64,256]{1,0:T(8,128)(2,1)S(1)}, bf16[64,256]{1,0:T(8,128)(2,1)S(1)}, u32[]{:S(2)}, u32[]{:S(2)}) collective-permute-start(bf16[64,256]{1,0:T(8,128)(2,1)S(1)} %convert_reduce_fusion), channel_id=1, source_target_pairs={{0,16},{1,17},{2,18},{3,19},{4,20},{5,21},{6,22},{7,23},{8,24},{9,... | collective-permute-start | bytes 98312 | tf_op jit(solution)/shard_map/ppermute | solution.py:435
  74.3 4.3 %collective-permute-start.12 = (bf16[64,256]{1,0:T(8,128)(2,1)S(1)}, bf16[64,256]{1,0:T(8,128)(2,1)S(1)}, u32[]{:S(2)}, u32[]{:S(2)}) collective-permute-start(bf16[64,256]{1,0:T(8,128)(2,1)S(1)} %add_convert_fusion.2), channel_id=1, source_target_pairs={{0,56},{1,57},{2,58},{3,59},{4,60},{5,61},{6,62},{7,63},{8,48},{9,... | collective-permute-start | bytes 98312 | tf_op jit(solution)/shard_map/ppermute | solution.py:435
  79.5 11.3 %copy-start.21 = (bf16[16,128,256]{2,1,0:T(8,128)(2,1)S(1)}, bf16[16,128,256]{2,1,0:T(8,128)(2,1)}, u32[]{:S(2)}) copy-start(bf16[16,128,256]{2,1,0:T(8,128)(2,1)} %copy-done.20) | copy-start | bytes 3145732
  79.5 22.7 %all-to-all-start.1 = ((bf16[16,64,256]{2,1,0:T(8,128)(2,1)}), bf16[16,64,256]{2,1,0:T(8,128)(2,1)S(1)}, u32[]{:S(2)}, u32[]{:S(2)}) async-start(bf16[16,64,256]{2,1,0:T(8,128)(2,1)} %broadcast_in_dim.2), calls=%async_computation.1 | async-start | bytes 1048576 | tf_op jit(solution)/shard_map/all_to_all | solution.py:446
  90.5 0.9 copy-start.11
  90.5 0.9 copy-start.13
  90.5 0.9 copy-start.15
  102.2 2.3 %collective-permute-start.13 = (bf16[16,64,256]{2,1,0:T(8,128)(2,1)S(1)}, bf16[16,64,256]{2,1,0:T(8,128)(2,1)S(1)}, u32[]{:S(2)}, u32[]{:S(2)}) collective-permute-start(bf16[16,64,256]{2,1,0:T(8,128)(2,1)S(1)} %all-to-all-done.1), channel_id=1, source_target_pairs={{0,1},{1,0},{2,3},{3,2},{4,5},{5,4},{6,7},{7,6},{8,9},{9,8},{10,11... | collective-permute-start | bytes 1572872 | tf_op jit(solution)/shard_map/ppermute | solution.py:435

commit v4 on v3

v4 whole, which is shorter than its diff:
```python
import math

import jax
import jax.numpy as jnp
from jax import lax
from jax.experimental import pallas as pl
from jax.experimental.pallas import tpu as pltpu
from jax.sharding import PartitionSpec as P

F32 = jnp.float32
BF16 = jnp.bfloat16
BOTH = ("row", "col")
SLOTS = 32
LARGE = pltpu.CompilerParams(vmem_limit_bytes=24 * 1024 * 1024)
SMALL = pltpu.CompilerParams(vmem_limit_bytes=6 * 1024 * 1024)


def dot(lhs, rhs, lhs_dim, rhs_dim):
    return lax.dot_general(
        lhs, rhs, (((lhs_dim,), (rhs_dim,)), ((), ())), preferred_element_type=F32
    )


def iota(shape, dim):
    return lax.broadcasted_iota(jnp.int32, shape, dim)


def as_mask(condition):
    return jnp.where(condition, 1.0, 0.0).astype(BF16)


def halves(value):
    return jnp.concatenate([value[:, :128], value[:, 128:]], axis=0)


def whole(ref, start, rows):
    return jnp.concatenate([ref[start : start + rows], ref[start + rows : start + 2 * rows]], axis=1)


def even(axis):
    return lax.axis_index(axis) % 2 == 0


def choose(condition, value, other):
    return jnp.where(condition, value, other), jnp.where(condition, other, value)


def column_kernel(f_ref, c_ref, st_ref, col0_ref, col1_ref):
    breadth = f_ref.shape[1]
    sides = []
    for col, first in ((breadth - 1, (1, 5)), (0, (2, 6))):
        base = 0 if col == 0 else breadth - 16
        parts = []
        for ref in (f_ref, c_ref):
            parts.append(halves(ref[:, base : base + 16, :].astype(F32)[:, col - base, :]).astype(BF16))
        parts += [st_ref[7 * k + slot] for slot in first for k in range(3)]
        sides.append(parts)
    start = 0
    for right, left in zip(*sides):
        rows = right.shape[0]
        col0_ref[start : start + rows], col1_ref[start : start + rows] = choose(even("col"), right, left)
        start += rows


def pack_columns(features, cotangent, stencil):
    shape = jax.ShapeDtypeStruct((10 * features.shape[0], 128), BF16)
    return pl.pallas_call(
        column_kernel, out_shape=[shape] * 2, compiler_params=SMALL, name="pack_columns"
    )(features, cotangent, stencil)


def row_kernel(f_ref, c_ref, stt_ref, col0_ref, col1_ref, row0_ref, row1_ref):
    height = f_ref.shape[0]
    right, left = choose(even("col"), col0_ref[...].astype(F32), col1_ref[...].astype(F32))
    sides = []
    for row in (height - 2, 0):
        lines = []
        for r in (row, row + 1):
            for field in range(2):
                for rim in (left, right):
                    lines += [rim[(2 * field + h) * height + r :][:1] for h in range(2)]
        for r in (row, row + 1):
            for rim in (left, right):
                lines += [rim[(4 + n) * height + r :][:1] for n in range(6)]
        sides.append(jnp.concatenate(lines + [jnp.zeros((8, 128), F32)], axis=0).astype(BF16))
    for out, side, first in zip((row0_ref, row1_ref), choose(even("row"), *sides), (True, False)):
        base = jnp.where(even("row") == first, height - 2, 0)
        for field, ref in enumerate((f_ref, c_ref)):
            for r in range(2):
                start = 512 * field + 256 * r
                out[start : start + 256] = halves(ref[base + r])
        for r in range(2):
            out[1024 + SLOTS * r : 1024 + SLOTS * (r + 1)] = stt_ref[base + r]
        out[1088:1136] = side


def pack_rows(features, cotangent, stencil_t, cols):
    return pl.pallas_call(
        row_kernel,
        out_shape=[jax.ShapeDtypeStruct((1136, 128), BF16)] * 2,
        compiler_params=SMALL,
        name="pack_rows",
    )(features, cotangent, stencil_t, *cols)


def side_lines(rim, row, field, side):
    start = 1088 + 8 * row + 4 * field + 2 * side
    return jnp.concatenate([rim[start : start + 1], rim[start + 1 : start + 2]], axis=1)


def side_weights(rim, row, side, number):
    start = 1104 + 12 * row + 6 * side + number
    return rim[start : start + 1]


def pair_swap(value, axis, offset):
    rows, cols = lax.axis_size("row"), lax.axis_size("col")
    pairs = []
    for r in range(rows):
        for c in range(cols):
            place = r if axis == "row" else c
            step = 1 if place % 2 == offset else -1
            to_r, to_c = (r + step, c) if axis == "row" else (r, (c + step) % cols)
            if 0 <= to_r < rows:
                pairs.append((r * cols + c, to_r * cols + to_c))
    return lax.ppermute(value, BOTH, pairs)


def both_swaps(first, second, axis):
    return pair_swap(first, axis, 0), pair_swap(second, axis, 1)


def fill_masks(mask_ref):
    j, c = iota((128, 128), 0), iota((128, 128), 1)
    mask_ref[0] = as_mask(j == c)
    mask_ref[1] = as_mask(j == c + 1)
    mask_ref[2] = as_mask(j == c - 1)
    mask_ref[3] = as_mask(((j == 0) & (c < 2)) | ((j == 127) & ((c == 2) | (c == 3))))
    e, l = iota((16, 128), 0), iota((16, 128), 1)
    spots = ((0, 0), (1, 0), (2, 127), (3, 127))
    for number, (edge, lane) in enumerate(spots):
        mask_ref[4, 16 * number : 16 * number + 16] = as_mask((e == edge) & (l == lane))


def beside(left_near, left_far, right_near, right_far):
    lane = iota(left_near.shape, 1)
    spot = lambda value, shift, place: jnp.where(lane == place, pltpu.roll(value, shift, 1), 0.0)
    near = spot(left_near, 1, 0) + spot(right_near, 2, 2)
    return near, spot(left_far, 2, 1), spot(right_far, 3, 3)


def line(weights, slot):
    return jnp.broadcast_to(weights[slot : slot + 1], (16, 128)).astype(BF16)


def tall(value):
    return jnp.concatenate([value] * 8, axis=0)


def field_block(ext_ref, lx_ref, rx_ref, i):
    channels = ext_ref.shape[2]
    e = iota((16, channels), 0)
    edge = jnp.where(e == 0, lx_ref[pl.ds(i, 1)], 0.0)
    edge = jnp.where(e == 1, lx_ref[pl.ds(i - 1, 1)], edge)
    edge = jnp.where(e == 2, rx_ref[pl.ds(i, 1)], edge)
    edge = jnp.where(e == 3, rx_ref[pl.ds(i + 1, 1)], edge)
    rows = ext_ref[pl.ds(i - 1, 3)].reshape(384, channels)
    return jnp.concatenate([rows, edge.astype(BF16), jnp.zeros((112, channels), BF16)], axis=0)


def forward_band(wx_ref, mask_ref, i):
    weights = wx_ref[i].astype(F32)
    same, ahead, back = mask_ref[0], mask_ref[1], mask_ref[2]
    bands = []
    for k in range(3):
        w = [line(weights, 7 * k + s) for s in range(7)]
        t = [tall(x) for x in w]
        spots = [mask_ref[4, 16 * n : 16 * n + 16] for n in range(4)]
        edge = spots[0] * w[2] + spots[1] * w[6] + spots[2] * w[1] + spots[3] * w[5]
        bands.append(
            jnp.concatenate(
                [
                    same * t[4] + back * t[6],
                    same * t[0] + ahead * t[1] + back * t[2],
                    same * t[3] + ahead * t[5],
                    edge,
                    jnp.zeros((112, 128), BF16),
                ],
                axis=0,
            )
        )
    return jnp.concatenate(bands, axis=1)


def transposed_band(wx_ref, we_ref, mask_ref, i):
    before, here, after = (wx_ref[i + d].astype(F32) for d in (-1, 0, 1))
    same, ahead, back = mask_ref[0], mask_ref[1], mask_ref[2]
    bands = []
    for k in range(3):
        at = lambda weights, slot: tall(line(weights, 7 * k + slot))
        edge = we_ref[0, k, pl.ds(i, 1)] + we_ref[1, k, pl.ds(i - 1, 1)] + we_ref[2, k, pl.ds(i + 1, 1)]
        edge = jnp.broadcast_to(edge, (16, 128)).astype(BF16)
        bands.append(
            jnp.concatenate(
                [
                    same * at(before, 3) + ahead * at(before, 5),
                    same * at(here, 0) + ahead * at(here, 1) + back * at(here, 2),
                    same * at(after, 4) + back * at(after, 6),
                    mask_ref[3] * tall(edge),
                ],
                axis=1,
            )
        )
    return jnp.concatenate(bands, axis=0)


def spread(products):
    return [products[128 * k : 128 * k + 128].astype(BF16) for k in range(3)]


def stacks(f_ref, c_ref, wx_ref, we_ref, mask_ref, sides, i):
    flx_ref, frx_ref, clx_ref, crx_ref = sides
    forward = dot(forward_band(wx_ref, mask_ref, i), field_block(f_ref, flx_ref, frx_ref, i), 0, 0)
    turned = dot(
        transposed_band(wx_ref, we_ref, mask_ref, i), field_block(c_ref, clx_ref, crx_ref, i), 1, 0
    )
    return (
        jnp.concatenate([f_ref[i]] + spread(forward), axis=1),
        jnp.concatenate([c_ref[i]] + spread(turned), axis=1),
    )


def hidden_and_grad(ff, tt, w1, w2t):
    pre = dot(ff, w1, 1, 0)
    gate = jax.nn.sigmoid(pre)
    grad = dot(tt, w2t, 1, 0) * gate * (1.0 + pre * (1.0 - gate))
    return (pre * gate).astype(BF16), grad


def totals_of(hidden, tt, ff, grad):
    channels = hidden.shape[1]
    second = dot(hidden, tt, 0, 0)
    second = [
        second[:, k * channels : (k + 1) * channels].reshape(4, channels // 4, channels) for k in range(4)
    ]
    return second, dot(ff, grad, 0, 0).reshape(16, channels // 4, channels)


def inner_kernel(
    f_ref, c_ref, stt_ref, col0_ref, col1_ref, w1_ref, w2_ref,
    g_ref, total_ref, glx_ref, grx_ref,
    ff_ref, tt_ref, we_ref, mask_ref, *sides,
):
    height = f_ref.shape[0]
    fill_masks(mask_ref)
    right, left = choose(even("col"), col0_ref[...], col1_ref[...])
    for field in range(2):
        for rim, side in ((left, sides[2 * field]), (right, sides[2 * field + 1])):
            side[...] = whole(rim, 2 * field * height, height).astype(F32)
    for k in range(3):
        near, far = (4 + k) * height, (7 + k) * height
        weights = [rim[at : at + height].astype(F32) for rim in (left, right) for at in (near, far)]
        we_ref[0, k], we_ref[1, k], we_ref[2, k] = beside(*weights)

    @pl.loop(1, height - 1, unroll=7)
    def _(r):
        rows = pl.ds(pl.multiple_of((r - 1) * 128, 128), 128)
        ff_ref[rows], tt_ref[rows] = stacks(f_ref, c_ref, stt_ref, we_ref, mask_ref, sides, r)

    batch = (height - 2) // 2
    for i in range(2):
        rows = pl.ds(i * batch * 128, batch * 128)
        hidden, grad = hidden_and_grad(ff_ref[rows], tt_ref[rows], w1_ref[...], w2_ref[...])
        for q in range(batch):
            g_ref[i * batch + q] = grad[q * 128 : q * 128 + 128].astype(BF16)
            row = 1 + i * batch + q
            glx_ref[row : row + 1] = grad[q * 128 : q * 128 + 1]
            grx_ref[row : row + 1] = grad[q * 128 + 127 : q * 128 + 128]
        second, first = totals_of(hidden, tt_ref[rows], ff_ref[rows], grad.astype(BF16))
        for k in range(4):
            total_ref[0, 4 * k : 4 * k + 4] = second[k] if i == 0 else total_ref[0, 4 * k : 4 * k + 4] + second[k]
        total_ref[1] = first if i == 0 else total_ref[1] + first


def outer_kernel(
    f_ref, c_ref, stt_ref, col0_ref, col1_ref, row0_ref, row1_ref, w1_ref, w2_ref,
    total_ref, glx_ref, grx_ref,
    g_ref, gcol0_ref, gcol1_ref, keep_ref, send_ref,
    fext_ref, cext_ref, wx_ref, we_ref, mask_ref, *sides,
):
    height, breadth, channels = f_ref.shape
    fill_masks(mask_ref)
    below, above = choose(even("row"), row0_ref[...], row1_ref[...])
    right, left = choose(even("col"), col0_ref[...], col1_ref[...])
    ends = (0, 1, height - 2, height - 1)
    for n, (rim, at) in enumerate(((above, 0), (below, 6))):
        for r in range(2):
            fext_ref[at + r] = whole(rim, 256 * r, breadth)
            cext_ref[at + r] = whole(rim, 512 + 256 * r, breadth)
            wx_ref[at + r] = rim[1024 + SLOTS * r : 1024 + SLOTS * (r + 1)]
    for n, r in enumerate(ends):
        fext_ref[2 + n] = f_ref[r]
        cext_ref[2 + n] = c_ref[r]
        wx_ref[2 + n] = stt_ref[r]
    above, below = above.astype(F32), below.astype(F32)
    picked = lambda value: [value[r : r + 1] for r in ends]
    rims = (left.astype(F32), right.astype(F32))
    for field in range(2):
        for side in range(2):
            own = whole(rims[side], 2 * field * height, height)
            lines = [side_lines(above, r, field, side) for r in range(2)] + picked(own)
            lines += [side_lines(below, r, field, side) for r in range(2)]
            sides[2 * field + side][...] = jnp.concatenate(lines, axis=0)
    for k in range(3):
        weights = []
        for side in range(2):
            for number in (k, 3 + k):
                own = rims[side][(4 + number) * height : (5 + number) * height]
                lines = [side_weights(above, r, side, number) for r in range(2)] + picked(own)
                lines += [side_weights(below, r, side, number) for r in range(2)]
                weights.append(jnp.concatenate(lines, axis=0))
        we_ref[0, k], we_ref[1, k], we_ref[2, k] = beside(*weights)

    made = [stacks(fext_ref, cext_ref, wx_ref, we_ref, mask_ref, sides, i) for i in (2, 5, 1, 6)]
    ff = jnp.concatenate([m[0] for m in made], axis=0)
    tt = jnp.concatenate([m[1] for m in made], axis=0)
    hidden, grad = hidden_and_grad(ff, tt, w1_ref[...], w2_ref[...])
    own = 2 * breadth
    row, last = lax.axis_index("row"), lax.axis_size("row") - 1
    parts = [grad[128 * n : 128 * n + 128] for n in range(4)]
    parts[2] = jnp.where(row > 0, parts[2], 0.0)
    parts[3] = jnp.where(row < last, parts[3], 0.0)
    for n in range(4):
        g_ref[n] = parts[n].astype(BF16)
    spare = jnp.zeros((14, channels), F32)
    edges = []
    for inner, at in ((grx_ref, 127), (glx_ref, 0)):
        cut = lambda n: parts[n][at : at + 1]
        lines = [cut(2), cut(0), inner[1 : height - 1], cut(1), cut(3), spare]
        edges.append(jnp.concatenate(lines, axis=0).astype(BF16))
    gcol0_ref[...], gcol1_ref[...] = choose(even("col"), *edges)
    second, first = totals_of(hidden[:own], tt[:own], ff[:own], grad[:own].astype(BF16))
    core = lax.axis_index("col") % 2 == 0
    for k in range(4):
        at = slice(4 * k, 4 * k + 4)
        keep_ref[at], send_ref[at] = choose(
            core, total_ref[0, at] + second[k], total_ref[1, at] + first[at]
        )


def input_kernel(
    inner_ref, outer_ref, gcol0_ref, gcol1_ref, stt_ref, col0_ref, col1_ref, row0_ref, row1_ref, w1t_ref,
    out_ref,
    gext_ref, tt_ref, wx_ref, we_ref, mask_ref, lx_ref, rx_ref,
):
    height, breadth, _ = out_ref.shape
    fill_masks(mask_ref)
    below, above = choose(even("row"), row0_ref[1024:], row1_ref[1024:])
    right, left = choose(even("col"), col0_ref[4 * height :], col1_ref[4 * height :])
    wx_ref[0] = above[SLOTS : 2 * SLOTS]
    wx_ref[1 : 1 + height] = stt_ref[...]
    wx_ref[1 + height] = below[0:SLOTS]
    above, below = above.astype(F32), below.astype(F32)
    spare = jnp.zeros((6, 128), F32)
    for k in range(3):
        weights = []
        for side, rim in enumerate((left, right)):
            for number in (k, 3 + k):
                at = 80 + 6 * side + number
                lines = [above[at + 12 : at + 13], rim[number * height : (number + 1) * height].astype(F32)]
                weights.append(jnp.concatenate(lines + [below[at : at + 1], spare], axis=0))
        we_ref[0, k], we_ref[1, k], we_ref[2, k] = beside(*weights)
    gext_ref[0], gext_ref[1] = outer_ref[2], outer_ref[0]
    gext_ref[2:height] = inner_ref[...]
    gext_ref[height], gext_ref[height + 1] = outer_ref[1], outer_ref[3]
    right, left = choose(even("col"), gcol0_ref[...].astype(F32), gcol1_ref[...].astype(F32))
    lx_ref[...], rx_ref[...] = left, right

    @pl.loop(0, height, unroll=8)
    def _(r):
        rows = pl.ds(pl.multiple_of(r * 128, 128), 128)
        turned = dot(
            transposed_band(wx_ref, we_ref, mask_ref, r + 1), field_block(gext_ref, lx_ref, rx_ref, r + 1), 1, 0
        )
        tt_ref[rows] = jnp.concatenate([gext_ref[r + 1]] + spread(turned), axis=1)

    batch = 4

    @pl.loop(0, height // batch)
    def _(i):
        rows = pl.ds(pl.multiple_of(i * batch * 128, batch * 128), batch * 128)
        result = dot(tt_ref[rows], w1t_ref[...], 1, 0).astype(BF16)
        for q in range(batch):
            out_ref[i * batch + q] = result[q * 128 : q * 128 + 128]


MASKS = pltpu.VMEM((5, 128, 128), BF16)


def inner_gradients(features, cotangent, stencil_t, cols, w1, w2t):
    height, breadth, channels = features.shape
    shape = jax.ShapeDtypeStruct
    vertices = (height - 2) * breadth
    return pl.pallas_call(
        inner_kernel,
        out_shape=[
            shape((height - 2, breadth, channels), BF16),
            shape((2, 16, channels // 4, channels), F32),
            shape((height, channels), F32),
            shape((height, channels), F32),
        ],
        scratch_shapes=[
            pltpu.VMEM((vertices, 4 * channels), BF16),
            pltpu.VMEM((vertices, 4 * channels), BF16),
            pltpu.VMEM((3, 3, height, 128), F32),
            MASKS,
        ]
        + [pltpu.VMEM((height, channels), F32)] * 4,
        compiler_params=LARGE,
        cost_estimate=pl.CostEstimate(
            flops=9 * 10**9, bytes_accessed=9 * 10**6, transcendentals=vertices * channels
        ),
        name="inner_gradients",
    )(features, cotangent, stencil_t, *cols, w1, w2t)


def outer_gradients(features, cotangent, stencil_t, cols, rows, w1, w2t, inner):
    height, breadth, channels = features.shape
    shape = jax.ShapeDtypeStruct
    totals = (16, channels // 4, channels)
    return pl.pallas_call(
        outer_kernel,
        out_shape=[
            shape((4, breadth, channels), BF16),
            shape((height + 16, channels), BF16),
            shape((height + 16, channels), BF16),
            shape(totals, F32),
            shape(totals, F32),
        ],
        scratch_shapes=[
            pltpu.VMEM((8, breadth, channels), BF16),
            pltpu.VMEM((8, breadth, channels), BF16),
            pltpu.VMEM((8, SLOTS, 128), BF16),
            pltpu.VMEM((3, 3, 8, 128), F32),
            MASKS,
        ]
        + [pltpu.VMEM((8, channels), F32)] * 4,
        compiler_params=LARGE,
        cost_estimate=pl.CostEstimate(flops=2 * 10**9, bytes_accessed=5 * 10**6, transcendentals=10**5),
        name="outer_gradients",
    )(features, cotangent, stencil_t, *cols, *rows, w1, w2t, *inner)


def input_gradient(inner, outer, gcols, stencil_t, cols, rows, w1t):
    breadth, channels = inner.shape[1:]
    height = inner.shape[0] + 2
    return pl.pallas_call(
        input_kernel,
        out_shape=jax.ShapeDtypeStruct((height, breadth, channels), BF16),
        scratch_shapes=[
            pltpu.VMEM((height + 2, breadth, channels), BF16),
            pltpu.VMEM((height * breadth, 4 * channels), BF16),
            pltpu.VMEM((height + 2, SLOTS, 128), BF16),
            pltpu.VMEM((3, 3, height + 8, 128), F32),
            MASKS,
            pltpu.VMEM((height + 16, channels), F32),
            pltpu.VMEM((height + 16, channels), F32),
        ],
        compiler_params=LARGE,
        cost_estimate=pl.CostEstimate(flops=3 * 10**9, bytes_accessed=3 * 10**6, transcendentals=0),
        name="input_gradient",
    )(inner, outer, *gcols, stencil_t, *cols, *rows, w1t)


def swap(value, row_bits, col_bits):
    rows, cols = lax.axis_size("row"), lax.axis_size("col")
    pairs = [
        (r * cols + c, (r ^ row_bits) * cols + (c ^ col_bits)) for r in range(rows) for c in range(cols)
    ]
    return lax.ppermute(value, BOTH, pairs)


def plane_trade(value):
    cols = lax.axis_size("col")
    planes = [
        [cols * (4 * x + z) + 8 * h + 2 * y + core for x in range(4) for y in range(4)]
        for z in range(4)
        for h in range(2)
        for core in range(2)
    ]
    return lax.all_to_all(value, BOTH, 0, 0, axis_index_groups=planes, tiled=True)


def sum_line(total):
    total = total.astype(BF16)
    came = [swap(total, d, 0).astype(F32) for d in (1, 2, 3)]
    total = ((total.astype(F32) + came[0]) + (came[1] + came[2])).astype(BF16)
    return total, swap(total, 3, 8)


def body(features_in, stencil, weights_first, weights_second, cotangent):
    height, breadth, channels = features_in.shape
    scale = 1.0 / math.sqrt(height * breadth * lax.axis_size("row") * lax.axis_size("col"))
    flat = stencil.reshape(21, height, breadth)
    stencil_t = jnp.pad(flat.transpose(1, 0, 2), ((0, 0), (0, SLOTS - 21), (0, 0)))
    w1 = weights_first.reshape(4 * channels, channels)
    w1t = weights_first.transpose(0, 2, 1).reshape(4 * channels, channels)
    w2t = weights_second.transpose(0, 2, 1).reshape(4 * channels, channels)

    cols = both_swaps(*pack_columns(features_in, cotangent, flat), "col")
    rows = both_swaps(*pack_rows(features_in, cotangent, stencil_t, cols), "row")
    inner, *sums = inner_gradients(features_in, cotangent, stencil_t, cols, w1, w2t)
    outer, gcol0, gcol1, keep, send = outer_gradients(
        features_in, cotangent, stencil_t, cols, rows, w1, w2t, sums
    )
    half = (keep + swap(send, 0, 1)).astype(BF16)
    gcols = both_swaps(gcol0, gcol1, "col")
    part = plane_trade(half).astype(F32).sum(0)
    part, gcols = lax.optimization_barrier((part, gcols))
    part, other = sum_line(part)
    part = (part.astype(F32) + other.astype(F32)).astype(BF16)
    part, inner = lax.optimization_barrier((part, inner))
    input_grad = input_gradient(inner, outer, gcols, stencil_t, cols, rows, w1t)
    mine = plane_trade(jnp.broadcast_to(part[None], keep.shape))
    mine, input_grad = lax.optimization_barrier((mine, input_grad))
    theirs = swap(mine, 0, 1)
    mine, theirs = mine.astype(F32) * scale, theirs.astype(F32) * scale
    second = jnp.where(even("col"), mine, theirs).reshape(4, channels, channels)
    first = jnp.where(even("col"), theirs, mine).reshape(4, channels, channels)
    return input_grad, first, second


def solution(mesh):
    return jax.shard_map(
        body,
        mesh=mesh,
        in_specs=(
            P("row", "col", None),
            P(None, None, "row", "col"),
            P(),
            P(),
            P("row", "col", None),
        ),
        out_specs=(P("row", "col", None), P(), P()),
        check_vma=False,
    )
```

time: 107 us -> 91.4 us (0.85)
  starting transfers between devices: 53.4 us -> 41.3 us
  local copies, waits for them, and re-layouts: 11.5 us -> 7.34 us
  waiting for transfers between devices: 18.2 us -> 21.6 us
  Pallas kernels: 19.5 us -> 16.1 us
    ppermute x8 -> x6, starting transfers between devices: 17.1 us -> 6.34 us  [pair_swap(): return lax.ppermute(value, BOTH, pairs)]
    all_to_all x2, starting transfers between devices: 21.9 us -> 16.7 us  [plane_trade(): lax.all_to_all(value, BOTH, 0, 0, axis_index_groups=planes, tiled=True)]
    ppermute x6, starting transfers between devices: 14.3 us -> 18.3 us  [swap(): return lax.ppermute(value, BOTH, pairs)]
    pallas_call x4, Pallas kernels: 14 us -> 10.7 us  [the longest x1 8.33 us: inner_gradients(): pl.pallas_call(inner_kernel, out_shape=[shape((height - 2, breadth, chann...]
    unnamed x44 -> x30, local copies, waits for them, and re-layouts: 7.53 us -> 5 us
    all_to_all x2, waiting for transfers between devices: 9.39 us -> 11.7 us  [plane_trade(): lax.all_to_all(value, BOTH, 0, 0, axis_index_groups=planes, tiled=True)]
    ppermute x6, waiting for transfers between devices: 5.6 us -> 7.84 us  [swap(): return lax.ppermute(value, BOTH, pairs)]
    ppermute x8 -> x6, waiting for transfers between devices: 3.27 us -> 2.12 us  [pair_swap(): return lax.ppermute(value, BOTH, pairs)]
  transfers between devices with their start and end apart: 16 -> 14, of which waited for: 10 -> 8; matrix products, arithmetic and copies ran while one was open for 4% -> 2% of each run, Pallas kernels for 7% -> 15%
where the time goes in v4:
time: 91.4 us; the launch traced here: 90.9 us
  starting transfers between devices  41.3 us (45%)
  waiting for transfers between devices  21.6 us (24%)
  Pallas kernels  16.1 us (18%)
  local copies, waits for them, and re-layouts  7.34 us (8%)
  other arithmetic  3.65 us (4%)
    ppermute x6, starting transfers between devices, swap(): return lax.ppermute(value, BOTH, pairs)  18.3 us
    all_to_all x2, starting transfers between devices, plane_trade(): lax.all_to_all(value, BOTH, 0, 0, axis_index_groups=planes, tiled=True)  16.7 us
    all_to_all x2, waiting for transfers between devices, plane_trade(): lax.all_to_all(value, BOTH, 0, 0, axis_index_groups=planes, tiled=True)  11.7 us
    pallas_call x1, Pallas kernels, inner_gradients(): pl.pallas_call(inner_kernel, out_shape=[shape((height - 2, breadth, chann...  8.33 us
    ppermute x6, waiting for transfers between devices, swap(): return lax.ppermute(value, BOTH, pairs)  7.84 us
    ppermute x6, starting transfers between devices, pair_swap(): return lax.ppermute(value, BOTH, pairs)  6.34 us
    pallas_call x1, Pallas kernels, input_gradient(): pl.pallas_call(input_kernel, out_shape=jax.ShapeDtypeStruct((height, brea...  5.37 us
    unnamed x30, local copies, waits for them, and re-layouts  5 us
  transfers between devices with their start and end apart: 14, of which 8 were waited for; matrix products, arithmetic and copies ran while one was open for 2% of the time, Pallas kernels for 15%

profile of v4, /device:TPU:1, one launch (start us, length us, event | category | flops | bytes accessed | tf_op | source)
XLA Modules:
  0.0 90.9 jit_solution(1643882516497828675)
XLA Ops:
  0.6 0.0 copy-start
  0.6 1.2 %copy-done = bf16[16,128,256]{2,1,0:T(8,128)(2,1)S(1)} copy-done((bf16[16,128,256]{2,1,0:T(8,128)(2,1)S(1)}, bf16[16,128,256]{2,1,0:T(8,128)(2,1)}, u32[]{:S(2)}) %copy-start) | copy-done | bytes 1048600
  1.9 0.0 copy-start.2
  1.9 1.2 %copy-done.2 = bf16[16,128,256]{2,1,0:T(8,128)(2,1)S(1)} copy-done((bf16[16,128,256]{2,1,0:T(8,128)(2,1)S(1)}, bf16[16,128,256]{2,1,0:T(8,128)(2,1)}, u32[]{:S(2)}) %copy-start.2) | copy-done | bytes 1048600
  3.1 0.0 copy-start.5
  3.1 0.9 copy-done.5
  4.0 0.0 copy-start.6
  4.0 0.0 copy-start.1
  4.0 0.0 copy-start.3
  4.0 0.1 pack_columns.1
  4.0 0.0 copy-start.4
  4.1 3.3 %collective-permute-start = (bf16[160,128]{1,0:T(8,128)(2,1)S(1)}, bf16[160,128]{1,0:T(8,128)(2,1)S(1)}, u32[]{:S(2)}, u32[]{:S(2)}) collective-permute-start(bf16[160,128]{1,0:T(8,128)(2,1)S(1)} %get-tuple-element.23), channel_id=1, source_target_pairs={{0,1},{1,0},{2,3},{3,2},{4,5},{5,4},{6,7},{7,6},{8,9},{9,8},{10,11... | collective-permute-start | bytes 122888 | tf_op jit(solution)/shard_map/ppermute | solution.py:126
  7.4 0.0 collective-permute-start.1
  7.4 0.0 copy-done.6
  7.4 1.2 %copy.13 = bf16[4,256,256]{2,1,0:T(8,128)(2,1)S(1)} copy(bf16[4,256,256]{1,2,0:T(8,128)(2,1)} %bitcast.21) | data formatting | bytes 1048576 | tf_op jit(solution)/shard_map/transpose | solution.py:508
  8.7 0.0 collective-permute-done.col0_ref
  8.7 2.1 %collective-permute-done.1.col1_ref = bf16[160,128]{1,0:T(8,128)(2,1)S(1)} collective-permute-done((bf16[160,128]{1,0:T(8,128)(2,1)S(1)}, bf16[160,128]{1,0:T(8,128)(2,1)S(1)}, u32[]{:S(2)}, u32[]{:S(2)}) %collective-permute-start.1) | collective-permute-done | bytes 40992 | tf_op jit(solution)/shard_map/ppermute | solution.py:126
  10.8 0.0 copy-done.1
  10.8 0.0 copy-done.3
  10.8 0.1 pack_rows.1
  10.9 0.1 collective-permute-start.2
  11.0 0.7 collective-permute-start.3
  11.7 0.0 copy-done.4
  11.7 8.3 %inner_gradients.1 = (bf16[14,128,256]{2,1,0:T(8,128)(2,1)S(1)}, f32[2,16,64,256]{3,2,1,0:T(8,128)S(1)}, f32[16,256]{1,0:T(8,128)S(1)}, f32[16,256]{1,0:T(8,128)S(1)}) custom-call(bf16[16,128,256]{2,1,0:T(8,128)(2,1)S(1)} %copy-done.1, bf16[16,128,256]{2,1,0:T(8,128)(2,1)S(1)} %copy-done.3, bf16[16,32,128]{2,1,0:T(8,128)(2,1)S(1)} %pad.4.stt_ref, ...), custom_call_target="tpu_custom_call" | custom-call | flops 8999999488 | bytes 9000000 | tf_op jit(solution)/shard_map/inner_gradients/pallas_call | solution.py:404
  20.1 0.0 copy-start.13
  20.1 0.9 %copy-done.13 = bf16[14,128,256]{2,1,0:T(8,128)(2,1)} copy-done((bf16[14,128,256]{2,1,0:T(8,128)(2,1)}, bf16[14,128,256]{2,1,0:T(8,128)(2,1)S(1)}, u32[]{:S(2)}) %copy-start.13) | copy-done | bytes 917528
  21.0 0.0 collective-permute-done.2.row0_ref
  21.0 0.0 collective-permute-done.3.row1_ref
  21.0 0.0 copy-start.9
  21.0 2.2 %outer_gradients.1 = (bf16[4,128,256]{2,1,0:T(8,128)(2,1)S(1)}, bf16[32,256]{1,0:T(8,128)(2,1)S(1)}, bf16[32,256]{1,0:T(8,128)(2,1)S(1)}, f32[16,64,256]{2,1,0:T(8,128)S(1)}, f32[16,64,256]{2,1,0:T(8,128)S(1)}) custom-call(bf16[16,128,256]{2,1,0:T(8,128)(2,1)S(1)} %copy-done.1, bf16[16,128,256]{2,1,0:T(8,128)(2,1)S(1)} %copy-done.3, ...), custom_call_target="tpu_custom_call" | custom-call | flops 2000000000 | bytes 5000000 | tf_op jit(solution)/shard_map/outer_gradients/pallas_call | solution.py:431
  23.2 0.0 copy-done.7
  23.2 0.0 copy-done.9
  23.2 0.0 copy-start.11
  23.2 0.7 copy-done.11
  23.9 7.3 %collective-permute-start.4 = (f32[16,64,256]{2,1,0:T(8,128)S(1)}, f32[16,64,256]{2,1,0:T(8,128)S(1)}, u32[]{:S(2)}, u32[]{:S(2)}) collective-permute-start(f32[16,64,256]{2,1,0:T(8,128)S(1)} %get-tuple-element.31), channel_id=1, source_target_pairs={{0,1},{1,0},{2,3},{3,2},{4,5},{5,4},{6,7},{7,6},{8,9},{9,8},{10,11... | collective-permute-start | bytes 3145736 | tf_op jit(solution)/shard_map/ppermute | solution.py:480
  31.2 2.3 %collective-permute-done.4 = f32[16,64,256]{2,1,0:T(8,128)S(1)} collective-permute-done((f32[16,64,256]{2,1,0:T(8,128)S(1)}, f32[16,64,256]{2,1,0:T(8,128)S(1)}, u32[]{:S(2)}, u32[]{:S(2)}) %collective-permute-start.4) | collective-permute-done | bytes 1048608 | tf_op jit(solution)/shard_map/ppermute | solution.py:480
  33.5 0.9 %add_convert_fusion = bf16[16,64,256]{2,1,0:T(8,128)(2,1)} fusion(f32[16,64,256]{2,1,0:T(8,128)S(1)} %get-tuple-element.30, f32[16,64,256]{2,1,0:T(8,128)S(1)} %collective-permute-done.4), kind=kLoop, calls=%fused_computation.5 | loop fusion | flops 524288 | bytes 2621440 | tf_op jit(solution)/shard_map/convert_element_type | solution.py:516
  34.4 9.9 %all-to-all-start = ((bf16[16,64,256]{2,1,0:T(8,128)(2,1)}), bf16[16,64,256]{2,1,0:T(8,128)(2,1)S(1)}, u32[]{:S(2)}, u32[]{:S(2)}) async-start(bf16[16,64,256]{2,1,0:T(8,128)(2,1)} %add_convert_fusion), calls=%async_computation | async-start | bytes 1048576 | tf_op jit(solution)/shard_map/all_to_all | solution.py:491
  44.4 0.5 collective-permute-start.5
  44.9 1.7 %collective-permute-start.6 = (bf16[32,256]{1,0:T(8,128)(2,1)S(1)}, bf16[32,256]{1,0:T(8,128)(2,1)S(1)}, u32[]{:S(2)}, u32[]{:S(2)}) collective-permute-start(bf16[32,256]{1,0:T(8,128)(2,1)S(1)} %get-tuple-element.33), channel_id=1, source_target_pairs={{0,15},{1,2},{2,1},{3,4},{4,3},{5,6},{6,5},{7,8},{8,7},{9,10},{10,... | collective-permute-start | bytes 49160 | tf_op jit(solution)/shard_map/ppermute | solution.py:126
  46.6 8.0 %all-to-all-done = bf16[16,64,256]{2,1,0:T(8,128)(2,1)S(1)} async-done(((bf16[16,64,256]{2,1,0:T(8,128)(2,1)}), bf16[16,64,256]{2,1,0:T(8,128)(2,1)S(1)}, u32[]{:S(2)}, u32[]{:S(2)}) %all-to-all-start) | async-done | bytes 524320 | tf_op jit(solution)/shard_map/all_to_all | solution.py:491
  54.7 0.1 convert_reduce_fusion
  54.7 0.0 collective-permute-done.5.gcol0_ref
  54.7 0.0 collective-permute-done.6.gcol1_ref
  54.7 0.6 collective-permute-start.7
  55.4 0.9 %collective-permute-start.8 = (bf16[64,256]{1,0:T(8,128)(2,1)S(1)}, bf16[64,256]{1,0:T(8,128)(2,1)S(1)}, u32[]{:S(2)}, u32[]{:S(2)}) collective-permute-start(bf16[64,256]{1,0:T(8,128)(2,1)S(1)} %convert_reduce_fusion), channel_id=1, source_target_pairs={{0,32},{1,33},{2,34},{3,35},{4,36},{5,37},{6,38},{7,39},{8,40},{9,... | collective-permute-start | bytes 98312 | tf_op jit(solution)/shard_map/ppermute | solution.py:480
  56.3 2.1 %collective-permute-start.9 = (bf16[64,256]{1,0:T(8,128)(2,1)S(1)}, bf16[64,256]{1,0:T(8,128)(2,1)S(1)}, u32[]{:S(2)}, u32[]{:S(2)}) collective-permute-start(bf16[64,256]{1,0:T(8,128)(2,1)S(1)} %convert_reduce_fusion), channel_id=1, source_target_pairs={{0,48},{1,49},{2,50},{3,51},{4,52},{5,53},{6,54},{7,55},{8,56},{9,... | collective-permute-start | bytes 98312 | tf_op jit(solution)/shard_map/ppermute | solution.py:480
  58.4 0.0 collective-permute-done.7
  58.4 0.7 collective-permute-done.8
  59.0 1.8 %collective-permute-done.9 = bf16[64,256]{1,0:T(8,128)(2,1)S(1)} collective-permute-done((bf16[64,256]{1,0:T(8,128)(2,1)S(1)}, bf16[64,256]{1,0:T(8,128)(2,1)S(1)}, u32[]{:S(2)}, u32[]{:S(2)}) %collective-permute-start.9) | collective-permute-done | bytes 32800 | tf_op jit(solution)/shard_map/ppermute | solution.py:480
  60.9 4.2 %collective-permute-start.10 = (bf16[64,256]{1,0:T(8,128)(2,1)S(1)}, bf16[64,256]{1,0:T(8,128)(2,1)S(1)}, u32[]{:S(2)}, u32[]{:S(2)}) collective-permute-start(bf16[64,256]{1,0:T(8,128)(2,1)S(1)} %add_convert_fusion.2), channel_id=1, source_target_pairs={{0,56},{1,57},{2,58},{3,59},{4,60},{5,61},{6,62},{7,63},{8,48},{9,... | collective-permute-start | bytes 98312 | tf_op jit(solution)/shard_map/ppermute | solution.py:480
  65.1 1.3 %collective-permute-done.10 = bf16[64,256]{1,0:T(8,128)(2,1)S(1)} collective-permute-done((bf16[64,256]{1,0:T(8,128)(2,1)S(1)}, bf16[64,256]{1,0:T(8,128)(2,1)S(1)}, u32[]{:S(2)}, u32[]{:S(2)}) %collective-permute-start.10) | collective-permute-done | bytes 32800 | tf_op jit(solution)/shard_map/ppermute | solution.py:480
  66.4 0.8 broadcast_in_dim.2
  67.2 6.7 %all-to-all-start.1 = ((bf16[16,64,256]{2,1,0:T(8,128)(2,1)}), bf16[16,64,256]{2,1,0:T(8,128)(2,1)}, u32[]{:S(2)}, u32[]{:S(2)}) async-start(bf16[16,64,256]{2,1,0:T(8,128)(2,1)} %broadcast_in_dim.2), calls=%async_computation.1 | async-start | bytes 1048576 | tf_op jit(solution)/shard_map/all_to_all | solution.py:491
  74.0 0.2 copy.14
  74.2 0.0 copy-done.8
  74.2 0.0 copy-done.10
  74.2 0.0 copy-done.12
  74.2 0.0 copy-done.14
  74.2 5.4 %input_gradient.1 = bf16[16,128,256]{2,1,0:T(8,128)(2,1)} custom-call(bf16[14,128,256]{2,1,0:T(8,128)(2,1)S(1)} %copy-done.14, bf16[4,128,256]{2,1,0:T(8,128)(2,1)S(1)} %copy-done.12, bf16[32,256]{1,0:T(8,128)(2,1)S(1)} %collective-permute-done.5.gcol0_ref, bf16[32,256]{1,0:T(8,128)(2,1)S(1)} %collective-permute-done.6.gcol1_ref, ...), custom_call_target="tpu_custom_call" | custom-call | flops 3000000000 | bytes 3000000 | tf_op jit(solution)/shard_map/input_gradient/pallas_call | solution.py:457
  79.6 3.6 %all-to-all-done.1 = bf16[16,64,256]{2,1,0:T(8,128)(2,1)} async-done(((bf16[16,64,256]{2,1,0:T(8,128)(2,1)}), bf16[16,64,256]{2,1,0:T(8,128)(2,1)}, u32[]{:S(2)}, u32[]{:S(2)}) %all-to-all-start.1) | async-done | bytes 524320 | tf_op jit(solution)/shard_map/all_to_all | solution.py:491
  83.3 3.2 %collective-permute-start.11 = (bf16[16,64,256]{2,1,0:T(8,128)(2,1)}, bf16[16,64,256]{2,1,0:T(8,128)(2,1)S(1)}, u32[]{:S(2)}, u32[]{:S(2)}) collective-permute-start(bf16[16,64,256]{2,1,0:T(8,128)(2,1)} %all-to-all-done.1), channel_id=1, source_target_pairs={{0,1},{1,0},{2,3},{3,2},{4,5},{5,4},{6,7},{7,6},{8,9},{9,8},{10,11... | collective-permute-start | bytes 1572872 | tf_op jit(solution)/shard_map/ppermute | solution.py:480
  86.5 1.7 %collective-permute-done.11 = bf16[16,64,256]{2,1,0:T(8,128)(2,1)S(1)} collective-permute-done((bf16[16,64,256]{2,1,0:T(8,128)(2,1)}, bf16[16,64,256]{2,1,0:T(8,128)(2,1)S(1)}, u32[]{:S(2)}, u32[]{:S(2)}) %collective-permute-start.11) | collective-permute-done | bytes 524320 | tf_op jit(solution)/shard_map/ppermute | solution.py:480
  88.2 2.6 %fusion = (f32[16,64,256]{2,1,0:T(8,128)}, f32[16,64,256]{2,1,0:T(8,128)}) fusion(bf16[16,64,256]{2,1,0:T(8,128)(2,1)} %all-to-all-done.1, bf16[16,64,256]{2,1,0:T(8,128)(2,1)S(1)} %collective-permute-done.11, pred[]{:T(512)S(6)} %eq.7), kind=kLoop, calls=%fused_computation.1 | loop fusion | flops 1572864 | bytes 3145729 | tf_op jit(solution)/shard_map/jit(_where)/select_n | solution.py:528
  (9 shorter events, 0.1 us)
Async XLA Ops:
  0.6 1.2 %copy-start = (bf16[16,128,256]{2,1,0:T(8,128)(2,1)S(1)}, bf16[16,128,256]{2,1,0:T(8,128)(2,1)}, u32[]{:S(2)}) copy-start(bf16[16,128,256]{2,1,0:T(8,128)(2,1)} %f_ref.7) | copy-start | bytes 3145732
  1.9 1.2 %copy-start.2 = (bf16[16,128,256]{2,1,0:T(8,128)(2,1)S(1)}, bf16[16,128,256]{2,1,0:T(8,128)(2,1)}, u32[]{:S(2)}) copy-start(bf16[16,128,256]{2,1,0:T(8,128)(2,1)} %c_ref.7) | copy-start | bytes 3145732
  3.1 0.9 copy-start.5
  4.0 3.4 %copy-start.6 = (bf16[3,7,16,128]{3,2,1,0:T(8,128)(2,1)S(1)}, bf16[3,7,16,128]{3,2,1,0:T(8,128)(2,1)}, u32[]{:S(2)}) copy-start(bf16[3,7,16,128]{3,2,1,0:T(8,128)(2,1)} %param.6) | copy-start | bytes 258052
  4.0 6.8 %copy-start.1 = (bf16[16,128,256]{2,1,0:T(8,128)(2,1)S(1)}, bf16[16,128,256]{2,1,0:T(8,128)(2,1)}, u32[]{:S(2)}) copy-start(bf16[16,128,256]{2,1,0:T(8,128)(2,1)} %f_ref.7) | copy-start | bytes 3145732
  4.0 6.8 %copy-start.3 = (bf16[16,128,256]{2,1,0:T(8,128)(2,1)S(1)}, bf16[16,128,256]{2,1,0:T(8,128)(2,1)}, u32[]{:S(2)}) copy-start(bf16[16,128,256]{2,1,0:T(8,128)(2,1)} %c_ref.7) | copy-start | bytes 3145732
  4.0 7.7 %copy-start.4 = (bf16[4,256,256]{2,1,0:T(8,128)(2,1)S(1)}, bf16[4,256,256]{2,1,0:T(8,128)(2,1)}, u32[]{:S(2)}) copy-start(bf16[4,256,256]{2,1,0:T(8,128)(2,1)} %param.7) | copy-start | bytes 1572868
  4.1 4.6 %collective-permute-start = (bf16[160,128]{1,0:T(8,128)(2,1)S(1)}, bf16[160,128]{1,0:T(8,128)(2,1)S(1)}, u32[]{:S(2)}, u32[]{:S(2)}) collective-permute-start(bf16[160,128]{1,0:T(8,128)(2,1)S(1)} %get-tuple-element.23), channel_id=1, source_target_pairs={{0,1},{1,0},{2,3},{3,2},{4,5},{5,4},{6,7},{7,6},{8,9},{9,8},{10,11... | collective-permute-start | bytes 122888 | tf_op jit(solution)/shard_map/ppermute | solution.py:126
  7.4 3.4 %collective-permute-start.1 = (bf16[160,128]{1,0:T(8,128)(2,1)S(1)}, bf16[160,128]{1,0:T(8,128)(2,1)S(1)}, u32[]{:S(2)}, u32[]{:S(2)}) collective-permute-start(bf16[160,128]{1,0:T(8,128)(2,1)S(1)} %get-tuple-element.24), channel_id=1, source_target_pairs={{0,15},{1,2},{2,1},{3,4},{4,3},{5,6},{6,5},{7,8},{8,7},{9,10},{10,... | collective-permute-start | bytes 122888 | tf_op jit(solution)/shard_map/ppermute | solution.py:126
  10.9 10.1 %collective-permute-start.2 = (bf16[1136,128]{1,0:T(8,128)(2,1)S(1)}, bf16[1136,128]{1,0:T(8,128)(2,1)S(1)}, u32[]{:S(2)}, u32[]{:S(2)}) collective-permute-start(bf16[1136,128]{1,0:T(8,128)(2,1)S(1)} %get-tuple-element.25), channel_id=1, source_target_pairs={{0,16},{1,17},{2,18},{3,19},{4,20},{5,21},{6,22},{7,23},{8,24},{9,... | collective-permute-start | bytes 872456 | tf_op jit(solution)/shard_map/ppermute | solution.py:126
  11.0 10.0 %collective-permute-start.3 = (bf16[1136,128]{1,0:T(8,128)(2,1)S(1)}, bf16[1136,128]{1,0:T(8,128)(2,1)S(1)}, u32[]{:S(2)}, u32[]{:S(2)}) collective-permute-start(bf16[1136,128]{1,0:T(8,128)(2,1)S(1)} %get-tuple-element.26), channel_id=1, source_target_pairs={{16,32},{17,33},{18,34},{19,35},{20,36},{21,37},{22,38},{23,39},{2... | collective-permute-start | bytes 872456 | tf_op jit(solution)/shard_map/ppermute | solution.py:126
  20.1 0.9 %copy-start.13 = (bf16[14,128,256]{2,1,0:T(8,128)(2,1)}, bf16[14,128,256]{2,1,0:T(8,128)(2,1)S(1)}, u32[]{:S(2)}) copy-start(bf16[14,128,256]{2,1,0:T(8,128)(2,1)S(1)} %get-tuple-element.37.inner_ref) | copy-start | bytes 2752516
  21.0 2.2 %copy-start.7 = (bf16[1136,128]{1,0:T(8,128)(2,1)}, bf16[1136,128]{1,0:T(8,128)(2,1)S(1)}, u32[]{:S(2)}) copy-start(bf16[1136,128]{1,0:T(8,128)(2,1)S(1)} %collective-permute-done.2.row0_ref) | copy-start | bytes 872452
  21.0 2.2 %copy-start.9 = (bf16[1136,128]{1,0:T(8,128)(2,1)}, bf16[1136,128]{1,0:T(8,128)(2,1)S(1)}, u32[]{:S(2)}) copy-start(bf16[1136,128]{1,0:T(8,128)(2,1)S(1)} %collective-permute-done.3.row1_ref) | copy-start | bytes 872452
  23.2 0.7 copy-start.11
  23.9 9.6 %collective-permute-start.4 = (f32[16,64,256]{2,1,0:T(8,128)S(1)}, f32[16,64,256]{2,1,0:T(8,128)S(1)}, u32[]{:S(2)}, u32[]{:S(2)}) collective-permute-start(f32[16,64,256]{2,1,0:T(8,128)S(1)} %get-tuple-element.31), channel_id=1, source_target_pairs={{0,1},{1,0},{2,3},{3,2},{4,5},{5,4},{6,7},{7,6},{8,9},{9,8},{10,11... | collective-permute-start | bytes 3145736 | tf_op jit(solution)/shard_map/ppermute | solution.py:480
  34.4 39.8 %copy-start.8 = (bf16[1136,128]{1,0:T(8,128)(2,1)S(1)}, bf16[1136,128]{1,0:T(8,128)(2,1)}, u32[]{:S(2)}) copy-start(bf16[1136,128]{1,0:T(8,128)(2,1)} %copy-done.7) | copy-start | bytes 872452
  34.4 39.8 %copy-start.10 = (bf16[1136,128]{1,0:T(8,128)(2,1)S(1)}, bf16[1136,128]{1,0:T(8,128)(2,1)}, u32[]{:S(2)}) copy-start(bf16[1136,128]{1,0:T(8,128)(2,1)} %copy-done.9) | copy-start | bytes 872452
  34.4 39.8 %copy-start.12 = (bf16[4,128,256]{2,1,0:T(8,128)(2,1)S(1)}, bf16[4,128,256]{2,1,0:T(8,128)(2,1)}, u32[]{:S(2)}) copy-start(bf16[4,128,256]{2,1,0:T(8,128)(2,1)} %copy-done.11) | copy-start | bytes 786436
  34.4 39.8 %copy-start.14 = (bf16[14,128,256]{2,1,0:T(8,128)(2,1)S(1)}, bf16[14,128,256]{2,1,0:T(8,128)(2,1)}, u32[]{:S(2)}) copy-start(bf16[14,128,256]{2,1,0:T(8,128)(2,1)} %copy-done.13) | copy-start | bytes 2752516
  34.4 20.2 %all-to-all-start = ((bf16[16,64,256]{2,1,0:T(8,128)(2,1)}), bf16[16,64,256]{2,1,0:T(8,128)(2,1)S(1)}, u32[]{:S(2)}, u32[]{:S(2)}) async-start(bf16[16,64,256]{2,1,0:T(8,128)(2,1)} %add_convert_fusion), calls=%async_computation | async-start | bytes 1048576 | tf_op jit(solution)/shard_map/all_to_all | solution.py:491
  44.4 10.4 %collective-permute-start.5 = (bf16[32,256]{1,0:T(8,128)(2,1)S(1)}, bf16[32,256]{1,0:T(8,128)(2,1)S(1)}, u32[]{:S(2)}, u32[]{:S(2)}) collective-permute-start(bf16[32,256]{1,0:T(8,128)(2,1)S(1)} %get-tuple-element.32), channel_id=1, source_target_pairs={{0,1},{1,0},{2,3},{3,2},{4,5},{5,4},{6,7},{7,6},{8,9},{9,8},{10,11... | collective-permute-start | bytes 49160 | tf_op jit(solution)/shard_map/ppermute | solution.py:126
  44.9 9.8 %collective-permute-start.6 = (bf16[32,256]{1,0:T(8,128)(2,1)S(1)}, bf16[32,256]{1,0:T(8,128)(2,1)S(1)}, u32[]{:S(2)}, u32[]{:S(2)}) collective-permute-start(bf16[32,256]{1,0:T(8,128)(2,1)S(1)} %get-tuple-element.33), channel_id=1, source_target_pairs={{0,15},{1,2},{2,1},{3,4},{4,3},{5,6},{6,5},{7,8},{8,7},{9,10},{10,... | collective-permute-start | bytes 49160 | tf_op jit(solution)/shard_map/ppermute | solution.py:126
  54.7 3.6 %collective-permute-start.7 = (bf16[64,256]{1,0:T(8,128)(2,1)S(1)}, bf16[64,256]{1,0:T(8,128)(2,1)S(1)}, u32[]{:S(2)}, u32[]{:S(2)}) collective-permute-start(bf16[64,256]{1,0:T(8,128)(2,1)S(1)} %convert_reduce_fusion), channel_id=1, source_target_pairs={{0,16},{1,17},{2,18},{3,19},{4,20},{5,21},{6,22},{7,23},{8,24},{9,... | collective-permute-start | bytes 98312 | tf_op jit(solution)/shard_map/ppermute | solution.py:480
  55.4 3.7 %collective-permute-start.8 = (bf16[64,256]{1,0:T(8,128)(2,1)S(1)}, bf16[64,256]{1,0:T(8,128)(2,1)S(1)}, u32[]{:S(2)}, u32[]{:S(2)}) collective-permute-start(bf16[64,256]{1,0:T(8,128)(2,1)S(1)} %convert_reduce_fusion), channel_id=1, source_target_pairs={{0,32},{1,33},{2,34},{3,35},{4,36},{5,37},{6,38},{7,39},{8,40},{9,... | collective-permute-start | bytes 98312 | tf_op jit(solution)/shard_map/ppermute | solution.py:480
  56.3 4.6 %collective-permute-start.9 = (bf16[64,256]{1,0:T(8,128)(2,1)S(1)}, bf16[64,256]{1,0:T(8,128)(2,1)S(1)}, u32[]{:S(2)}, u32[]{:S(2)}) collective-permute-start(bf16[64,256]{1,0:T(8,128)(2,1)S(1)} %convert_reduce_fusion), channel_id=1, source_target_pairs={{0,48},{1,49},{2,50},{3,51},{4,52},{5,53},{6,54},{7,55},{8,56},{9,... | collective-permute-start | bytes 98312 | tf_op jit(solution)/shard_map/ppermute | solution.py:480
  60.9 5.5 %collective-permute-start.10 = (bf16[64,256]{1,0:T(8,128)(2,1)S(1)}, bf16[64,256]{1,0:T(8,128)(2,1)S(1)}, u32[]{:S(2)}, u32[]{:S(2)}) collective-permute-start(bf16[64,256]{1,0:T(8,128)(2,1)S(1)} %add_convert_fusion.2), channel_id=1, source_target_pairs={{0,56},{1,57},{2,58},{3,59},{4,60},{5,61},{6,62},{7,63},{8,48},{9,... | collective-permute-start | bytes 98312 | tf_op jit(solution)/shard_map/ppermute | solution.py:480
  67.2 16.0 %all-to-all-start.1 = ((bf16[16,64,256]{2,1,0:T(8,128)(2,1)}), bf16[16,64,256]{2,1,0:T(8,128)(2,1)}, u32[]{:S(2)}, u32[]{:S(2)}) async-start(bf16[16,64,256]{2,1,0:T(8,128)(2,1)} %broadcast_in_dim.2), calls=%async_computation.1 | async-start | bytes 1048576 | tf_op jit(solution)/shard_map/all_to_all | solution.py:491
  83.3 5.0 %collective-permute-start.11 = (bf16[16,64,256]{2,1,0:T(8,128)(2,1)}, bf16[16,64,256]{2,1,0:T(8,128)(2,1)S(1)}, u32[]{:S(2)}, u32[]{:S(2)}) collective-permute-start(bf16[16,64,256]{2,1,0:T(8,128)(2,1)} %all-to-all-done.1), channel_id=1, source_target_pairs={{0,1},{1,0},{2,3},{3,2},{4,5},{5,4},{6,7},{7,6},{8,9},{9,8},{10,11... | collective-permute-start | bytes 1572872 | tf_op jit(solution)/shard_map/ppermute | solution.py:480

commit v5 on v4

--- a/solution.py
+++ b/solution.py
@@ -12,6 +12,7 @@
 BOTH = ("row", "col")
 SLOTS = 32
 LARGE = pltpu.CompilerParams(vmem_limit_bytes=24 * 1024 * 1024)
+WIDE = pltpu.CompilerParams(vmem_limit_bytes=60 * 1024 * 1024)
 SMALL = pltpu.CompilerParams(vmem_limit_bytes=6 * 1024 * 1024)
 
 
@@ -45,14 +46,22 @@
     return jnp.where(condition, value, other), jnp.where(condition, other, value)
 
 
-def column_kernel(f_ref, c_ref, st_ref, col0_ref, col1_ref):
+def column_kernel(f_ref, c_ref, stencil_ref, col0_ref, col1_ref, strip_ref, st_ref, sems):
     breadth = f_ref.shape[1]
+    copies = [pltpu.make_async_copy(stencil_ref, st_ref, sems.at[4])]
+    for n, base in enumerate((breadth - 16, 0)):
+        for field, ref in enumerate((f_ref, c_ref)):
+            at = 2 * n + field
+            copies.append(pltpu.make_async_copy(ref.at[:, pl.ds(base, 16), :], strip_ref.at[at], sems.at[at]))
+    for copy in copies:
+        copy.start()
+    for copy in copies:
+        copy.wait()
     sides = []
-    for col, first in ((breadth - 1, (1, 5)), (0, (2, 6))):
-        base = 0 if col == 0 else breadth - 16
+    for n, (line_at, first) in enumerate(((15, (1, 5)), (0, (2, 6)))):
         parts = []
-        for ref in (f_ref, c_ref):
-            parts.append(halves(ref[:, base : base + 16, :].astype(F32)[:, col - base, :]).astype(BF16))
+        for field in range(2):
+            parts.append(halves(strip_ref[2 * n + field].astype(F32)[:, line_at, :]).astype(BF16))
         parts += [st_ref[7 * k + slot] for slot in first for k in range(3)]
         sides.append(parts)
     start = 0
@@ -63,9 +72,19 @@
 
 
 def pack_columns(features, cotangent, stencil):
-    shape = jax.ShapeDtypeStruct((10 * features.shape[0], 128), BF16)
+    height, _, channels = features.shape
+    shape = jax.ShapeDtypeStruct((10 * height, 128), BF16)
     return pl.pallas_call(
-        column_kernel, out_shape=[shape] * 2, compiler_params=SMALL, name="pack_columns"
+        column_kernel,
+        out_shape=[shape] * 2,
+        in_specs=[pl.BlockSpec(memory_space=pltpu.HBM)] * 3,
+        scratch_shapes=[
+            pltpu.VMEM((4, height, 16, channels), BF16),
+            pltpu.VMEM(stencil.shape, BF16),
+            pltpu.SemaphoreType.DMA((5,)),
+        ],
+        compiler_params=WIDE,
+        name="pack_columns",
     )(features, cotangent, stencil)
 
 
@@ -343,9 +362,8 @@
     core = lax.axis_index("col") % 2 == 0
     for k in range(4):
         at = slice(4 * k, 4 * k + 4)
-        keep_ref[at], send_ref[at] = choose(
-            core, total_ref[0, at] + second[k], total_ref[1, at] + first[at]
-        )
+        keep_ref[at], send = choose(core, total_ref[0, at] + second[k], total_ref[1, at] + first[at])
+        send_ref[at] = send.astype(BF16)
 
 
 def input_kernel(
@@ -435,7 +453,7 @@
             shape((height + 16, channels), BF16),
             shape((height + 16, channels), BF16),
             shape(totals, F32),
-            shape(totals, F32),
+            shape(totals, BF16),
         ],
         scratch_shapes=[
             pltpu.VMEM((8, breadth, channels), BF16),
@@ -466,7 +484,7 @@
             pltpu.VMEM((height + 16, channels), F32),
             pltpu.VMEM((height + 16, channels), F32),
         ],
-        compiler_params=LARGE,
+        compiler_params=WIDE,
         cost_estimate=pl.CostEstimate(flops=3 * 10**9, bytes_accessed=3 * 10**6, transcendentals=0),
         name="input_gradient",
     )(inner, outer, *gcols, stencil_t, *cols, *rows, w1t)
@@ -507,19 +525,20 @@
     w1t = weights_first.transpose(0, 2, 1).reshape(4 * channels, channels)
     w2t = weights_second.transpose(0, 2, 1).reshape(4 * channels, channels)
 
+    w1t, w2t = lax.optimization_barrier((w1t, w2t))
     cols = both_swaps(*pack_columns(features_in, cotangent, flat), "col")
     rows = both_swaps(*pack_rows(features_in, cotangent, stencil_t, cols), "row")
     inner, *sums = inner_gradients(features_in, cotangent, stencil_t, cols, w1, w2t)
     outer, gcol0, gcol1, keep, send = outer_gradients(
         features_in, cotangent, stencil_t, cols, rows, w1, w2t, sums
     )
-    half = (keep + swap(send, 0, 1)).astype(BF16)
+    half = (keep + swap(send, 0, 1).astype(F32)).astype(BF16)
     gcols = both_swaps(gcol0, gcol1, "col")
     part = plane_trade(half).astype(F32).sum(0)
     part, gcols = lax.optimization_barrier((part, gcols))
     part, other = sum_line(part)
     part = (part.astype(F32) + other.astype(F32)).astype(BF16)
-    part, inner = lax.optimization_barrier((part, inner))
+    part, gcols = lax.optimization_barrier((part, gcols))
     input_grad = input_gradient(inner, outer, gcols, stencil_t, cols, rows, w1t)
     mine = plane_trade(jnp.broadcast_to(part[None], keep.shape))
     mine, input_grad = lax.optimization_barrier((mine, input_grad))

time: 91.4 us -> 88 us (0.963)
  waiting for transfers between devices: 21.6 us -> 18 us
  Pallas kernels: 16.1 us -> 19.7 us
  local copies, waits for them, and re-layouts: 7.34 us -> 4.81 us
  other arithmetic: 3.65 us -> 2.68 us
    unnamed x30 -> x26, local copies, waits for them, and re-layouts: 5 us -> 1.66 us
    pallas_call x1, Pallas kernels: 0.06 us -> 2.02 us  [pack_columns(): pl.pallas_call(column_kernel, out_shape=[shape] * 2, in_specs=[pl.BlockSp...]
    all_to_all x2, waiting for transfers between devices: 11.7 us -> 9.78 us  [plane_trade(): lax.all_to_all(value, BOTH, 0, 0, axis_index_groups=planes, tiled=True)]
    pallas_call x1, Pallas kernels: 5.37 us -> 7.08 us  [input_gradient(): pl.pallas_call(input_kernel, out_shape=jax.ShapeDtypeStruct((height, brea...]
    select_n x1, other arithmetic: 2.63 us -> 1.6 us  [body(): second = jnp.where(even('col'), mine, theirs).reshape(4, channels, channels)]
    ppermute x6, waiting for transfers between devices: 7.84 us -> 6.91 us  [swap(): return lax.ppermute(value, BOTH, pairs)]
  transfers between devices with their start and end apart: 14 -> 14, of which waited for: 8 -> 8; matrix products, arithmetic and copies ran while one was open for 2% -> 3% of each run, Pallas kernels for 15% -> 18%
where the time goes in v5:
time: 88 us; the launch traced here: 87.6 us
  starting transfers between devices  41.5 us (47%)
  Pallas kernels  19.7 us (22%)
  waiting for transfers between devices  18 us (20%)
  local copies, waits for them, and re-layouts  4.81 us (5%)
  other arithmetic  2.68 us (3%)
  between operations  0.91 us (1%)
    ppermute x6, starting transfers between devices, swap(): return lax.ppermute(value, BOTH, pairs)  19.2 us
    all_to_all x2, starting transfers between devices, plane_trade(): lax.all_to_all(value, BOTH, 0, 0, axis_index_groups=planes, tiled=True)  16 us
    all_to_all x2, waiting for transfers between devices, plane_trade(): lax.all_to_all(value, BOTH, 0, 0, axis_index_groups=planes, tiled=True)  9.78 us
    pallas_call x1, Pallas kernels, inner_gradients(): pl.pallas_call(inner_kernel, out_shape=[shape((height - 2, breadth, chann...  8.3 us
    pallas_call x1, Pallas kernels, input_gradient(): pl.pallas_call(input_kernel, out_shape=jax.ShapeDtypeStruct((height, brea...  7.08 us
    ppermute x6, waiting for transfers between devices, swap(): return lax.ppermute(value, BOTH, pairs)  6.91 us
    ppermute x6, starting transfers between devices, pair_swap(): return lax.ppermute(value, BOTH, pairs)  6.34 us
    pallas_call x1, Pallas kernels, outer_gradients(): pl.pallas_call(outer_kernel, out_shape=[shape((4, breadth, channels), BF1...  2.17 us
  transfers between devices with their start and end apart: 14, of which 8 were waited for; matrix products, arithmetic and copies ran while one was open for 3% of the time, Pallas kernels for 18%

profile of v5, /device:TPU:1, one launch (start us, length us, event | category | flops | bytes accessed | tf_op | source)
XLA Modules:
  0.0 87.6 jit_solution(14085742504320798821)
XLA Ops:
  0.6 0.0 copy-start.10
  0.6 0.0 copy-start.3
  0.7 0.0 copy-start
  0.7 0.0 copy-start.1
  0.7 2.0 %pack_columns.1 = (bf16[160,128]{1,0:T(8,128)(2,1)}, bf16[160,128]{1,0:T(8,128)(2,1)}) custom-call(bf16[16,128,256]{2,1,0:T(8,128)(2,1)} %f_ref.7, bf16[16,128,256]{2,1,0:T(8,128)(2,1)} %c_ref.7, bf16[21,16,128]{2,1,0:T(8,128)(2,1)} %bitcast.21), custom_call_target="tpu_custom_call" | custom-call | tf_op jit(solution)/shard_map/pack_columns/pallas_call | solution.py:77
  2.7 3.3 %collective-permute-start = (bf16[160,128]{1,0:T(8,128)(2,1)}, bf16[160,128]{1,0:T(8,128)(2,1)S(1)}, u32[]{:S(2)}, u32[]{:S(2)}) collective-permute-start(bf16[160,128]{1,0:T(8,128)(2,1)} %get-tuple-element.26), channel_id=1, source_target_pairs={{0,1},{1,0},{2,3},{3,2},{4,5},{5,4},{6,7},{7,6},{8,9},{9,8},{10,11... | collective-permute-start | bytes 122888 | tf_op jit(solution)/shard_map/ppermute | solution.py:145
  6.0 0.0 collective-permute-start.1
  6.0 0.0 copy-done.10
  6.1 0.0 copy-done.3
  6.1 1.0 %copy.13 = bf16[4,256,256]{2,1,0:T(8,128)(2,1)} copy(bf16[4,256,256]{1,2,0:T(8,128)(2,1)S(1)} %bitcast.11) | data formatting | bytes 1048576 | tf_op jit(solution)/shard_map/transpose | solution.py:525
  7.1 1.2 %copy.14 = bf16[4,256,256]{2,1,0:T(8,128)(2,1)S(1)} copy(bf16[4,256,256]{1,2,0:T(8,128)(2,1)} %bitcast.18) | data formatting | bytes 1048576 | tf_op jit(solution)/shard_map/transpose | solution.py:526
  8.3 0.0 copy-start.2
  8.4 0.0 collective-permute-done.col0_ref
  8.4 0.0 copy-start.4
  8.4 1.3 %collective-permute-done.1.col1_ref = bf16[160,128]{1,0:T(8,128)(2,1)S(1)} collective-permute-done((bf16[160,128]{1,0:T(8,128)(2,1)}, bf16[160,128]{1,0:T(8,128)(2,1)S(1)}, u32[]{:S(2)}, u32[]{:S(2)}) %collective-permute-start.1) | collective-permute-done | bytes 40992 | tf_op jit(solution)/shard_map/ppermute | solution.py:145
  9.7 0.0 copy-done
  9.7 0.0 copy-done.1
  9.7 0.0 copy-start.5
  9.7 0.1 pack_rows.1
  9.8 0.1 collective-permute-start.2
  9.9 0.7 collective-permute-start.3
  10.6 8.3 %inner_gradients.1 = (bf16[14,128,256]{2,1,0:T(8,128)(2,1)S(1)}, f32[2,16,64,256]{3,2,1,0:T(8,128)S(1)}, f32[16,256]{1,0:T(8,128)S(1)}, f32[16,256]{1,0:T(8,128)S(1)}) custom-call(bf16[16,128,256]{2,1,0:T(8,128)(2,1)S(1)} %copy-done, bf16[16,128,256]{2,1,0:T(8,128)(2,1)S(1)} %copy-done.1, bf16[16,32,128]{2,1,0:T(8,128)(2,1)S(1)} %pad.4.stt_ref, ...), custom_call_target="tpu_custom_call" | custom-call | flops 8999999488 | bytes 9000000 | tf_op jit(solution)/shard_map/inner_gradients/pallas_call | solution.py:422
  18.9 0.0 copy-start.9
  18.9 0.9 %copy-done.9 = bf16[14,128,256]{2,1,0:T(8,128)(2,1)} copy-done((bf16[14,128,256]{2,1,0:T(8,128)(2,1)}, bf16[14,128,256]{2,1,0:T(8,128)(2,1)S(1)}, u32[]{:S(2)}) %copy-start.9) | copy-done | bytes 917528
  19.8 0.0 collective-permute-done.2.row0_ref
  19.8 0.0 collective-permute-done.3.row1_ref
  19.8 0.0 copy-start.7
  19.8 0.0 copy-done.2
  19.8 0.0 copy-done.4
  19.9 0.0 copy-done.5
  19.9 2.2 %outer_gradients.1 = (bf16[4,128,256]{2,1,0:T(8,128)(2,1)S(1)}, bf16[32,256]{1,0:T(8,128)(2,1)S(1)}, bf16[32,256]{1,0:T(8,128)(2,1)S(1)}, f32[16,64,256]{2,1,0:T(8,128)S(1)}, bf16[16,64,256]{2,1,0:T(8,128)(2,1)S(1)}) custom-call(bf16[16,128,256]{2,1,0:T(8,128)(2,1)S(1)} %copy-done, bf16[16,128,256]{2,1,0:T(8,128)(2,1)S(1)} %copy-done.1, ...), custom_call_target="tpu_custom_call" | custom-call | flops 2000000000 | bytes 5000000 | tf_op jit(solution)/shard_map/outer_gradients/pallas_call | solution.py:449
  22.0 0.0 copy-done.6
  22.1 0.0 copy-done.7
  22.1 0.0 copy-start.8
  22.1 0.7 copy-done.8
  22.8 7.8 %collective-permute-start.4 = (bf16[16,64,256]{2,1,0:T(8,128)(2,1)S(1)}, bf16[16,64,256]{2,1,0:T(8,128)(2,1)S(1)}, u32[]{:S(2)}, u32[]{:S(2)}) collective-permute-start(bf16[16,64,256]{2,1,0:T(8,128)(2,1)S(1)} %get-tuple-element.35), channel_id=1, source_target_pairs={{0,1},{1,0},{2,3},{3,2},{4,5},{5,4},{6,7},{7,6},{8,9},{9,8},{10,11... | collective-permute-start | bytes 1572872 | tf_op jit(solution)/shard_map/ppermute | solution.py:498
  30.5 1.5 %collective-permute-done.4 = bf16[16,64,256]{2,1,0:T(8,128)(2,1)S(1)} collective-permute-done((bf16[16,64,256]{2,1,0:T(8,128)(2,1)S(1)}, bf16[16,64,256]{2,1,0:T(8,128)(2,1)S(1)}, u32[]{:S(2)}, u32[]{:S(2)}) %collective-permute-start.4) | collective-permute-done | bytes 524320 | tf_op jit(solution)/shard_map/ppermute | solution.py:498
  32.1 1.0 %add_convert_fusion = bf16[16,64,256]{2,1,0:T(8,128)(2,1)} fusion(f32[16,64,256]{2,1,0:T(8,128)S(1)} %get-tuple-element.34, bf16[16,64,256]{2,1,0:T(8,128)(2,1)S(1)} %collective-permute-done.4), kind=kLoop, calls=%fused_computation.5 | loop fusion | flops 786432 | bytes 2097152 | tf_op jit(solution)/shard_map/convert_element_type | solution.py:535
  33.1 9.3 %all-to-all-start = ((bf16[16,64,256]{2,1,0:T(8,128)(2,1)}), bf16[16,64,256]{2,1,0:T(8,128)(2,1)S(1)}, u32[]{:S(2)}, u32[]{:S(2)}) async-start(bf16[16,64,256]{2,1,0:T(8,128)(2,1)} %add_convert_fusion), calls=%async_computation | async-start | bytes 1048576 | tf_op jit(solution)/shard_map/all_to_all | solution.py:509
  42.3 0.5 collective-permute-start.5
  42.9 1.7 %collective-permute-start.6 = (bf16[32,256]{1,0:T(8,128)(2,1)S(1)}, bf16[32,256]{1,0:T(8,128)(2,1)S(1)}, u32[]{:S(2)}, u32[]{:S(2)}) collective-permute-start(bf16[32,256]{1,0:T(8,128)(2,1)S(1)} %get-tuple-element.37), channel_id=1, source_target_pairs={{0,15},{1,2},{2,1},{3,4},{4,3},{5,6},{6,5},{7,8},{8,7},{9,10},{10,... | collective-permute-start | bytes 49160 | tf_op jit(solution)/shard_map/ppermute | solution.py:145
  44.6 8.0 %all-to-all-done = bf16[16,64,256]{2,1,0:T(8,128)(2,1)S(1)} async-done(((bf16[16,64,256]{2,1,0:T(8,128)(2,1)}), bf16[16,64,256]{2,1,0:T(8,128)(2,1)S(1)}, u32[]{:S(2)}, u32[]{:S(2)}) %all-to-all-start) | async-done | bytes 524320 | tf_op jit(solution)/shard_map/all_to_all | solution.py:509
  52.6 0.1 convert_reduce_fusion
  52.7 0.0 collective-permute-done.5.gcol0_ref
  52.7 0.0 copy-start.11
  52.7 0.0 collective-permute-done.6.gcol1_ref
  52.7 0.0 copy-start.12
  52.7 0.6 collective-permute-start.7
  53.4 1.0 %collective-permute-start.8 = (bf16[64,256]{1,0:T(8,128)(2,1)S(1)}, bf16[64,256]{1,0:T(8,128)(2,1)S(1)}, u32[]{:S(2)}, u32[]{:S(2)}) collective-permute-start(bf16[64,256]{1,0:T(8,128)(2,1)S(1)} %convert_reduce_fusion), channel_id=1, source_target_pairs={{0,32},{1,33},{2,34},{3,35},{4,36},{5,37},{6,38},{7,39},{8,40},{9,... | collective-permute-start | bytes 98312 | tf_op jit(solution)/shard_map/ppermute | solution.py:498
  54.3 2.0 %collective-permute-start.9 = (bf16[64,256]{1,0:T(8,128)(2,1)S(1)}, bf16[64,256]{1,0:T(8,128)(2,1)S(1)}, u32[]{:S(2)}, u32[]{:S(2)}) collective-permute-start(bf16[64,256]{1,0:T(8,128)(2,1)S(1)} %convert_reduce_fusion), channel_id=1, source_target_pairs={{0,48},{1,49},{2,50},{3,51},{4,52},{5,53},{6,54},{7,55},{8,56},{9,... | collective-permute-start | bytes 98312 | tf_op jit(solution)/shard_map/ppermute | solution.py:498
  56.4 0.0 collective-permute-done.7
  56.4 0.7 collective-permute-done.8
  57.0 1.9 %collective-permute-done.9 = bf16[64,256]{1,0:T(8,128)(2,1)S(1)} collective-permute-done((bf16[64,256]{1,0:T(8,128)(2,1)S(1)}, bf16[64,256]{1,0:T(8,128)(2,1)S(1)}, u32[]{:S(2)}, u32[]{:S(2)}) %collective-permute-start.9) | collective-permute-done | bytes 32800 | tf_op jit(solution)/shard_map/ppermute | solution.py:498
  58.9 4.2 %collective-permute-start.10 = (bf16[64,256]{1,0:T(8,128)(2,1)S(1)}, bf16[64,256]{1,0:T(8,128)(2,1)S(1)}, u32[]{:S(2)}, u32[]{:S(2)}) collective-permute-start(bf16[64,256]{1,0:T(8,128)(2,1)S(1)} %add_convert_fusion.2), channel_id=1, source_target_pairs={{0,56},{1,57},{2,58},{3,59},{4,60},{5,61},{6,62},{7,63},{8,48},{9,... | collective-permute-start | bytes 98312 | tf_op jit(solution)/shard_map/ppermute | solution.py:498
  63.1 1.3 %collective-permute-done.10 = bf16[64,256]{1,0:T(8,128)(2,1)S(1)} collective-permute-done((bf16[64,256]{1,0:T(8,128)(2,1)S(1)}, bf16[64,256]{1,0:T(8,128)(2,1)S(1)}, u32[]{:S(2)}, u32[]{:S(2)}) %collective-permute-start.10) | collective-permute-done | bytes 32800 | tf_op jit(solution)/shard_map/ppermute | solution.py:498
  64.4 0.9 broadcast_in_dim.2
  65.3 6.7 %all-to-all-start.1 = ((bf16[16,64,256]{2,1,0:T(8,128)(2,1)}), bf16[16,64,256]{2,1,0:T(8,128)(2,1)S(1)}, u32[]{:S(2)}, u32[]{:S(2)}) async-start(bf16[16,64,256]{2,1,0:T(8,128)(2,1)} %broadcast_in_dim.2), calls=%async_computation.1 | async-start | bytes 1048576 | tf_op jit(solution)/shard_map/all_to_all | solution.py:509
  72.0 0.0 copy-done.11
  72.0 0.0 copy-done.12
  72.0 7.1 %input_gradient.1 = bf16[16,128,256]{2,1,0:T(8,128)(2,1)} custom-call(bf16[14,128,256]{2,1,0:T(8,128)(2,1)} %copy-done.9, bf16[4,128,256]{2,1,0:T(8,128)(2,1)} %copy-done.8, bf16[32,256]{1,0:T(8,128)(2,1)} %copy-done.11, bf16[32,256]{1,0:T(8,128)(2,1)} %copy-done.12, bf16[16,32,128]{2,1,0:T(8,128)(2,1)} %copy-done.2, bf16[160,128]{1,0:T(8,128)(2,1)} %copy-done.4, ...), custom_call_target="tpu_custom_call" | custom-call | flops 3000000000 | bytes 3000000 | tf_op jit(solution)/shard_map/input_gradient/pallas_call | solution.py:475
  79.1 1.7 %all-to-all-done.1 = bf16[16,64,256]{2,1,0:T(8,128)(2,1)S(1)} async-done(((bf16[16,64,256]{2,1,0:T(8,128)(2,1)}), bf16[16,64,256]{2,1,0:T(8,128)(2,1)S(1)}, u32[]{:S(2)}, u32[]{:S(2)}) %all-to-all-start.1) | async-done | bytes 524320 | tf_op jit(solution)/shard_map/all_to_all | solution.py:509
  80.8 3.6 %collective-permute-start.11 = (bf16[16,64,256]{2,1,0:T(8,128)(2,1)S(1)}, bf16[16,64,256]{2,1,0:T(8,128)(2,1)S(1)}, u32[]{:S(2)}, u32[]{:S(2)}) collective-permute-start(bf16[16,64,256]{2,1,0:T(8,128)(2,1)S(1)} %all-to-all-done.1), channel_id=1, source_target_pairs={{0,1},{1,0},{2,3},{3,2},{4,5},{5,4},{6,7},{7,6},{8,9},{9,8},{10,11... | collective-permute-start | bytes 1572872 | tf_op jit(solution)/shard_map/ppermute | solution.py:498
  84.5 1.5 %collective-permute-done.11 = bf16[16,64,256]{2,1,0:T(8,128)(2,1)S(1)} collective-permute-done((bf16[16,64,256]{2,1,0:T(8,128)(2,1)S(1)}, bf16[16,64,256]{2,1,0:T(8,128)(2,1)S(1)}, u32[]{:S(2)}, u32[]{:S(2)}) %collective-permute-start.11) | collective-permute-done | bytes 524320 | tf_op jit(solution)/shard_map/ppermute | solution.py:498
  86.0 1.6 %fusion = (f32[16,64,256]{2,1,0:T(8,128)}, f32[16,64,256]{2,1,0:T(8,128)}) fusion(bf16[16,64,256]{2,1,0:T(8,128)(2,1)S(1)} %all-to-all-done.1, bf16[16,64,256]{2,1,0:T(8,128)(2,1)S(1)} %collective-permute-done.11, pred[]{:T(512)S(6)} %eq.7), kind=kLoop, calls=%fused_computation.1 | loop fusion | flops 1572864 | bytes 3145729 | tf_op jit(solution)/shard_map/jit(_where)/select_n | solution.py:547
  (5 shorter events, 0.1 us)
Async XLA Ops:
  0.6 5.4 %copy-start.10 = (bf16[3,7,16,128]{3,2,1,0:T(8,128)(2,1)S(1)}, bf16[3,7,16,128]{3,2,1,0:T(8,128)(2,1)}, u32[]{:S(2)}) copy-start(bf16[3,7,16,128]{3,2,1,0:T(8,128)(2,1)} %param.6) | copy-start | bytes 258052
  0.6 5.4 %copy-start.3 = (bf16[4,256,256]{2,1,0:T(8,128)(2,1)S(1)}, bf16[4,256,256]{2,1,0:T(8,128)(2,1)}, u32[]{:S(2)}) copy-start(bf16[4,256,256]{2,1,0:T(8,128)(2,1)} %param.7) | copy-start | bytes 1572868
  0.7 9.0 %copy-start = (bf16[16,128,256]{2,1,0:T(8,128)(2,1)S(1)}, bf16[16,128,256]{2,1,0:T(8,128)(2,1)}, u32[]{:S(2)}) copy-start(bf16[16,128,256]{2,1,0:T(8,128)(2,1)} %f_ref.7) | copy-start | bytes 3145732
  0.7 9.0 %copy-start.1 = (bf16[16,128,256]{2,1,0:T(8,128)(2,1)S(1)}, bf16[16,128,256]{2,1,0:T(8,128)(2,1)}, u32[]{:S(2)}) copy-start(bf16[16,128,256]{2,1,0:T(8,128)(2,1)} %c_ref.7) | copy-start | bytes 3145732
  2.7 5.7 %collective-permute-start = (bf16[160,128]{1,0:T(8,128)(2,1)}, bf16[160,128]{1,0:T(8,128)(2,1)S(1)}, u32[]{:S(2)}, u32[]{:S(2)}) collective-permute-start(bf16[160,128]{1,0:T(8,128)(2,1)} %get-tuple-element.26), channel_id=1, source_target_pairs={{0,1},{1,0},{2,3},{3,2},{4,5},{5,4},{6,7},{7,6},{8,9},{9,8},{10,11... | collective-permute-start | bytes 122888 | tf_op jit(solution)/shard_map/ppermute | solution.py:145
  6.0 3.6 %collective-permute-start.1 = (bf16[160,128]{1,0:T(8,128)(2,1)}, bf16[160,128]{1,0:T(8,128)(2,1)S(1)}, u32[]{:S(2)}, u32[]{:S(2)}) collective-permute-start(bf16[160,128]{1,0:T(8,128)(2,1)} %get-tuple-element.27), channel_id=1, source_target_pairs={{0,15},{1,2},{2,1},{3,4},{4,3},{5,6},{6,5},{7,8},{8,7},{9,10},{10,... | collective-permute-start | bytes 122888 | tf_op jit(solution)/shard_map/ppermute | solution.py:145
  8.3 11.5 %copy-start.2 = (bf16[16,32,128]{2,1,0:T(8,128)(2,1)}, bf16[16,32,128]{2,1,0:T(8,128)(2,1)S(1)}, u32[]{:S(2)}) copy-start(bf16[16,32,128]{2,1,0:T(8,128)(2,1)S(1)} %pad.4.stt_ref) | copy-start | bytes 393220
  8.4 11.5 %copy-start.4 = (bf16[160,128]{1,0:T(8,128)(2,1)}, bf16[160,128]{1,0:T(8,128)(2,1)S(1)}, u32[]{:S(2)}) copy-start(bf16[160,128]{1,0:T(8,128)(2,1)S(1)} %collective-permute-done.col0_ref) | copy-start | bytes 122884
  9.7 10.2 %copy-start.5 = (bf16[160,128]{1,0:T(8,128)(2,1)}, bf16[160,128]{1,0:T(8,128)(2,1)S(1)}, u32[]{:S(2)}) copy-start(bf16[160,128]{1,0:T(8,128)(2,1)S(1)} %collective-permute-done.1.col1_ref) | copy-start | bytes 122884
  9.8 10.0 %collective-permute-start.2 = (bf16[1136,128]{1,0:T(8,128)(2,1)S(1)}, bf16[1136,128]{1,0:T(8,128)(2,1)S(1)}, u32[]{:S(2)}, u32[]{:S(2)}) collective-permute-start(bf16[1136,128]{1,0:T(8,128)(2,1)S(1)} %get-tuple-element.28), channel_id=1, source_target_pairs={{0,16},{1,17},{2,18},{3,19},{4,20},{5,21},{6,22},{7,23},{8,24},{9,... | collective-permute-start | bytes 872456 | tf_op jit(solution)/shard_map/ppermute | solution.py:145
  9.9 9.9 %collective-permute-start.3 = (bf16[1136,128]{1,0:T(8,128)(2,1)S(1)}, bf16[1136,128]{1,0:T(8,128)(2,1)S(1)}, u32[]{:S(2)}, u32[]{:S(2)}) collective-permute-start(bf16[1136,128]{1,0:T(8,128)(2,1)S(1)} %get-tuple-element.29), channel_id=1, source_target_pairs={{16,32},{17,33},{18,34},{19,35},{20,36},{21,37},{22,38},{23,39},{2... | collective-permute-start | bytes 872456 | tf_op jit(solution)/shard_map/ppermute | solution.py:145
  18.9 0.9 %copy-start.9 = (bf16[14,128,256]{2,1,0:T(8,128)(2,1)}, bf16[14,128,256]{2,1,0:T(8,128)(2,1)S(1)}, u32[]{:S(2)}) copy-start(bf16[14,128,256]{2,1,0:T(8,128)(2,1)S(1)} %get-tuple-element.42.inner_ref) | copy-start | bytes 2752516
  19.8 2.2 %copy-start.6 = (bf16[1136,128]{1,0:T(8,128)(2,1)}, bf16[1136,128]{1,0:T(8,128)(2,1)S(1)}, u32[]{:S(2)}) copy-start(bf16[1136,128]{1,0:T(8,128)(2,1)S(1)} %collective-permute-done.2.row0_ref) | copy-start | bytes 872452
  19.8 2.2 %copy-start.7 = (bf16[1136,128]{1,0:T(8,128)(2,1)}, bf16[1136,128]{1,0:T(8,128)(2,1)S(1)}, u32[]{:S(2)}) copy-start(bf16[1136,128]{1,0:T(8,128)(2,1)S(1)} %collective-permute-done.3.row1_ref) | copy-start | bytes 872452
  22.1 0.7 copy-start.8
  22.8 9.3 %collective-permute-start.4 = (bf16[16,64,256]{2,1,0:T(8,128)(2,1)S(1)}, bf16[16,64,256]{2,1,0:T(8,128)(2,1)S(1)}, u32[]{:S(2)}, u32[]{:S(2)}) collective-permute-start(bf16[16,64,256]{2,1,0:T(8,128)(2,1)S(1)} %get-tuple-element.35), channel_id=1, source_target_pairs={{0,1},{1,0},{2,3},{3,2},{4,5},{5,4},{6,7},{7,6},{8,9},{9,8},{10,11... | collective-permute-start | bytes 1572872 | tf_op jit(solution)/shard_map/ppermute | solution.py:498
  33.1 19.6 %all-to-all-start = ((bf16[16,64,256]{2,1,0:T(8,128)(2,1)}), bf16[16,64,256]{2,1,0:T(8,128)(2,1)S(1)}, u32[]{:S(2)}, u32[]{:S(2)}) async-start(bf16[16,64,256]{2,1,0:T(8,128)(2,1)} %add_convert_fusion), calls=%async_computation | async-start | bytes 1048576 | tf_op jit(solution)/shard_map/all_to_all | solution.py:509
  42.3 10.4 %collective-permute-start.5 = (bf16[32,256]{1,0:T(8,128)(2,1)S(1)}, bf16[32,256]{1,0:T(8,128)(2,1)S(1)}, u32[]{:S(2)}, u32[]{:S(2)}) collective-permute-start(bf16[32,256]{1,0:T(8,128)(2,1)S(1)} %get-tuple-element.36), channel_id=1, source_target_pairs={{0,1},{1,0},{2,3},{3,2},{4,5},{5,4},{6,7},{7,6},{8,9},{9,8},{10,11... | collective-permute-start | bytes 49160 | tf_op jit(solution)/shard_map/ppermute | solution.py:145
  42.9 9.9 %collective-permute-start.6 = (bf16[32,256]{1,0:T(8,128)(2,1)S(1)}, bf16[32,256]{1,0:T(8,128)(2,1)S(1)}, u32[]{:S(2)}, u32[]{:S(2)}) collective-permute-start(bf16[32,256]{1,0:T(8,128)(2,1)S(1)} %get-tuple-element.37), channel_id=1, source_target_pairs={{0,15},{1,2},{2,1},{3,4},{4,3},{5,6},{6,5},{7,8},{8,7},{9,10},{10,... | collective-permute-start | bytes 49160 | tf_op jit(solution)/shard_map/ppermute | solution.py:145
  52.7 19.3 %copy-start.11 = (bf16[32,256]{1,0:T(8,128)(2,1)}, bf16[32,256]{1,0:T(8,128)(2,1)S(1)}, u32[]{:S(2)}) copy-start(bf16[32,256]{1,0:T(8,128)(2,1)S(1)} %collective-permute-done.5.gcol0_ref) | copy-start | bytes 49156
  52.7 19.3 %copy-start.12 = (bf16[32,256]{1,0:T(8,128)(2,1)}, bf16[32,256]{1,0:T(8,128)(2,1)S(1)}, u32[]{:S(2)}) copy-start(bf16[32,256]{1,0:T(8,128)(2,1)S(1)} %collective-permute-done.6.gcol1_ref) | copy-start | bytes 49156
  52.7 3.6 %collective-permute-start.7 = (bf16[64,256]{1,0:T(8,128)(2,1)S(1)}, bf16[64,256]{1,0:T(8,128)(2,1)S(1)}, u32[]{:S(2)}, u32[]{:S(2)}) collective-permute-start(bf16[64,256]{1,0:T(8,128)(2,1)S(1)} %convert_reduce_fusion), channel_id=1, source_target_pairs={{0,16},{1,17},{2,18},{3,19},{4,20},{5,21},{6,22},{7,23},{8,24},{9,... | collective-permute-start | bytes 98312 | tf_op jit(solution)/shard_map/ppermute | solution.py:498
  53.4 3.7 %collective-permute-start.8 = (bf16[64,256]{1,0:T(8,128)(2,1)S(1)}, bf16[64,256]{1,0:T(8,128)(2,1)S(1)}, u32[]{:S(2)}, u32[]{:S(2)}) collective-permute-start(bf16[64,256]{1,0:T(8,128)(2,1)S(1)} %convert_reduce_fusion), channel_id=1, source_target_pairs={{0,32},{1,33},{2,34},{3,35},{4,36},{5,37},{6,38},{7,39},{8,40},{9,... | collective-permute-start | bytes 98312 | tf_op jit(solution)/shard_map/ppermute | solution.py:498
  54.3 4.6 %collective-permute-start.9 = (bf16[64,256]{1,0:T(8,128)(2,1)S(1)}, bf16[64,256]{1,0:T(8,128)(2,1)S(1)}, u32[]{:S(2)}, u32[]{:S(2)}) collective-permute-start(bf16[64,256]{1,0:T(8,128)(2,1)S(1)} %convert_reduce_fusion), channel_id=1, source_target_pairs={{0,48},{1,49},{2,50},{3,51},{4,52},{5,53},{6,54},{7,55},{8,56},{9,... | collective-permute-start | bytes 98312 | tf_op jit(solution)/shard_map/ppermute | solution.py:498
  58.9 5.5 %collective-permute-start.10 = (bf16[64,256]{1,0:T(8,128)(2,1)S(1)}, bf16[64,256]{1,0:T(8,128)(2,1)S(1)}, u32[]{:S(2)}, u32[]{:S(2)}) collective-permute-start(bf16[64,256]{1,0:T(8,128)(2,1)S(1)} %add_convert_fusion.2), channel_id=1, source_target_pairs={{0,56},{1,57},{2,58},{3,59},{4,60},{5,61},{6,62},{7,63},{8,48},{9,... | collective-permute-start | bytes 98312 | tf_op jit(solution)/shard_map/ppermute | solution.py:498
  65.3 15.5 %all-to-all-start.1 = ((bf16[16,64,256]{2,1,0:T(8,128)(2,1)}), bf16[16,64,256]{2,1,0:T(8,128)(2,1)S(1)}, u32[]{:S(2)}, u32[]{:S(2)}) async-start(bf16[16,64,256]{2,1,0:T(8,128)(2,1)} %broadcast_in_dim.2), calls=%async_computation.1 | async-start | bytes 1048576 | tf_op jit(solution)/shard_map/all_to_all | solution.py:509
  80.8 5.1 %collective-permute-start.11 = (bf16[16,64,256]{2,1,0:T(8,128)(2,1)S(1)}, bf16[16,64,256]{2,1,0:T(8,128)(2,1)S(1)}, u32[]{:S(2)}, u32[]{:S(2)}) collective-permute-start(bf16[16,64,256]{2,1,0:T(8,128)(2,1)S(1)} %all-to-all-done.1), channel_id=1, source_target_pairs={{0,1},{1,0},{2,3},{3,2},{4,5},{5,4},{6,7},{7,6},{8,9},{9,8},{10,11... | collective-permute-start | bytes 1572872 | tf_op jit(solution)/shard_map/ppermute | solution.py:498

commit v6 on v5

--- a/solution.py
+++ b/solution.py
@@ -484,7 +484,7 @@
             pltpu.VMEM((height + 16, channels), F32),
             pltpu.VMEM((height + 16, channels), F32),
         ],
-        compiler_params=WIDE,
+        compiler_params=pltpu.CompilerParams(vmem_limit_bytes=36 * 1024 * 1024),
         cost_estimate=pl.CostEstimate(flops=3 * 10**9, bytes_accessed=3 * 10**6, transcendentals=0),
         name="input_gradient",
     )(inner, outer, *gcols, stencil_t, *cols, *rows, w1t)

time: 88 us -> 88.5 us (level)
  waiting for transfers between devices: 18 us -> 21.1 us
  Pallas kernels: 19.7 us -> 17.9 us
    all_to_all x2, waiting for transfers between devices: 9.78 us -> 12.9 us  [plane_trade(): lax.all_to_all(value, BOTH, 0, 0, axis_index_groups=planes, tiled=True)]
    pallas_call x1, Pallas kernels: 7.08 us -> 5.34 us  [input_gradient(): pl.pallas_call(input_kernel, out_shape=jax.ShapeDtypeStruct((height, brea...]
    ppermute x6, starting transfers between devices: 19.2 us -> 17.8 us  [swap(): return lax.ppermute(value, BOTH, pairs)]
  transfers between devices with their start and end apart: 14 -> 14, of which waited for: 8 -> 8; matrix products, arithmetic and copies ran while one was open for 3% -> 3% of each run, Pallas kernels for 18% -> 15%
where the time goes in v6:
time: 88.5 us; the launch traced here: 88.1 us
  starting transfers between devices  40.7 us (46%)
  waiting for transfers between devices  21.1 us (24%)
  Pallas kernels  17.9 us (20%)
  local copies, waits for them, and re-layouts  4.79 us (5%)
  other arithmetic  2.68 us (3%)
    ppermute x6, starting transfers between devices, swap(): return lax.ppermute(value, BOTH, pairs)  17.8 us
    all_to_all x2, starting transfers between devices, plane_trade(): lax.all_to_all(value, BOTH, 0, 0, axis_index_groups=planes, tiled=True)  16.6 us
    all_to_all x2, waiting for transfers between devices, plane_trade(): lax.all_to_all(value, BOTH, 0, 0, axis_index_groups=planes, tiled=True)  12.9 us
    pallas_call x1, Pallas kernels, inner_gradients(): pl.pallas_call(inner_kernel, out_shape=[shape((height - 2, breadth, chann...  8.31 us
    ppermute x6, waiting for transfers between devices, swap(): return lax.ppermute(value, BOTH, pairs)  6.87 us
    ppermute x6, starting transfers between devices, pair_swap(): return lax.ppermute(value, BOTH, pairs)  6.34 us
    pallas_call x1, Pallas kernels, input_gradient(): pl.pallas_call(input_kernel, out_shape=jax.ShapeDtypeStruct((height, brea...  5.34 us
    pallas_call x1, Pallas kernels, outer_gradients(): pl.pallas_call(outer_kernel, out_shape=[shape((4, breadth, channels), BF1...  2.17 us
  transfers between devices with their start and end apart: 14, of which 8 were waited for; matrix products, arithmetic and copies ran while one was open for 3% of the time, Pallas kernels for 15%

profile of v6, /device:TPU:1, one launch (start us, length us, event | category | flops | bytes accessed | tf_op | source)
XLA Modules:
  0.0 88.1 jit_solution(2071253195361369215)
XLA Ops:
  0.6 0.0 copy-start.12
  0.6 0.0 copy-start.2
  0.7 0.0 copy-start
  0.7 0.0 copy-start.1
  0.7 2.0 %pack_columns.1 = (bf16[160,128]{1,0:T(8,128)(2,1)}, bf16[160,128]{1,0:T(8,128)(2,1)}) custom-call(bf16[16,128,256]{2,1,0:T(8,128)(2,1)} %f_ref.7, bf16[16,128,256]{2,1,0:T(8,128)(2,1)} %c_ref.7, bf16[21,16,128]{2,1,0:T(8,128)(2,1)} %bitcast.21), custom_call_target="tpu_custom_call" | custom-call | tf_op jit(solution)/shard_map/pack_columns/pallas_call | solution.py:77
  2.7 3.3 %collective-permute-start = (bf16[160,128]{1,0:T(8,128)(2,1)}, bf16[160,128]{1,0:T(8,128)(2,1)S(1)}, u32[]{:S(2)}, u32[]{:S(2)}) collective-permute-start(bf16[160,128]{1,0:T(8,128)(2,1)} %get-tuple-element.26), channel_id=1, source_target_pairs={{0,1},{1,0},{2,3},{3,2},{4,5},{5,4},{6,7},{7,6},{8,9},{9,8},{10,11... | collective-permute-start | bytes 122888 | tf_op jit(solution)/shard_map/ppermute | solution.py:145
  6.0 0.0 collective-permute-start.1
  6.0 0.0 copy-done.12
  6.1 0.0 copy-done.2
  6.1 0.2 copy.13
  6.3 2.0 %copy.14 = bf16[4,256,256]{2,1,0:T(8,128)(2,1)} copy(bf16[4,256,256]{1,2,0:T(8,128)(2,1)} %bitcast.19) | data formatting | bytes 1048576 | tf_op jit(solution)/shard_map/transpose | solution.py:526
  8.3 0.0 copy-start.3
  8.3 0.0 collective-permute-done.col0_ref
  8.4 1.3 %collective-permute-done.1.col1_ref = bf16[160,128]{1,0:T(8,128)(2,1)S(1)} collective-permute-done((bf16[160,128]{1,0:T(8,128)(2,1)}, bf16[160,128]{1,0:T(8,128)(2,1)S(1)}, u32[]{:S(2)}, u32[]{:S(2)}) %collective-permute-start.1) | collective-permute-done | bytes 40992 | tf_op jit(solution)/shard_map/ppermute | solution.py:145
  9.7 0.0 copy-done
  9.7 0.0 copy-done.1
  9.7 0.1 pack_rows.1
  9.8 0.1 collective-permute-start.2
  9.9 0.7 collective-permute-start.3
  10.6 0.0 copy-done.3
  10.6 8.3 %inner_gradients.1 = (bf16[14,128,256]{2,1,0:T(8,128)(2,1)S(1)}, f32[2,16,64,256]{3,2,1,0:T(8,128)S(1)}, f32[16,256]{1,0:T(8,128)S(1)}, f32[16,256]{1,0:T(8,128)S(1)}) custom-call(bf16[16,128,256]{2,1,0:T(8,128)(2,1)S(1)} %copy-done, bf16[16,128,256]{2,1,0:T(8,128)(2,1)S(1)} %copy-done.1, bf16[16,32,128]{2,1,0:T(8,128)(2,1)S(1)} %pad.4.stt_ref, ...), custom_call_target="tpu_custom_call" | custom-call | flops 8999999488 | bytes 9000000 | tf_op jit(solution)/shard_map/inner_gradients/pallas_call | solution.py:422
  18.9 0.0 copy-start.10
  18.9 0.9 %copy-done.10 = bf16[14,128,256]{2,1,0:T(8,128)(2,1)} copy-done((bf16[14,128,256]{2,1,0:T(8,128)(2,1)}, bf16[14,128,256]{2,1,0:T(8,128)(2,1)S(1)}, u32[]{:S(2)}) %copy-start.10) | copy-done | bytes 917528
  19.8 0.0 collective-permute-done.2.row0_ref
  19.8 0.0 copy-start.4
  19.8 0.0 collective-permute-done.3.row1_ref
  19.8 0.0 copy-start.6
  19.8 2.2 %outer_gradients.1 = (bf16[4,128,256]{2,1,0:T(8,128)(2,1)S(1)}, bf16[32,256]{1,0:T(8,128)(2,1)S(1)}, bf16[32,256]{1,0:T(8,128)(2,1)S(1)}, f32[16,64,256]{2,1,0:T(8,128)S(1)}, bf16[16,64,256]{2,1,0:T(8,128)(2,1)S(1)}) custom-call(bf16[16,128,256]{2,1,0:T(8,128)(2,1)S(1)} %copy-done, bf16[16,128,256]{2,1,0:T(8,128)(2,1)S(1)} %copy-done.1, ...), custom_call_target="tpu_custom_call" | custom-call | flops 2000000000 | bytes 5000000 | tf_op jit(solution)/shard_map/outer_gradients/pallas_call | solution.py:449
  22.0 0.0 copy-done.4
  22.0 0.0 copy-done.6
  22.0 0.0 copy-start.8
  22.1 0.7 copy-done.8
  22.7 7.7 %collective-permute-start.4 = (bf16[16,64,256]{2,1,0:T(8,128)(2,1)S(1)}, bf16[16,64,256]{2,1,0:T(8,128)(2,1)S(1)}, u32[]{:S(2)}, u32[]{:S(2)}) collective-permute-start(bf16[16,64,256]{2,1,0:T(8,128)(2,1)S(1)} %get-tuple-element.35), channel_id=1, source_target_pairs={{0,1},{1,0},{2,3},{3,2},{4,5},{5,4},{6,7},{7,6},{8,9},{9,8},{10,11... | collective-permute-start | bytes 1572872 | tf_op jit(solution)/shard_map/ppermute | solution.py:498
  30.5 1.5 %collective-permute-done.4 = bf16[16,64,256]{2,1,0:T(8,128)(2,1)S(1)} collective-permute-done((bf16[16,64,256]{2,1,0:T(8,128)(2,1)S(1)}, bf16[16,64,256]{2,1,0:T(8,128)(2,1)S(1)}, u32[]{:S(2)}, u32[]{:S(2)}) %collective-permute-start.4) | collective-permute-done | bytes 524320 | tf_op jit(solution)/shard_map/ppermute | solution.py:498
  32.0 1.0 %add_convert_fusion = bf16[16,64,256]{2,1,0:T(8,128)(2,1)} fusion(f32[16,64,256]{2,1,0:T(8,128)S(1)} %get-tuple-element.34, bf16[16,64,256]{2,1,0:T(8,128)(2,1)S(1)} %collective-permute-done.4), kind=kLoop, calls=%fused_computation.5 | loop fusion | flops 786432 | bytes 2097152 | tf_op jit(solution)/shard_map/convert_element_type | solution.py:535
  33.0 0.0 copy-start.5
  33.0 0.0 copy-start.7
  33.0 0.0 copy-start.9
  33.0 9.5 %all-to-all-start = ((bf16[16,64,256]{2,1,0:T(8,128)(2,1)}), bf16[16,64,256]{2,1,0:T(8,128)(2,1)S(1)}, u32[]{:S(2)}, u32[]{:S(2)}) async-start(bf16[16,64,256]{2,1,0:T(8,128)(2,1)} %add_convert_fusion), calls=%async_computation | async-start | bytes 1048576 | tf_op jit(solution)/shard_map/all_to_all | solution.py:509
  42.5 0.5 collective-permute-start.5
  43.0 1.7 %collective-permute-start.6 = (bf16[32,256]{1,0:T(8,128)(2,1)S(1)}, bf16[32,256]{1,0:T(8,128)(2,1)S(1)}, u32[]{:S(2)}, u32[]{:S(2)}) collective-permute-start(bf16[32,256]{1,0:T(8,128)(2,1)S(1)} %get-tuple-element.37), channel_id=1, source_target_pairs={{0,15},{1,2},{2,1},{3,4},{4,3},{5,6},{6,5},{7,8},{8,7},{9,10},{10,... | collective-permute-start | bytes 49160 | tf_op jit(solution)/shard_map/ppermute | solution.py:145
  44.7 8.0 %all-to-all-done = bf16[16,64,256]{2,1,0:T(8,128)(2,1)S(1)} async-done(((bf16[16,64,256]{2,1,0:T(8,128)(2,1)}), bf16[16,64,256]{2,1,0:T(8,128)(2,1)S(1)}, u32[]{:S(2)}, u32[]{:S(2)}) %all-to-all-start) | async-done | bytes 524320 | tf_op jit(solution)/shard_map/all_to_all | solution.py:509
  52.8 0.1 convert_reduce_fusion
  52.8 0.0 collective-permute-done.5.gcol0_ref
  52.9 0.0 collective-permute-done.6.gcol1_ref
  52.9 0.6 collective-permute-start.7
  53.5 0.9 %collective-permute-start.8 = (bf16[64,256]{1,0:T(8,128)(2,1)S(1)}, bf16[64,256]{1,0:T(8,128)(2,1)S(1)}, u32[]{:S(2)}, u32[]{:S(2)}) collective-permute-start(bf16[64,256]{1,0:T(8,128)(2,1)S(1)} %convert_reduce_fusion), channel_id=1, source_target_pairs={{0,32},{1,33},{2,34},{3,35},{4,36},{5,37},{6,38},{7,39},{8,40},{9,... | collective-permute-start | bytes 98312 | tf_op jit(solution)/shard_map/ppermute | solution.py:498
  54.4 2.1 %collective-permute-start.9 = (bf16[64,256]{1,0:T(8,128)(2,1)S(1)}, bf16[64,256]{1,0:T(8,128)(2,1)S(1)}, u32[]{:S(2)}, u32[]{:S(2)}) collective-permute-start(bf16[64,256]{1,0:T(8,128)(2,1)S(1)} %convert_reduce_fusion), channel_id=1, source_target_pairs={{0,48},{1,49},{2,50},{3,51},{4,52},{5,53},{6,54},{7,55},{8,56},{9,... | collective-permute-start | bytes 98312 | tf_op jit(solution)/shard_map/ppermute | solution.py:498
  56.5 0.0 collective-permute-done.7
  56.5 0.7 collective-permute-done.8
  57.2 1.8 %collective-permute-done.9 = bf16[64,256]{1,0:T(8,128)(2,1)S(1)} collective-permute-done((bf16[64,256]{1,0:T(8,128)(2,1)S(1)}, bf16[64,256]{1,0:T(8,128)(2,1)S(1)}, u32[]{:S(2)}, u32[]{:S(2)}) %collective-permute-start.9) | collective-permute-done | bytes 32800 | tf_op jit(solution)/shard_map/ppermute | solution.py:498
  59.0 4.2 %collective-permute-start.10 = (bf16[64,256]{1,0:T(8,128)(2,1)S(1)}, bf16[64,256]{1,0:T(8,128)(2,1)S(1)}, u32[]{:S(2)}, u32[]{:S(2)}) collective-permute-start(bf16[64,256]{1,0:T(8,128)(2,1)S(1)} %add_convert_fusion.2), channel_id=1, source_target_pairs={{0,56},{1,57},{2,58},{3,59},{4,60},{5,61},{6,62},{7,63},{8,48},{9,... | collective-permute-start | bytes 98312 | tf_op jit(solution)/shard_map/ppermute | solution.py:498
  63.2 1.3 %collective-permute-done.10 = bf16[64,256]{1,0:T(8,128)(2,1)S(1)} collective-permute-done((bf16[64,256]{1,0:T(8,128)(2,1)S(1)}, bf16[64,256]{1,0:T(8,128)(2,1)S(1)}, u32[]{:S(2)}, u32[]{:S(2)}) %collective-permute-start.10) | collective-permute-done | bytes 32800 | tf_op jit(solution)/shard_map/ppermute | solution.py:498
  64.5 0.8 broadcast_in_dim.2
  65.4 7.2 %all-to-all-start.1 = ((bf16[16,64,256]{2,1,0:T(8,128)(2,1)}), bf16[16,64,256]{2,1,0:T(8,128)(2,1)S(1)}, u32[]{:S(2)}, u32[]{:S(2)}) async-start(bf16[16,64,256]{2,1,0:T(8,128)(2,1)} %broadcast_in_dim.2), calls=%async_computation.1 | async-start | bytes 1048576 | tf_op jit(solution)/shard_map/all_to_all | solution.py:509
  72.5 0.0 copy-done.5
  72.5 0.0 copy-done.7
  72.6 0.0 copy-done.9
  72.6 0.0 copy-done.11
  72.6 5.3 %input_gradient.1 = bf16[16,128,256]{2,1,0:T(8,128)(2,1)} custom-call(bf16[14,128,256]{2,1,0:T(8,128)(2,1)S(1)} %copy-done.11, bf16[4,128,256]{2,1,0:T(8,128)(2,1)S(1)} %copy-done.9, bf16[32,256]{1,0:T(8,128)(2,1)S(1)} %collective-permute-done.5.gcol0_ref, bf16[32,256]{1,0:T(8,128)(2,1)S(1)} %collective-permute-done.6.gcol1_ref, ...), custom_call_target="tpu_custom_call" | custom-call | flops 3000000000 | bytes 3000000 | tf_op jit(solution)/shard_map/input_gradient/pallas_call | solution.py:475
  77.9 4.9 %all-to-all-done.1 = bf16[16,64,256]{2,1,0:T(8,128)(2,1)S(1)} async-done(((bf16[16,64,256]{2,1,0:T(8,128)(2,1)}), bf16[16,64,256]{2,1,0:T(8,128)(2,1)S(1)}, u32[]{:S(2)}, u32[]{:S(2)}) %all-to-all-start.1) | async-done | bytes 524320 | tf_op jit(solution)/shard_map/all_to_all | solution.py:509
  82.8 2.2 %collective-permute-start.11 = (bf16[16,64,256]{2,1,0:T(8,128)(2,1)S(1)}, bf16[16,64,256]{2,1,0:T(8,128)(2,1)S(1)}, u32[]{:S(2)}, u32[]{:S(2)}) collective-permute-start(bf16[16,64,256]{2,1,0:T(8,128)(2,1)S(1)} %all-to-all-done.1), channel_id=1, source_target_pairs={{0,1},{1,0},{2,3},{3,2},{4,5},{5,4},{6,7},{7,6},{8,9},{9,8},{10,11... | collective-permute-start | bytes 1572872 | tf_op jit(solution)/shard_map/ppermute | solution.py:498
  85.0 1.5 %collective-permute-done.11 = bf16[16,64,256]{2,1,0:T(8,128)(2,1)S(1)} collective-permute-done((bf16[16,64,256]{2,1,0:T(8,128)(2,1)S(1)}, bf16[16,64,256]{2,1,0:T(8,128)(2,1)S(1)}, u32[]{:S(2)}, u32[]{:S(2)}) %collective-permute-start.11) | collective-permute-done | bytes 524320 | tf_op jit(solution)/shard_map/ppermute | solution.py:498
  86.5 1.6 %fusion = (f32[16,64,256]{2,1,0:T(8,128)}, f32[16,64,256]{2,1,0:T(8,128)}) fusion(bf16[16,64,256]{2,1,0:T(8,128)(2,1)S(1)} %all-to-all-done.1, bf16[16,64,256]{2,1,0:T(8,128)(2,1)S(1)} %collective-permute-done.11, pred[]{:T(512)S(6)} %eq.7), kind=kLoop, calls=%fused_computation.1 | loop fusion | flops 1572864 | bytes 3145729 | tf_op jit(solution)/shard_map/jit(_where)/select_n | solution.py:547
  (5 shorter events, 0.1 us)
Async XLA Ops:
  0.6 5.4 %copy-start.12 = (bf16[3,7,16,128]{3,2,1,0:T(8,128)(2,1)S(1)}, bf16[3,7,16,128]{3,2,1,0:T(8,128)(2,1)}, u32[]{:S(2)}) copy-start(bf16[3,7,16,128]{3,2,1,0:T(8,128)(2,1)} %param.6) | copy-start | bytes 258052
  0.6 5.4 %copy-start.2 = (bf16[4,256,256]{2,1,0:T(8,128)(2,1)S(1)}, bf16[4,256,256]{2,1,0:T(8,128)(2,1)}, u32[]{:S(2)}) copy-start(bf16[4,256,256]{2,1,0:T(8,128)(2,1)} %param.7) | copy-start | bytes 1572868
  0.7 9.0 %copy-start = (bf16[16,128,256]{2,1,0:T(8,128)(2,1)S(1)}, bf16[16,128,256]{2,1,0:T(8,128)(2,1)}, u32[]{:S(2)}) copy-start(bf16[16,128,256]{2,1,0:T(8,128)(2,1)} %f_ref.7) | copy-start | bytes 3145732
  0.7 9.0 %copy-start.1 = (bf16[16,128,256]{2,1,0:T(8,128)(2,1)S(1)}, bf16[16,128,256]{2,1,0:T(8,128)(2,1)}, u32[]{:S(2)}) copy-start(bf16[16,128,256]{2,1,0:T(8,128)(2,1)} %c_ref.7) | copy-start | bytes 3145732
  2.7 5.6 %collective-permute-start = (bf16[160,128]{1,0:T(8,128)(2,1)}, bf16[160,128]{1,0:T(8,128)(2,1)S(1)}, u32[]{:S(2)}, u32[]{:S(2)}) collective-permute-start(bf16[160,128]{1,0:T(8,128)(2,1)} %get-tuple-element.26), channel_id=1, source_target_pairs={{0,1},{1,0},{2,3},{3,2},{4,5},{5,4},{6,7},{7,6},{8,9},{9,8},{10,11... | collective-permute-start | bytes 122888 | tf_op jit(solution)/shard_map/ppermute | solution.py:145
  6.0 3.6 %collective-permute-start.1 = (bf16[160,128]{1,0:T(8,128)(2,1)}, bf16[160,128]{1,0:T(8,128)(2,1)S(1)}, u32[]{:S(2)}, u32[]{:S(2)}) collective-permute-start(bf16[160,128]{1,0:T(8,128)(2,1)} %get-tuple-element.27), channel_id=1, source_target_pairs={{0,15},{1,2},{2,1},{3,4},{4,3},{5,6},{6,5},{7,8},{8,7},{9,10},{10,... | collective-permute-start | bytes 122888 | tf_op jit(solution)/shard_map/ppermute | solution.py:145
  8.3 2.3 %copy-start.3 = (bf16[4,256,256]{2,1,0:T(8,128)(2,1)S(1)}, bf16[4,256,256]{2,1,0:T(8,128)(2,1)}, u32[]{:S(2)}) copy-start(bf16[4,256,256]{2,1,0:T(8,128)(2,1)} %copy.14) | copy-start | bytes 1572868
  9.8 10.0 %collective-permute-start.2 = (bf16[1136,128]{1,0:T(8,128)(2,1)S(1)}, bf16[1136,128]{1,0:T(8,128)(2,1)S(1)}, u32[]{:S(2)}, u32[]{:S(2)}) collective-permute-start(bf16[1136,128]{1,0:T(8,128)(2,1)S(1)} %get-tuple-element.28), channel_id=1, source_target_pairs={{0,16},{1,17},{2,18},{3,19},{4,20},{5,21},{6,22},{7,23},{8,24},{9,... | collective-permute-start | bytes 872456 | tf_op jit(solution)/shard_map/ppermute | solution.py:145
  9.9 9.9 %collective-permute-start.3 = (bf16[1136,128]{1,0:T(8,128)(2,1)S(1)}, bf16[1136,128]{1,0:T(8,128)(2,1)S(1)}, u32[]{:S(2)}, u32[]{:S(2)}) collective-permute-start(bf16[1136,128]{1,0:T(8,128)(2,1)S(1)} %get-tuple-element.29), channel_id=1, source_target_pairs={{16,32},{17,33},{18,34},{19,35},{20,36},{21,37},{22,38},{23,39},{2... | collective-permute-start | bytes 872456 | tf_op jit(solution)/shard_map/ppermute | solution.py:145
  18.9 0.9 %copy-start.10 = (bf16[14,128,256]{2,1,0:T(8,128)(2,1)}, bf16[14,128,256]{2,1,0:T(8,128)(2,1)S(1)}, u32[]{:S(2)}) copy-start(bf16[14,128,256]{2,1,0:T(8,128)(2,1)S(1)} %get-tuple-element.42.inner_ref) | copy-start | bytes 2752516
  19.8 2.2 %copy-start.4 = (bf16[1136,128]{1,0:T(8,128)(2,1)}, bf16[1136,128]{1,0:T(8,128)(2,1)S(1)}, u32[]{:S(2)}) copy-start(bf16[1136,128]{1,0:T(8,128)(2,1)S(1)} %collective-permute-done.2.row0_ref) | copy-start | bytes 872452
  19.8 2.2 %copy-start.6 = (bf16[1136,128]{1,0:T(8,128)(2,1)}, bf16[1136,128]{1,0:T(8,128)(2,1)S(1)}, u32[]{:S(2)}) copy-start(bf16[1136,128]{1,0:T(8,128)(2,1)S(1)} %collective-permute-done.3.row1_ref) | copy-start | bytes 872452
  22.0 0.7 copy-start.8
  22.7 9.3 %collective-permute-start.4 = (bf16[16,64,256]{2,1,0:T(8,128)(2,1)S(1)}, bf16[16,64,256]{2,1,0:T(8,128)(2,1)S(1)}, u32[]{:S(2)}, u32[]{:S(2)}) collective-permute-start(bf16[16,64,256]{2,1,0:T(8,128)(2,1)S(1)} %get-tuple-element.35), channel_id=1, source_target_pairs={{0,1},{1,0},{2,3},{3,2},{4,5},{5,4},{6,7},{7,6},{8,9},{9,8},{10,11... | collective-permute-start | bytes 1572872 | tf_op jit(solution)/shard_map/ppermute | solution.py:498
  33.0 39.5 %copy-start.5 = (bf16[1136,128]{1,0:T(8,128)(2,1)S(1)}, bf16[1136,128]{1,0:T(8,128)(2,1)}, u32[]{:S(2)}) copy-start(bf16[1136,128]{1,0:T(8,128)(2,1)} %copy-done.4) | copy-start | bytes 872452
  33.0 39.5 %copy-start.7 = (bf16[1136,128]{1,0:T(8,128)(2,1)S(1)}, bf16[1136,128]{1,0:T(8,128)(2,1)}, u32[]{:S(2)}) copy-start(bf16[1136,128]{1,0:T(8,128)(2,1)} %copy-done.6) | copy-start | bytes 872452
  33.0 39.6 %copy-start.9 = (bf16[4,128,256]{2,1,0:T(8,128)(2,1)S(1)}, bf16[4,128,256]{2,1,0:T(8,128)(2,1)}, u32[]{:S(2)}) copy-start(bf16[4,128,256]{2,1,0:T(8,128)(2,1)} %copy-done.8) | copy-start | bytes 786436
  33.0 39.6 %copy-start.11 = (bf16[14,128,256]{2,1,0:T(8,128)(2,1)S(1)}, bf16[14,128,256]{2,1,0:T(8,128)(2,1)}, u32[]{:S(2)}) copy-start(bf16[14,128,256]{2,1,0:T(8,128)(2,1)} %copy-done.10) | copy-start | bytes 2752516
  33.0 19.8 %all-to-all-start = ((bf16[16,64,256]{2,1,0:T(8,128)(2,1)}), bf16[16,64,256]{2,1,0:T(8,128)(2,1)S(1)}, u32[]{:S(2)}, u32[]{:S(2)}) async-start(bf16[16,64,256]{2,1,0:T(8,128)(2,1)} %add_convert_fusion), calls=%async_computation | async-start | bytes 1048576 | tf_op jit(solution)/shard_map/all_to_all | solution.py:509
  42.5 10.4 %collective-permute-start.5 = (bf16[32,256]{1,0:T(8,128)(2,1)S(1)}, bf16[32,256]{1,0:T(8,128)(2,1)S(1)}, u32[]{:S(2)}, u32[]{:S(2)}) collective-permute-start(bf16[32,256]{1,0:T(8,128)(2,1)S(1)} %get-tuple-element.36), channel_id=1, source_target_pairs={{0,1},{1,0},{2,3},{3,2},{4,5},{5,4},{6,7},{7,6},{8,9},{9,8},{10,11... | collective-permute-start | bytes 49160 | tf_op jit(solution)/shard_map/ppermute | solution.py:145
  43.0 9.8 %collective-permute-start.6 = (bf16[32,256]{1,0:T(8,128)(2,1)S(1)}, bf16[32,256]{1,0:T(8,128)(2,1)S(1)}, u32[]{:S(2)}, u32[]{:S(2)}) collective-permute-start(bf16[32,256]{1,0:T(8,128)(2,1)S(1)} %get-tuple-element.37), channel_id=1, source_target_pairs={{0,15},{1,2},{2,1},{3,4},{4,3},{5,6},{6,5},{7,8},{8,7},{9,10},{10,... | collective-permute-start | bytes 49160 | tf_op jit(solution)/shard_map/ppermute | solution.py:145
  52.9 3.6 %collective-permute-start.7 = (bf16[64,256]{1,0:T(8,128)(2,1)S(1)}, bf16[64,256]{1,0:T(8,128)(2,1)S(1)}, u32[]{:S(2)}, u32[]{:S(2)}) collective-permute-start(bf16[64,256]{1,0:T(8,128)(2,1)S(1)} %convert_reduce_fusion), channel_id=1, source_target_pairs={{0,16},{1,17},{2,18},{3,19},{4,20},{5,21},{6,22},{7,23},{8,24},{9,... | collective-permute-start | bytes 98312 | tf_op jit(solution)/shard_map/ppermute | solution.py:498
  53.5 3.7 %collective-permute-start.8 = (bf16[64,256]{1,0:T(8,128)(2,1)S(1)}, bf16[64,256]{1,0:T(8,128)(2,1)S(1)}, u32[]{:S(2)}, u32[]{:S(2)}) collective-permute-start(bf16[64,256]{1,0:T(8,128)(2,1)S(1)} %convert_reduce_fusion), channel_id=1, source_target_pairs={{0,32},{1,33},{2,34},{3,35},{4,36},{5,37},{6,38},{7,39},{8,40},{9,... | collective-permute-start | bytes 98312 | tf_op jit(solution)/shard_map/ppermute | solution.py:498
  54.4 4.6 %collective-permute-start.9 = (bf16[64,256]{1,0:T(8,128)(2,1)S(1)}, bf16[64,256]{1,0:T(8,128)(2,1)S(1)}, u32[]{:S(2)}, u32[]{:S(2)}) collective-permute-start(bf16[64,256]{1,0:T(8,128)(2,1)S(1)} %convert_reduce_fusion), channel_id=1, source_target_pairs={{0,48},{1,49},{2,50},{3,51},{4,52},{5,53},{6,54},{7,55},{8,56},{9,... | collective-permute-start | bytes 98312 | tf_op jit(solution)/shard_map/ppermute | solution.py:498
  59.0 5.5 %collective-permute-start.10 = (bf16[64,256]{1,0:T(8,128)(2,1)S(1)}, bf16[64,256]{1,0:T(8,128)(2,1)S(1)}, u32[]{:S(2)}, u32[]{:S(2)}) collective-permute-start(bf16[64,256]{1,0:T(8,128)(2,1)S(1)} %add_convert_fusion.2), channel_id=1, source_target_pairs={{0,56},{1,57},{2,58},{3,59},{4,60},{5,61},{6,62},{7,63},{8,48},{9,... | collective-permute-start | bytes 98312 | tf_op jit(solution)/shard_map/ppermute | solution.py:498
  65.4 17.4 %all-to-all-start.1 = ((bf16[16,64,256]{2,1,0:T(8,128)(2,1)}), bf16[16,64,256]{2,1,0:T(8,128)(2,1)S(1)}, u32[]{:S(2)}, u32[]{:S(2)}) async-start(bf16[16,64,256]{2,1,0:T(8,128)(2,1)} %broadcast_in_dim.2), calls=%async_computation.1 | async-start | bytes 1048576 | tf_op jit(solution)/shard_map/all_to_all | solution.py:509
  82.8 3.7 %collective-permute-start.11 = (bf16[16,64,256]{2,1,0:T(8,128)(2,1)S(1)}, bf16[16,64,256]{2,1,0:T(8,128)(2,1)S(1)}, u32[]{:S(2)}, u32[]{:S(2)}) collective-permute-start(bf16[16,64,256]{2,1,0:T(8,128)(2,1)S(1)} %all-to-all-done.1), channel_id=1, source_target_pairs={{0,1},{1,0},{2,3},{3,2},{4,5},{5,4},{6,7},{7,6},{8,9},{9,8},{10,11... | collective-permute-start | bytes 1572872 | tf_op jit(solution)/shard_map/ppermute | solution.py:498

commit v7 on v6

--- a/solution.py
+++ b/solution.py
@@ -281,7 +281,7 @@
         weights = [rim[at : at + height].astype(F32) for rim in (left, right) for at in (near, far)]
         we_ref[0, k], we_ref[1, k], we_ref[2, k] = beside(*weights)
 
-    @pl.loop(1, height - 1, unroll=7)
+    @pl.loop(1, height - 1, unroll=14)
     def _(r):
         rows = pl.ds(pl.multiple_of((r - 1) * 128, 128), 128)
         ff_ref[rows], tt_ref[rows] = stacks(f_ref, c_ref, stt_ref, we_ref, mask_ref, sides, r)
@@ -516,6 +516,18 @@
     return total, swap(total, 3, 8)
 
 
+def copies_kernel(part_ref, other_ref, out_ref):
+    total = (part_ref[...].astype(F32) + other_ref[...].astype(F32)).astype(BF16)
+    for n in range(out_ref.shape[0]):
+        out_ref[n] = total
+
+
+def sum_copies(part, other, shape):
+    return pl.pallas_call(
+        copies_kernel, out_shape=jax.ShapeDtypeStruct(shape, BF16), compiler_params=SMALL, name="sum_copies"
+    )(part, other)
+
+
 def body(features_in, stencil, weights_first, weights_second, cotangent):
     height, breadth, channels = features_in.shape
     scale = 1.0 / math.sqrt(height * breadth * lax.axis_size("row") * lax.axis_size("col"))
@@ -537,10 +549,9 @@
     part = plane_trade(half).astype(F32).sum(0)
     part, gcols = lax.optimization_barrier((part, gcols))
     part, other = sum_line(part)
-    part = (part.astype(F32) + other.astype(F32)).astype(BF16)
-    part, gcols = lax.optimization_barrier((part, gcols))
+    part, other, gcols = lax.optimization_barrier((part, other, gcols))
     input_grad = input_gradient(inner, outer, gcols, stencil_t, cols, rows, w1t)
-    mine = plane_trade(jnp.broadcast_to(part[None], keep.shape))
+    mine = plane_trade(sum_copies(part, other, keep.shape))
     mine, input_grad = lax.optimization_barrier((mine, input_grad))
     theirs = swap(mine, 0, 1)
     mine, theirs = mine.astype(F32) * scale, theirs.astype(F32) * scale

time: 88.5 us -> 87.5 us (0.989)
    ppermute x6, starting transfers between devices: 17.8 us -> 18.7 us  [swap(): return lax.ppermute(value, BOTH, pairs)]
where the time goes in v7:
time: 87.5 us; the launch traced here: 87.1 us
  starting transfers between devices  40.8 us (47%)
  waiting for transfers between devices  20.3 us (23%)
  Pallas kernels  18.5 us (21%)
  local copies, waits for them, and re-layouts  3.94 us (5%)
  other arithmetic  2.67 us (3%)
    ppermute x6, starting transfers between devices, swap(): return lax.ppermute(value, BOTH, pairs)  18.7 us
    all_to_all x2, starting transfers between devices, plane_trade(): lax.all_to_all(value, BOTH, 0, 0, axis_index_groups=planes, tiled=True)  16 us
    all_to_all x2, waiting for transfers between devices, plane_trade(): lax.all_to_all(value, BOTH, 0, 0, axis_index_groups=planes, tiled=True)  12 us
    pallas_call x1, Pallas kernels, inner_gradients(): pl.pallas_call(inner_kernel, out_shape=[shape((height - 2, breadth, chann...  8 us
    ppermute x6, waiting for transfers between devices, swap(): return lax.ppermute(value, BOTH, pairs)  6.99 us
    ppermute x6, starting transfers between devices, pair_swap(): return lax.ppermute(value, BOTH, pairs)  6.16 us
    pallas_call x1, Pallas kernels, input_gradient(): pl.pallas_call(input_kernel, out_shape=jax.ShapeDtypeStruct((height, brea...  5.34 us
    pallas_call x1, Pallas kernels, outer_gradients(): pl.pallas_call(outer_kernel, out_shape=[shape((4, breadth, channels), BF1...  2.17 us
  transfers between devices with their start and end apart: 14, of which 8 were waited for; matrix products, arithmetic and copies ran while one was open for 3% of the time, Pallas kernels for 15%

profile of v7, /device:TPU:1, one launch (start us, length us, event | category | flops | bytes accessed | tf_op | source)
XLA Modules:
  0.0 87.1 jit_solution(11117184352198555039)
XLA Ops:
  0.6 0.0 copy-start.12
  0.6 0.0 copy-start.2
  0.7 0.0 copy-start
  0.7 0.0 copy-start.1
  0.7 2.0 %pack_columns.1 = (bf16[160,128]{1,0:T(8,128)(2,1)}, bf16[160,128]{1,0:T(8,128)(2,1)}) custom-call(bf16[16,128,256]{2,1,0:T(8,128)(2,1)} %f_ref.7, bf16[16,128,256]{2,1,0:T(8,128)(2,1)} %c_ref.7, bf16[21,16,128]{2,1,0:T(8,128)(2,1)} %bitcast.21), custom_call_target="tpu_custom_call" | custom-call | tf_op jit(solution)/shard_map/pack_columns/pallas_call | solution.py:77
  2.7 3.3 %collective-permute-start = (bf16[160,128]{1,0:T(8,128)(2,1)}, bf16[160,128]{1,0:T(8,128)(2,1)S(1)}, u32[]{:S(2)}, u32[]{:S(2)}) collective-permute-start(bf16[160,128]{1,0:T(8,128)(2,1)} %get-tuple-element.27), channel_id=1, source_target_pairs={{0,1},{1,0},{2,3},{3,2},{4,5},{5,4},{6,7},{7,6},{8,9},{9,8},{10,11... | collective-permute-start | bytes 122888 | tf_op jit(solution)/shard_map/ppermute | solution.py:145
  6.0 0.0 collective-permute-start.1
  6.0 0.0 copy-done.12
  6.1 0.0 copy-done.2
  6.1 0.2 copy.13
  6.3 2.0 %copy.14 = bf16[4,256,256]{2,1,0:T(8,128)(2,1)} copy(bf16[4,256,256]{1,2,0:T(8,128)(2,1)} %bitcast.19) | data formatting | bytes 1048576 | tf_op jit(solution)/shard_map/transpose | solution.py:538
  8.3 0.0 copy-start.3
  8.3 0.0 collective-permute-done.col0_ref
  8.4 1.3 %collective-permute-done.1.col1_ref = bf16[160,128]{1,0:T(8,128)(2,1)S(1)} collective-permute-done((bf16[160,128]{1,0:T(8,128)(2,1)}, bf16[160,128]{1,0:T(8,128)(2,1)S(1)}, u32[]{:S(2)}, u32[]{:S(2)}) %collective-permute-start.1) | collective-permute-done | bytes 40992 | tf_op jit(solution)/shard_map/ppermute | solution.py:145
  9.7 0.0 copy-done
  9.7 0.0 copy-done.1
  9.7 0.1 pack_rows.1
  9.8 0.1 collective-permute-start.2
  9.9 0.7 collective-permute-start.3
  10.6 0.0 copy-done.3
  10.6 8.0 %inner_gradients.1 = (bf16[14,128,256]{2,1,0:T(8,128)(2,1)S(1)}, f32[2,16,64,256]{3,2,1,0:T(8,128)S(1)}, f32[16,256]{1,0:T(8,128)S(1)}, f32[16,256]{1,0:T(8,128)S(1)}) custom-call(bf16[16,128,256]{2,1,0:T(8,128)(2,1)S(1)} %copy-done, bf16[16,128,256]{2,1,0:T(8,128)(2,1)S(1)} %copy-done.1, bf16[16,32,128]{2,1,0:T(8,128)(2,1)S(1)} %pad.4.stt_ref, ...), custom_call_target="tpu_custom_call" | custom-call | flops 8999999488 | bytes 9000000 | tf_op jit(solution)/shard_map/inner_gradients/pallas_call | solution.py:422
  18.6 0.0 copy-start.10
  18.6 0.9 %copy-done.10 = bf16[14,128,256]{2,1,0:T(8,128)(2,1)} copy-done((bf16[14,128,256]{2,1,0:T(8,128)(2,1)}, bf16[14,128,256]{2,1,0:T(8,128)(2,1)S(1)}, u32[]{:S(2)}) %copy-start.10) | copy-done | bytes 917528
  19.5 0.0 collective-permute-done.2.row0_ref
  19.5 0.0 copy-start.4
  19.5 0.0 collective-permute-done.3.row1_ref
  19.5 0.0 copy-start.6
  19.5 2.2 %outer_gradients.1 = (bf16[4,128,256]{2,1,0:T(8,128)(2,1)S(1)}, bf16[32,256]{1,0:T(8,128)(2,1)S(1)}, bf16[32,256]{1,0:T(8,128)(2,1)S(1)}, f32[16,64,256]{2,1,0:T(8,128)S(1)}, bf16[16,64,256]{2,1,0:T(8,128)(2,1)S(1)}) custom-call(bf16[16,128,256]{2,1,0:T(8,128)(2,1)S(1)} %copy-done, bf16[16,128,256]{2,1,0:T(8,128)(2,1)S(1)} %copy-done.1, ...), custom_call_target="tpu_custom_call" | custom-call | flops 2000000000 | bytes 5000000 | tf_op jit(solution)/shard_map/outer_gradients/pallas_call | solution.py:449
  21.7 0.0 copy-done.4
  21.7 0.0 copy-done.6
  21.7 0.0 copy-start.8
  21.8 0.7 copy-done.8
  22.4 7.7 %collective-permute-start.4 = (bf16[16,64,256]{2,1,0:T(8,128)(2,1)S(1)}, bf16[16,64,256]{2,1,0:T(8,128)(2,1)S(1)}, u32[]{:S(2)}, u32[]{:S(2)}) collective-permute-start(bf16[16,64,256]{2,1,0:T(8,128)(2,1)S(1)} %get-tuple-element.36), channel_id=1, source_target_pairs={{0,1},{1,0},{2,3},{3,2},{4,5},{5,4},{6,7},{7,6},{8,9},{9,8},{10,11... | collective-permute-start | bytes 1572872 | tf_op jit(solution)/shard_map/ppermute | solution.py:498
  30.2 1.5 %collective-permute-done.4 = bf16[16,64,256]{2,1,0:T(8,128)(2,1)S(1)} collective-permute-done((bf16[16,64,256]{2,1,0:T(8,128)(2,1)S(1)}, bf16[16,64,256]{2,1,0:T(8,128)(2,1)S(1)}, u32[]{:S(2)}, u32[]{:S(2)}) %collective-permute-start.4) | collective-permute-done | bytes 524320 | tf_op jit(solution)/shard_map/ppermute | solution.py:498
  31.7 1.0 %add_convert_fusion = bf16[16,64,256]{2,1,0:T(8,128)(2,1)} fusion(f32[16,64,256]{2,1,0:T(8,128)S(1)} %get-tuple-element.35, bf16[16,64,256]{2,1,0:T(8,128)(2,1)S(1)} %collective-permute-done.4), kind=kLoop, calls=%fused_computation.5 | loop fusion | flops 786432 | bytes 2097152 | tf_op jit(solution)/shard_map/convert_element_type | solution.py:547
  32.7 0.0 copy-start.5
  32.7 0.0 copy-start.7
  32.7 0.0 copy-start.9
  32.7 9.5 %all-to-all-start = ((bf16[16,64,256]{2,1,0:T(8,128)(2,1)}), bf16[16,64,256]{2,1,0:T(8,128)(2,1)S(1)}, u32[]{:S(2)}, u32[]{:S(2)}) async-start(bf16[16,64,256]{2,1,0:T(8,128)(2,1)} %add_convert_fusion), calls=%async_computation | async-start | bytes 1048576 | tf_op jit(solution)/shard_map/all_to_all | solution.py:509
  42.2 0.5 collective-permute-start.5
  42.7 1.5 %collective-permute-start.6 = (bf16[32,256]{1,0:T(8,128)(2,1)S(1)}, bf16[32,256]{1,0:T(8,128)(2,1)S(1)}, u32[]{:S(2)}, u32[]{:S(2)}) collective-permute-start(bf16[32,256]{1,0:T(8,128)(2,1)S(1)} %get-tuple-element.38), channel_id=1, source_target_pairs={{0,15},{1,2},{2,1},{3,4},{4,3},{5,6},{6,5},{7,8},{8,7},{9,10},{10,... | collective-permute-start | bytes 49160 | tf_op jit(solution)/shard_map/ppermute | solution.py:145
  44.2 8.2 %all-to-all-done = bf16[16,64,256]{2,1,0:T(8,128)(2,1)S(1)} async-done(((bf16[16,64,256]{2,1,0:T(8,128)(2,1)}), bf16[16,64,256]{2,1,0:T(8,128)(2,1)S(1)}, u32[]{:S(2)}, u32[]{:S(2)}) %all-to-all-start) | async-done | bytes 524320 | tf_op jit(solution)/shard_map/all_to_all | solution.py:509
  52.5 0.1 convert_reduce_fusion
  52.5 0.0 collective-permute-done.5.gcol0_ref
  52.6 0.0 collective-permute-done.6.gcol1_ref
  52.6 0.6 collective-permute-start.7
  53.2 0.9 %collective-permute-start.8 = (bf16[64,256]{1,0:T(8,128)(2,1)S(1)}, bf16[64,256]{1,0:T(8,128)(2,1)S(1)}, u32[]{:S(2)}, u32[]{:S(2)}) collective-permute-start(bf16[64,256]{1,0:T(8,128)(2,1)S(1)} %convert_reduce_fusion), channel_id=1, source_target_pairs={{0,32},{1,33},{2,34},{3,35},{4,36},{5,37},{6,38},{7,39},{8,40},{9,... | collective-permute-start | bytes 98312 | tf_op jit(solution)/shard_map/ppermute | solution.py:498
  54.1 2.1 %collective-permute-start.9 = (bf16[64,256]{1,0:T(8,128)(2,1)S(1)}, bf16[64,256]{1,0:T(8,128)(2,1)S(1)}, u32[]{:S(2)}, u32[]{:S(2)}) collective-permute-start(bf16[64,256]{1,0:T(8,128)(2,1)S(1)} %convert_reduce_fusion), channel_id=1, source_target_pairs={{0,48},{1,49},{2,50},{3,51},{4,52},{5,53},{6,54},{7,55},{8,56},{9,... | collective-permute-start | bytes 98312 | tf_op jit(solution)/shard_map/ppermute | solution.py:498
  56.2 0.0 collective-permute-done.7
  56.2 0.7 collective-permute-done.8
  56.9 2.0 %collective-permute-done.9 = bf16[64,256]{1,0:T(8,128)(2,1)S(1)} collective-permute-done((bf16[64,256]{1,0:T(8,128)(2,1)S(1)}, bf16[64,256]{1,0:T(8,128)(2,1)S(1)}, u32[]{:S(2)}, u32[]{:S(2)}) %collective-permute-start.9) | collective-permute-done | bytes 32800 | tf_op jit(solution)/shard_map/ppermute | solution.py:498
  58.8 4.1 %collective-permute-start.10 = (bf16[64,256]{1,0:T(8,128)(2,1)S(1)}, bf16[64,256]{1,0:T(8,128)(2,1)S(1)}, u32[]{:S(2)}, u32[]{:S(2)}) collective-permute-start(bf16[64,256]{1,0:T(8,128)(2,1)S(1)} %add_convert_fusion.1.part_ref), channel_id=1, source_target_pairs={{0,56},{1,57},{2,58},{3,59},{4,60},{5,61},{6,62},{7,63},{8,48},{9,... | collective-permute-start | bytes 98312 | tf_op jit(solution)/shard_map/ppermute | solution.py:498
  62.9 1.3 %collective-permute-done.10.other_ref = bf16[64,256]{1,0:T(8,128)(2,1)S(1)} collective-permute-done((bf16[64,256]{1,0:T(8,128)(2,1)S(1)}, bf16[64,256]{1,0:T(8,128)(2,1)S(1)}, u32[]{:S(2)}, u32[]{:S(2)}) %collective-permute-start.10) | collective-permute-done | bytes 32800 | tf_op jit(solution)/shard_map/ppermute | solution.py:498
  64.2 0.8 sum_copies.1
  65.1 6.5 %all-to-all-start.1 = ((bf16[16,64,256]{2,1,0:T(8,128)(2,1)}), bf16[16,64,256]{2,1,0:T(8,128)(2,1)S(1)}, u32[]{:S(2)}, u32[]{:S(2)}) async-start(bf16[16,64,256]{2,1,0:T(8,128)(2,1)} %sum_copies.1), calls=%async_computation.1 | async-start | bytes 1048576 | tf_op jit(solution)/shard_map/all_to_all | solution.py:509
  71.5 0.0 copy-done.5
  71.5 0.0 copy-done.7
  71.6 0.0 copy-done.9
  71.6 0.0 copy-done.11
  71.6 5.3 %input_gradient.1 = bf16[16,128,256]{2,1,0:T(8,128)(2,1)} custom-call(bf16[14,128,256]{2,1,0:T(8,128)(2,1)S(1)} %copy-done.11, bf16[4,128,256]{2,1,0:T(8,128)(2,1)S(1)} %copy-done.9, bf16[32,256]{1,0:T(8,128)(2,1)S(1)} %collective-permute-done.5.gcol0_ref, bf16[32,256]{1,0:T(8,128)(2,1)S(1)} %collective-permute-done.6.gcol1_ref, ...), custom_call_target="tpu_custom_call" | custom-call | flops 3000000000 | bytes 3000000 | tf_op jit(solution)/shard_map/input_gradient/pallas_call | solution.py:475
  76.9 3.8 %all-to-all-done.1 = bf16[16,64,256]{2,1,0:T(8,128)(2,1)S(1)} async-done(((bf16[16,64,256]{2,1,0:T(8,128)(2,1)}), bf16[16,64,256]{2,1,0:T(8,128)(2,1)S(1)}, u32[]{:S(2)}, u32[]{:S(2)}) %all-to-all-start.1) | async-done | bytes 524320 | tf_op jit(solution)/shard_map/all_to_all | solution.py:509
  80.7 3.3 %collective-permute-start.11 = (bf16[16,64,256]{2,1,0:T(8,128)(2,1)S(1)}, bf16[16,64,256]{2,1,0:T(8,128)(2,1)S(1)}, u32[]{:S(2)}, u32[]{:S(2)}) collective-permute-start(bf16[16,64,256]{2,1,0:T(8,128)(2,1)S(1)} %all-to-all-done.1), channel_id=1, source_target_pairs={{0,1},{1,0},{2,3},{3,2},{4,5},{5,4},{6,7},{7,6},{8,9},{9,8},{10,11... | collective-permute-start | bytes 1572872 | tf_op jit(solution)/shard_map/ppermute | solution.py:498
  84.0 1.5 %collective-permute-done.11 = bf16[16,64,256]{2,1,0:T(8,128)(2,1)S(1)} collective-permute-done((bf16[16,64,256]{2,1,0:T(8,128)(2,1)S(1)}, bf16[16,64,256]{2,1,0:T(8,128)(2,1)S(1)}, u32[]{:S(2)}, u32[]{:S(2)}) %collective-permute-start.11) | collective-permute-done | bytes 524320 | tf_op jit(solution)/shard_map/ppermute | solution.py:498
  85.5 1.6 %fusion = (f32[16,64,256]{2,1,0:T(8,128)}, f32[16,64,256]{2,1,0:T(8,128)}) fusion(bf16[16,64,256]{2,1,0:T(8,128)(2,1)S(1)} %all-to-all-done.1, bf16[16,64,256]{2,1,0:T(8,128)(2,1)S(1)} %collective-permute-done.11, pred[]{:T(512)S(6)} %eq.7), kind=kLoop, calls=%fused_computation.1 | loop fusion | flops 1572864 | bytes 3145729 | tf_op jit(solution)/shard_map/jit(_where)/select_n | solution.py:558
  (4 shorter events, 0.1 us)
Async XLA Ops:
  0.6 5.4 %copy-start.12 = (bf16[3,7,16,128]{3,2,1,0:T(8,128)(2,1)S(1)}, bf16[3,7,16,128]{3,2,1,0:T(8,128)(2,1)}, u32[]{:S(2)}) copy-start(bf16[3,7,16,128]{3,2,1,0:T(8,128)(2,1)} %param.6) | copy-start | bytes 258052
  0.6 5.4 %copy-start.2 = (bf16[4,256,256]{2,1,0:T(8,128)(2,1)S(1)}, bf16[4,256,256]{2,1,0:T(8,128)(2,1)}, u32[]{:S(2)}) copy-start(bf16[4,256,256]{2,1,0:T(8,128)(2,1)} %param.7) | copy-start | bytes 1572868
  0.7 9.0 %copy-start = (bf16[16,128,256]{2,1,0:T(8,128)(2,1)S(1)}, bf16[16,128,256]{2,1,0:T(8,128)(2,1)}, u32[]{:S(2)}) copy-start(bf16[16,128,256]{2,1,0:T(8,128)(2,1)} %f_ref.7) | copy-start | bytes 3145732
  0.7 9.0 %copy-start.1 = (bf16[16,128,256]{2,1,0:T(8,128)(2,1)S(1)}, bf16[16,128,256]{2,1,0:T(8,128)(2,1)}, u32[]{:S(2)}) copy-start(bf16[16,128,256]{2,1,0:T(8,128)(2,1)} %c_ref.7) | copy-start | bytes 3145732
  2.7 5.6 %collective-permute-start = (bf16[160,128]{1,0:T(8,128)(2,1)}, bf16[160,128]{1,0:T(8,128)(2,1)S(1)}, u32[]{:S(2)}, u32[]{:S(2)}) collective-permute-start(bf16[160,128]{1,0:T(8,128)(2,1)} %get-tuple-element.27), channel_id=1, source_target_pairs={{0,1},{1,0},{2,3},{3,2},{4,5},{5,4},{6,7},{7,6},{8,9},{9,8},{10,11... | collective-permute-start | bytes 122888 | tf_op jit(solution)/shard_map/ppermute | solution.py:145
  6.0 3.6 %collective-permute-start.1 = (bf16[160,128]{1,0:T(8,128)(2,1)}, bf16[160,128]{1,0:T(8,128)(2,1)S(1)}, u32[]{:S(2)}, u32[]{:S(2)}) collective-permute-start(bf16[160,128]{1,0:T(8,128)(2,1)} %get-tuple-element.28), channel_id=1, source_target_pairs={{0,15},{1,2},{2,1},{3,4},{4,3},{5,6},{6,5},{7,8},{8,7},{9,10},{10,... | collective-permute-start | bytes 122888 | tf_op jit(solution)/shard_map/ppermute | solution.py:145
  8.3 2.3 %copy-start.3 = (bf16[4,256,256]{2,1,0:T(8,128)(2,1)S(1)}, bf16[4,256,256]{2,1,0:T(8,128)(2,1)}, u32[]{:S(2)}) copy-start(bf16[4,256,256]{2,1,0:T(8,128)(2,1)} %copy.14) | copy-start | bytes 1572868
  9.8 9.7 %collective-permute-start.2 = (bf16[1136,128]{1,0:T(8,128)(2,1)S(1)}, bf16[1136,128]{1,0:T(8,128)(2,1)S(1)}, u32[]{:S(2)}, u32[]{:S(2)}) collective-permute-start(bf16[1136,128]{1,0:T(8,128)(2,1)S(1)} %get-tuple-element.29), channel_id=1, source_target_pairs={{0,16},{1,17},{2,18},{3,19},{4,20},{5,21},{6,22},{7,23},{8,24},{9,... | collective-permute-start | bytes 872456 | tf_op jit(solution)/shard_map/ppermute | solution.py:145
  9.9 9.6 %collective-permute-start.3 = (bf16[1136,128]{1,0:T(8,128)(2,1)S(1)}, bf16[1136,128]{1,0:T(8,128)(2,1)S(1)}, u32[]{:S(2)}, u32[]{:S(2)}) collective-permute-start(bf16[1136,128]{1,0:T(8,128)(2,1)S(1)} %get-tuple-element.30), channel_id=1, source_target_pairs={{16,32},{17,33},{18,34},{19,35},{20,36},{21,37},{22,38},{23,39},{2... | collective-permute-start | bytes 872456 | tf_op jit(solution)/shard_map/ppermute | solution.py:145
  18.6 0.9 %copy-start.10 = (bf16[14,128,256]{2,1,0:T(8,128)(2,1)}, bf16[14,128,256]{2,1,0:T(8,128)(2,1)S(1)}, u32[]{:S(2)}) copy-start(bf16[14,128,256]{2,1,0:T(8,128)(2,1)S(1)} %get-tuple-element.44.inner_ref) | copy-start | bytes 2752516
  19.5 2.2 %copy-start.4 = (bf16[1136,128]{1,0:T(8,128)(2,1)}, bf16[1136,128]{1,0:T(8,128)(2,1)S(1)}, u32[]{:S(2)}) copy-start(bf16[1136,128]{1,0:T(8,128)(2,1)S(1)} %collective-permute-done.2.row0_ref) | copy-start | bytes 872452
  19.5 2.2 %copy-start.6 = (bf16[1136,128]{1,0:T(8,128)(2,1)}, bf16[1136,128]{1,0:T(8,128)(2,1)S(1)}, u32[]{:S(2)}) copy-start(bf16[1136,128]{1,0:T(8,128)(2,1)S(1)} %collective-permute-done.3.row1_ref) | copy-start | bytes 872452
  21.7 0.7 copy-start.8
  22.4 9.3 %collective-permute-start.4 = (bf16[16,64,256]{2,1,0:T(8,128)(2,1)S(1)}, bf16[16,64,256]{2,1,0:T(8,128)(2,1)S(1)}, u32[]{:S(2)}, u32[]{:S(2)}) collective-permute-start(bf16[16,64,256]{2,1,0:T(8,128)(2,1)S(1)} %get-tuple-element.36), channel_id=1, source_target_pairs={{0,1},{1,0},{2,3},{3,2},{4,5},{5,4},{6,7},{7,6},{8,9},{9,8},{10,11... | collective-permute-start | bytes 1572872 | tf_op jit(solution)/shard_map/ppermute | solution.py:498
  32.7 38.8 %copy-start.5 = (bf16[1136,128]{1,0:T(8,128)(2,1)S(1)}, bf16[1136,128]{1,0:T(8,128)(2,1)}, u32[]{:S(2)}) copy-start(bf16[1136,128]{1,0:T(8,128)(2,1)} %copy-done.4) | copy-start | bytes 872452
  32.7 38.9 %copy-start.7 = (bf16[1136,128]{1,0:T(8,128)(2,1)S(1)}, bf16[1136,128]{1,0:T(8,128)(2,1)}, u32[]{:S(2)}) copy-start(bf16[1136,128]{1,0:T(8,128)(2,1)} %copy-done.6) | copy-start | bytes 872452
  32.7 38.9 %copy-start.9 = (bf16[4,128,256]{2,1,0:T(8,128)(2,1)S(1)}, bf16[4,128,256]{2,1,0:T(8,128)(2,1)}, u32[]{:S(2)}) copy-start(bf16[4,128,256]{2,1,0:T(8,128)(2,1)} %copy-done.8) | copy-start | bytes 786436
  32.7 38.9 %copy-start.11 = (bf16[14,128,256]{2,1,0:T(8,128)(2,1)S(1)}, bf16[14,128,256]{2,1,0:T(8,128)(2,1)}, u32[]{:S(2)}) copy-start(bf16[14,128,256]{2,1,0:T(8,128)(2,1)} %copy-done.10) | copy-start | bytes 2752516
  32.7 19.8 %all-to-all-start = ((bf16[16,64,256]{2,1,0:T(8,128)(2,1)}), bf16[16,64,256]{2,1,0:T(8,128)(2,1)S(1)}, u32[]{:S(2)}, u32[]{:S(2)}) async-start(bf16[16,64,256]{2,1,0:T(8,128)(2,1)} %add_convert_fusion), calls=%async_computation | async-start | bytes 1048576 | tf_op jit(solution)/shard_map/all_to_all | solution.py:509
  42.2 10.4 %collective-permute-start.5 = (bf16[32,256]{1,0:T(8,128)(2,1)S(1)}, bf16[32,256]{1,0:T(8,128)(2,1)S(1)}, u32[]{:S(2)}, u32[]{:S(2)}) collective-permute-start(bf16[32,256]{1,0:T(8,128)(2,1)S(1)} %get-tuple-element.37), channel_id=1, source_target_pairs={{0,1},{1,0},{2,3},{3,2},{4,5},{5,4},{6,7},{7,6},{8,9},{9,8},{10,11... | collective-permute-start | bytes 49160 | tf_op jit(solution)/shard_map/ppermute | solution.py:145
  42.7 9.8 %collective-permute-start.6 = (bf16[32,256]{1,0:T(8,128)(2,1)S(1)}, bf16[32,256]{1,0:T(8,128)(2,1)S(1)}, u32[]{:S(2)}, u32[]{:S(2)}) collective-permute-start(bf16[32,256]{1,0:T(8,128)(2,1)S(1)} %get-tuple-element.38), channel_id=1, source_target_pairs={{0,15},{1,2},{2,1},{3,4},{4,3},{5,6},{6,5},{7,8},{8,7},{9,10},{10,... | collective-permute-start | bytes 49160 | tf_op jit(solution)/shard_map/ppermute | solution.py:145
  52.6 3.6 %collective-permute-start.7 = (bf16[64,256]{1,0:T(8,128)(2,1)S(1)}, bf16[64,256]{1,0:T(8,128)(2,1)S(1)}, u32[]{:S(2)}, u32[]{:S(2)}) collective-permute-start(bf16[64,256]{1,0:T(8,128)(2,1)S(1)} %convert_reduce_fusion), channel_id=1, source_target_pairs={{0,16},{1,17},{2,18},{3,19},{4,20},{5,21},{6,22},{7,23},{8,24},{9,... | collective-permute-start | bytes 98312 | tf_op jit(solution)/shard_map/ppermute | solution.py:498
  53.2 3.7 %collective-permute-start.8 = (bf16[64,256]{1,0:T(8,128)(2,1)S(1)}, bf16[64,256]{1,0:T(8,128)(2,1)S(1)}, u32[]{:S(2)}, u32[]{:S(2)}) collective-permute-start(bf16[64,256]{1,0:T(8,128)(2,1)S(1)} %convert_reduce_fusion), channel_id=1, source_target_pairs={{0,32},{1,33},{2,34},{3,35},{4,36},{5,37},{6,38},{7,39},{8,40},{9,... | collective-permute-start | bytes 98312 | tf_op jit(solution)/shard_map/ppermute | solution.py:498
  54.1 4.7 %collective-permute-start.9 = (bf16[64,256]{1,0:T(8,128)(2,1)S(1)}, bf16[64,256]{1,0:T(8,128)(2,1)S(1)}, u32[]{:S(2)}, u32[]{:S(2)}) collective-permute-start(bf16[64,256]{1,0:T(8,128)(2,1)S(1)} %convert_reduce_fusion), channel_id=1, source_target_pairs={{0,48},{1,49},{2,50},{3,51},{4,52},{5,53},{6,54},{7,55},{8,56},{9,... | collective-permute-start | bytes 98312 | tf_op jit(solution)/shard_map/ppermute | solution.py:498
  58.8 5.4 %collective-permute-start.10 = (bf16[64,256]{1,0:T(8,128)(2,1)S(1)}, bf16[64,256]{1,0:T(8,128)(2,1)S(1)}, u32[]{:S(2)}, u32[]{:S(2)}) collective-permute-start(bf16[64,256]{1,0:T(8,128)(2,1)S(1)} %add_convert_fusion.1.part_ref), channel_id=1, source_target_pairs={{0,56},{1,57},{2,58},{3,59},{4,60},{5,61},{6,62},{7,63},{8,48},{9,... | collective-permute-start | bytes 98312 | tf_op jit(solution)/shard_map/ppermute | solution.py:498
  65.1 15.7 %all-to-all-start.1 = ((bf16[16,64,256]{2,1,0:T(8,128)(2,1)}), bf16[16,64,256]{2,1,0:T(8,128)(2,1)S(1)}, u32[]{:S(2)}, u32[]{:S(2)}) async-start(bf16[16,64,256]{2,1,0:T(8,128)(2,1)} %sum_copies.1), calls=%async_computation.1 | async-start | bytes 1048576 | tf_op jit(solution)/shard_map/all_to_all | solution.py:509
  80.7 4.8 %collective-permute-start.11 = (bf16[16,64,256]{2,1,0:T(8,128)(2,1)S(1)}, bf16[16,64,256]{2,1,0:T(8,128)(2,1)S(1)}, u32[]{:S(2)}, u32[]{:S(2)}) collective-permute-start(bf16[16,64,256]{2,1,0:T(8,128)(2,1)S(1)} %all-to-all-done.1), channel_id=1, source_target_pairs={{0,1},{1,0},{2,3},{3,2},{4,5},{5,4},{6,7},{7,6},{8,9},{9,8},{10,11... | collective-permute-start | bytes 1572872 | tf_op jit(solution)/shard_map/ppermute | solution.py:498
